TPU v7x, 128 devices: a whole 4x4x4 slice. The times are simulated.
128 devices in a mesh: row: 8 (over x, core), col: 16 (over z, y).
Axes of the slice: x: 4, y: 4, z: 4, core: 2. Of those that a mesh axis runs over, the one named last changes fastest.
Arguments:
- blocks: bfloat16 [16, 1024, 4096], P('row', 'col'), may hold values from -6 to 6
- block_atom: int32 [16, 16], P('row', 'col'), may hold values from 0 to 127, as said below
- block_pair: int32 [16, 16], P('row', 'col'), may hold values from 0 to 8, as said below
- atom_sizes: int32 [128], replicated, may hold values from 32 to 64
- density: bfloat16 [8192, 8192], P('col', 'row'), may hold values from -0.125 to 0.125
- density_pattern: int32 [128, 128], P('col', 'row'), may hold values 0 or 1
Outputs:
- contracted: bfloat16 [8, 8192, 4096], P('row', 'col')
Inputs may be any that keep to these rules, and one draw needn't show every extreme that they name: `block_pair`: empty slots hold 8. The slots of one device name any one target row at most 1 times, and all slots with the same col index name any one target row at most 2 times; both bounds are reached in every draw. `block_atom`: A block in col index c has an atom of c * 8 to (c + 1) * 8 - 1; no two present blocks share both atom and pair.
All inputs are finite; a program needn't handle non-finite values. No bound on the sum of `density_pattern` on one device may be relied on, other than what follows from the above.
Results may differ from a plain program's by a relative error of at most 0.001.
Values may be sent and summed in bfloat16 or wider, within the bound.
No kernel may reach another device: no remote copies, remote signals or barrier semaphores. Data moves between devices by JAX's collectives and lax.ppermute only.
A program may use at most 128 MiB of HBM per device.

v0:
```python
import jax
import jax.numpy as jnp
from jax import lax
from jax.sharding import PartitionSpec as P

CAP = 2


def per_device(blocks, block_atom, block_pair, atom_sizes, density, density_pattern):
    block_width = blocks.shape[1]
    tile_width = blocks.shape[2]
    atom_count = atom_sizes.shape[0]
    lam_count = density.shape[0] // block_width
    density_all, pattern_all = (
        lax.all_gather(density, "row", axis=1, tiled=True),
        lax.all_gather(density_pattern, "row", axis=1, tiled=True),
    )
    col_index = lax.axis_index("col")
    lam_sizes = lax.dynamic_slice_in_dim(atom_sizes, col_index * lam_count, lam_count)
    offsets = jnp.arange(block_width, dtype=jnp.int32)
    row_inside = (offsets[None, :] < lam_sizes[:, None]).astype(jnp.bfloat16)
    col_inside = (offsets[None, :] < atom_sizes[:, None]).astype(jnp.bfloat16)
    factor = (
        pattern_all.astype(jnp.bfloat16)[:, None, :, None]
        * row_inside[:, :, None, None]
        * col_inside[None, None, :, :]
    )
    masked_density = (
        density_all.reshape(lam_count, block_width, atom_count, block_width) * factor
    ).reshape(lam_count * block_width, atom_count, block_width)
    source_pair = block_pair[:, 0]
    source_atom = block_atom[:, 0]
    all_tiles, all_pairs, all_atoms = (
        lax.all_gather(blocks, "row", axis=0, tiled=True),
        lax.all_gather(source_pair, "row", axis=0, tiled=True),
        lax.all_gather(source_atom, "row", axis=0, tiled=True),
    )
    mine_mask = all_pairs == lax.axis_index("row")
    got_atoms = jnp.where(mine_mask, all_atoms, atom_count)
    ordering = jnp.argsort((got_atoms >= atom_count).astype(jnp.int32), stable=True)[:CAP]
    own_tiles = jnp.take(all_tiles, ordering, axis=0)
    own_atoms = jnp.take(got_atoms, ordering)
    panel_tiles, panel_atoms = (
        lax.all_gather(own_tiles, "col", axis=0, tiled=True),
        lax.all_gather(own_atoms, "col", axis=0, tiled=True),
    )
    present = (panel_atoms < atom_count).astype(jnp.bfloat16)
    chosen = jnp.take(masked_density, jnp.minimum(panel_atoms, atom_count - 1), axis=1)
    chosen = chosen * present[None, :, None]
    left_side = chosen.reshape(chosen.shape[0], -1)
    right_side = panel_tiles.reshape(-1, tile_width)
    result = jnp.dot(left_side, right_side, preferred_element_type=jnp.float32)
    return result.astype(jnp.bfloat16)[None]


def solution(mesh):
    placed = (
        P("row", "col", None),
        P("row", "col"),
        P("row", "col"),
        P(),
        P("col", "row"),
        P("col", "row"),
    )
    return jax.shard_map(
        per_device, mesh=mesh, in_specs=placed, out_specs=P("row", "col", None), check_vma=False
    )
```

profile of v0, /device:TPU:6, one launch (start us, length us, event | category | flops | bytes accessed | tf_op | source)
XLA Modules:
  0.0 247.2 jit_solution(2227969579544338013)
XLA Ops:
  6.5 0.0 all-gather.9.cloned.1.call-start
  6.5 0.7 all-gather.9.cloned.1.call-update
  7.3 0.0 all-gather.7.cloned.1.call-start
  7.3 2.3 copy.13
  9.6 0.0 all-gather.7.cloned.1.call-update
  9.7 0.0 all-gather.11.cloned.1.call-start
  9.7 1.2 dynamic-slice
  11.6 0.8 bitcast_dynamic-update-slice_fusion
  12.4 0.7 bitcast_dynamic-update-slice_fusion.1
  13.1 7.3 %all-reduce.3 = (s32[16]{0:T(128)S(1)}, s32[16]{0:T(128)S(1)}) all-reduce(s32[16]{0:T(128)S(1)} %bitcast_dynamic-update-slice_fusion, s32[16]{0:T(128)S(1)} %bitcast_dynamic-update-slice_fusion.1), channel_id=3, replica_groups=mesh['row'=8,'col'=16] {'row'}, use_global_device_ids=true, to_apply=%add.1 | all-reduce | flops 32 | bytes 256
  20.4 1.2 sort.17
  21.7 37.6 %all-gather.9.cloned.1.call-done = bf16[16,64,4096]{2,1,0:T(8,128)(2,1)} async-done(((bf16[2,64,4096]{2,1,0:T(8,128)(2,1)}), bf16[16,64,4096]{2,1,0:T(8,128)(2,1)}) %all-gather.9.cloned.1.call-update) | async-done | bytes 8388624 | tf_op jit(solution)/shard_map/all_gather | solution.py:34
  59.3 4.0 %gather_fusion.2 = bf16[2,64,4096]{2,1,0:T(8,128)(2,1)S(1)} fusion(bf16[16,64,4096]{2,1,0:T(8,128)(2,1)} %all-gather.9.cloned.1.call-done, s32[1024]{0:T(1024)S(1)} %pad_clamp_fusion.1), kind=kCustom, calls=%fused_computation.2 | custom fusion | bytes 2097160 | tf_op jit(solution)/shard_map/jit(_take)/gather | solution.py:41
  63.3 1.1 broadcast_select_fusion
  64.4 0.0 all-gather.11.cloned.1.call-update
  64.4 0.6 gather_fusion
  65.1 0.7 dynamic-slice.2
  66.4 0.1 dynamic_slice.3
  66.4 0.1 fusion.8
  66.5 0.1 reshape.76
  66.6 12.8 %all-gather.2 = s32[8,16,8]{1,2,0:T(8,128)S(1)} all-gather(s32[1,16,8]{1,2,0:T(8,128)S(1)} %bitcast.27), channel_id=1, replica_groups=mesh['row'=8,'col'=16] {'row'}, dimensions={0}, use_global_device_ids=true | all-gather | bytes 4608 | tf_op jit(solution)/shard_map/all_gather | solution.py:16
  79.4 0.1 reshape.131
  79.5 0.1 bitcast_multiply_fusion
  79.6 0.1 copy.15
  79.8 0.1 select_dynamic-update-slice_fusion
  79.9 16.6 %all-reduce.2 = s32[32]{0:T(128)S(1)} all-reduce(s32[32]{0:T(128)S(1)} %select_dynamic-update-slice_fusion), channel_id=1, replica_groups=mesh['row'=8,'col'=16] {'col'}, use_global_device_ids=true, to_apply=%add.2 | all-reduce | flops 32 | bytes 256
  96.5 0.1 fusion.7
  96.6 14.3 %all-gather.7.cloned.1.call-done = bf16[512,8192]{0,1:T(8,128)(2,1)} async-done(((bf16[512,1024]{0,1:T(8,128)(2,1)}), bf16[512,8192]{0,1:T(8,128)(2,1)}) %all-gather.7.cloned.1.call-update) | async-done | bytes 8388624 | tf_op jit(solution)/shard_map/all_gather | solution.py:15
  110.9 7.4 %multiply_multiply_fusion = bf16[512,128,64]{0,2,1:T(8,128)(2,1)} fusion(bf16[512,128,64]{0,2,1:T(8,128)(2,1)} %bitcast.25, bf16[128,64]{1,0:T(8,128)(2,1)S(1)} %fusion.7, bf16[512,128]{0,1:T(8,128)(2,1)S(1)} %copy.15), kind=kLoop, calls=%fused_computation.4 | loop fusion | flops 8388608 | bytes 16924672 | tf_op jit(solution)/shard_map/mul | solution.py:29
  118.3 4.1 %gather_fusion.1 = bf16[32,512,64]{1,2,0:T(8,128)(2,1)S(1)} fusion(bf16[512,128,64]{0,2,1:T(8,128)(2,1)} %multiply_multiply_fusion, s32[1024]{0:T(1024)S(1)} %pad_clamp_fusion), kind=kCustom, calls=%fused_computation.1 | custom fusion | bytes 4194432 | tf_op jit(solution)/shard_map/jit(_take)/gather | solution.py:48
  122.4 104.2 %all-gather.11.cloned.1.call-done = bf16[32,64,4096]{2,1,0:T(8,128)(2,1)} async-done(((bf16[2,64,4096]{2,1,0:T(8,128)(2,1)}), bf16[32,64,4096]{2,1,0:T(8,128)(2,1)}) %all-gather.11.cloned.1.call-update) | async-done | bytes 16777232 | tf_op jit(solution)/shard_map/all_gather | solution.py:44
  226.6 14.1 %fusion = bf16[1,512,4096]{2,1,0:T(8,128)(2,1)} fusion(bf16[32,64,4096]{2,1,0:T(8,128)(2,1)} %all-gather.11.cloned.1.call-done, bf16[32,512,64]{1,2,0:T(8,128)(2,1)S(1)} %gather_fusion.1, pred[32]{0:T(512)(128)(4,1)S(1)} %get-tuple-element.9, bf16[32]{0:T(256)(128)(2,1)S(1)} %get-tuple-element.15), kind=kOutput, calls=%fused_computation.5 | convolution fusion | flops 8594128896 | bytes 23068768 | tf_op jit(solution)/shard_map/dot_general | solution.py:52
  (17 shorter events, 0.1 us)
Async XLA Ops:
  6.5 58.5 %copy-start.2 = (u32[128]{0:T(128)S(1)}, u32[128]{0:T(128)}, u32[]{:S(2)}) copy-start(u32[128]{0:T(128)} %constant.75) | copy-start | bytes 1540
  6.5 59.8 %copy-start.1 = (s32[128]{0:T(128)S(1)}, s32[128]{0:T(128)}, u32[]{:S(2)}) copy-start(s32[128]{0:T(128)} %param.9) | copy-start | bytes 1540
  6.5 60.1 %copy-start = (s32[8,16]{1,0:T(8,128)S(1)}, s32[8,16]{1,0:T(8,128)}, u32[]{:S(2)}) copy-start(s32[8,16]{1,0:T(8,128)} %param.11) | copy-start | bytes 1540
  6.5 52.7 %all-gather.9.cloned.1.call-start = ((), (), s32[]{:S(2)}) async-start(), calls=%async_computation.1 | async-start | bytes 9437184 | tf_op jit(solution)/shard_map/all_gather | solution.py:34
  7.3 103.7 %all-gather.7.cloned.1.call-start = ((), (), s32[]{:S(2)}) async-start(), calls=%async_computation | async-start | bytes 9437184 | tf_op jit(solution)/shard_map/all_gather | solution.py:15
  9.7 216.9 %all-gather.11.cloned.1.call-start = ((), (), s32[]{:S(2)}) async-start(), calls=%async_computation.2 | async-start | bytes 17825792 | tf_op jit(solution)/shard_map/all_gather | solution.py:44
Sparse Core Ops, SparseCore 0:
  9.1 50.1 all-gather.8
  61.0 49.8 all-gather.6
  113.1 113.5 all-gather.10
where the time goes:
time: 248 us; the launch traced here: 247 us
  waiting for transfers between devices  157 us (63%)
  blocking collectives  36.6 us (15%)
  local copies, waits for them, and re-layouts  14.8 us (6%)
  between operations  14.5 us (6%)
  matrix products  14.1 us (6%)
  other arithmetic  10.2 us (4%)
    all_gather x1, waiting for transfers between devices, per_device(): lax.all_gather(own_tiles, 'col', axis=0, tiled=True)  104 us
    all_gather x1, waiting for transfers between devices, per_device(): lax.all_gather(blocks, 'row', axis=0, tiled=True)  37.6 us
    unnamed x2, blocking collectives  23.9 us
    all_gather x1, waiting for transfers between devices, per_device(): lax.all_gather(density, 'row', axis=1, tiled=True)  14.3 us
    dot_general x1, matrix products, per_device(): result = jnp.dot(left_side, right_side, preferred_element_type=jnp.float32)  14.1 us
    all_gather x1, blocking collectives, per_device(): lax.all_gather(density_pattern, 'row', axis=1, tiled=True)  12.8 us
    mul x1, other arithmetic, per_device(): density_all.reshape(lam_count, block_width, atom_count, block_width)  7.42 us
    unnamed x14, local copies, waits for them, and re-layouts  5.74 us
  transfers between devices with their start and end apart: 3, of which 3 were waited for; matrix products, arithmetic and copies ran while one was open for 10% of the time, Pallas kernels for 0%

commit v1 on v0

v1 whole, which is shorter than its diff:
```python
import jax
import jax.numpy as jnp
from jax import lax
from jax.experimental import pallas as pl
from jax.experimental.pallas import tpu as pltpu
from jax.sharding import PartitionSpec as P

FIRST = 1024
BN = 512
ORDER = (0, -1, 1, 2)
VMEM = 20 * 1024 * 1024
BESIDE = 128


def shift_row_x(v, d):
    return lax.ppermute(v, "row", [(2 * x + k, 2 * ((x + d) % 4) + k) for x in range(4) for k in range(2)])


def swap_core(v):
    return lax.ppermute(v, "row", [(r, r ^ 1) for r in range(8)])


def shift_z(v, d):
    return lax.ppermute(v, "col", [(4 * z + y, 4 * ((z + d) % 4) + y) for z in range(4) for y in range(4)])


def shift_y(v, d):
    return lax.ppermute(v, "col", [(4 * z + y, 4 * z + (y + d) % 4) for z in range(4) for y in range(4)])


def after(values):
    return lax.optimization_barrier(values)


def around(v, shift):
    return jnp.concatenate([v, shift(v, 1), shift(v, -1), shift(v, 2)], axis=0)


def relay(v, shift):
    half = v.shape[0] // 2
    minus, plus = shift(v, 1), shift(v, -1)
    return [v, minus, plus, jnp.concatenate([shift(minus[:half], 1), shift(plus[half:], -1)], axis=0)]


def spread_names(v, shift, place):
    slots = jnp.arange(4, dtype=jnp.int32).reshape((4,) + (1,) * v.ndim)
    total = jnp.where(slots == place, v[None], 0)
    for d in (1, -1, 2):
        total = total + jnp.where(slots == (place - d) % 4, shift(v, d)[None], 0)
    return total


def choose_kernel(density_ref, row_ref, pattern_ref, inside_ref, out_ref):
    rows = density_ref.shape[1]
    hit = lax.broadcasted_iota(jnp.int32, (rows, row_ref.shape[1]), 0) == row_ref[...]
    picked = jnp.dot(density_ref[...], hit.astype(jnp.bfloat16), preferred_element_type=jnp.float32)
    factor = jnp.dot(inside_ref[...], pattern_ref[...], preferred_element_type=jnp.float32)
    out_ref[0] = (picked * factor).astype(jnp.bfloat16)


def choose_columns(density, rows, pattern, inside):
    count = rows.shape[1] // 256
    m, width = density.shape
    return pl.pallas_call(
        choose_kernel,
        grid=(count,),
        in_specs=[
            pl.BlockSpec((m, width), lambda t: (0, 0)),
            pl.BlockSpec((1, 256), lambda t: (0, t)),
            pl.BlockSpec((pattern.shape[0], 256), lambda t: (0, t)),
            pl.BlockSpec(inside.shape, lambda t: (0, 0)),
        ],
        out_specs=pl.BlockSpec((1, m, 256), lambda t: (t, 0, 0)),
        out_shape=jax.ShapeDtypeStruct((count, m, 256), jnp.bfloat16),
        compiler_params=pltpu.CompilerParams(vmem_limit_bytes=VMEM),
        cost_estimate=pl.CostEstimate(
            flops=2 * m * width * rows.shape[1], bytes_accessed=2 * m * (width + rows.shape[1]), transcendentals=0
        ),
        name="choose_columns",
    )(density, rows, pattern, inside)


def order_kernel(place_ref, half_ref, *refs):
    own, other, (left1, left2) = refs[:4], refs[4], refs[5:]
    for i in range(16):
        place = place_ref[i]
        columns = pl.ds(pl.multiple_of(half_ref[i] * 128, 128), 128)
        j = (i % 4) * 4 + i // 4

        def put(block):
            left1[:, i * 128 : (i + 1) * 128] = block
            left2[:, j * 128 : (j + 1) * 128] = block

        for d in range(4):

            @pl.when(place == d)
            def _():
                put(own[d][0, :, columns])

        @pl.when(place >= 4)
        def _():
            put(other[jnp.maximum(place - 4, 0), :, columns])


def order_columns(place, half, own, other):
    m = other.shape[1]
    return pl.pallas_call(
        order_kernel,
        grid_spec=pltpu.PrefetchScalarGridSpec(
            num_scalar_prefetch=2,
            grid=(1,),
            in_specs=[pl.BlockSpec((1, m, 256), lambda i, p, h: (0, 0, 0))] * 4
            + [pl.BlockSpec(other.shape, lambda i, p, h: (0, 0, 0))],
            out_specs=[pl.BlockSpec((m, 2048), lambda i, p, h: (0, 0))] * 2,
        ),
        out_shape=[jax.ShapeDtypeStruct((m, 2048), jnp.bfloat16)] * 2,
        compiler_params=pltpu.CompilerParams(vmem_limit_bytes=VMEM),
        cost_estimate=pl.CostEstimate(flops=0, bytes_accessed=4 * 2 * m * 2048, transcendentals=0),
        name="order_columns",
    )(place, half, *own, other)


def sort_kernel(where_ref, *refs):
    names, pieces, outs = refs[:4], refs[4:8], refs[8:]
    b = outs[0].shape[1]
    spots = []
    for i, d in enumerate(ORDER):
        x = lax.rem(where_ref[2] + (d + 4), 4)
        for s in range(2):
            pair = jnp.tile(names[i][s, :1, :].astype(jnp.float32), (1, outs[0].shape[2] // BESIDE))
            spots.append((2 * x + s, pair, pieces[i][s, :b, :]))
    flip = where_ref[3] == 1
    for out, row in ((outs[0], where_ref[0]), (outs[1], where_ref[1])):
        row = row.astype(jnp.float32)
        match = [(pair == row).astype(jnp.float32) for _, pair, _ in spots]
        totals = [jnp.zeros(out.shape[1:], out.dtype), jnp.zeros(out.shape[1:], out.dtype)]
        for i, (at, _, tile) in enumerate(spots):
            before = sum(jnp.where(spots[j][0] < at, match[j], 0.0) for j in range(8) if j != i)
            first = match[i] * (1.0 - jnp.minimum(before, 1.0))
            second = match[i] * jnp.minimum(before, 1.0)
            for s, one in enumerate((jnp.where(flip, second, first), jnp.where(flip, first, second))):
                totals[s] = totals[s] + tile * one.astype(out.dtype)
        for s in range(2):
            out[s] = totals[s]


def sort_tiles(where, named, pieces):
    b, n, step = named[0].shape[1], pieces[0].shape[2], 256
    n -= BESIDE
    at = named[0].shape[2] // BESIDE - 1
    return pl.pallas_call(
        sort_kernel,
        grid_spec=pltpu.PrefetchScalarGridSpec(
            num_scalar_prefetch=1,
            grid=(n // step,),
            in_specs=[pl.BlockSpec((2, 16, BESIDE), lambda i, p: (0, 0, at))] * 4
            + [pl.BlockSpec((2, b, step), lambda i, p: (0, 0, i))] * 4,
            out_specs=[pl.BlockSpec((2, b, step), lambda i, p: (0, 0, i))] * 2,
        ),
        out_shape=[jax.ShapeDtypeStruct((2, b, n), jnp.bfloat16)] * 2,
        compiler_params=pltpu.CompilerParams(vmem_limit_bytes=VMEM),
        cost_estimate=pl.CostEstimate(flops=0, bytes_accessed=24 * b * n, transcendentals=0),
        name="sort_tiles",
    )(where, *named, *pieces)


def product_kernel(at, count, started, left_ref, *refs):
    total = refs[count][...] if started else None
    for piece in refs[:count]:
        depth = piece.shape[0] * piece.shape[1]
        right = piece[...].reshape(depth, piece.shape[2])
        term = jnp.dot(left_ref[:, at : at + depth], right, preferred_element_type=jnp.float32)
        total = term if total is None else total + term
        at += depth
    refs[-1][...] = total.astype(refs[-1].dtype)


def product(left, at, pieces, total=None, out=None, column=0, width=None):
    m = left.shape[0]
    n = pieces[0].shape[2]
    depth = sum(p.shape[0] * p.shape[1] for p in pieces)
    first = column // BN
    specs = [pl.BlockSpec(left.shape, lambda i: (0, 0))]
    specs += [pl.BlockSpec(p.shape[:2] + (BN,), lambda i: (0, 0, i)) for p in pieces]
    operands = [left, *pieces]
    if total is not None:
        specs.append(pl.BlockSpec((m, BN), lambda i: (0, i)))
        operands.append(total)
    alias = {}
    if out is not None:
        specs.append(pl.BlockSpec(memory_space=pl.ANY))
        alias = {len(operands): 0}
        operands.append(out)

    def kernel(*refs):
        product_kernel(at, len(pieces), total is not None, *refs)

    shape = jax.ShapeDtypeStruct((m, n), jnp.float32) if width is None else jax.ShapeDtypeStruct((m, width), jnp.bfloat16)
    return pl.pallas_call(
        kernel,
        grid=(n // BN,),
        in_specs=specs,
        out_specs=pl.BlockSpec((m, BN), lambda i: (0, first + i)),
        out_shape=shape,
        input_output_aliases=alias,
        compiler_params=pltpu.CompilerParams(vmem_limit_bytes=VMEM),
        cost_estimate=pl.CostEstimate(
            flops=2 * m * depth * n, bytes_accessed=2 * (left.size + (depth + 2 * m) * n), transcendentals=0
        ),
        name="product",
    )(*operands)


def per_device(blocks, block_atom, block_pair, atom_sizes, density, density_pattern):
    b, width = blocks.shape[1], blocks.shape[2]
    r, c = lax.axis_index("row"), lax.axis_index("col")
    x, k, z, y = r // 2, r % 2, c // 4, c % 4
    i32 = jnp.int32
    offsets = jnp.array(ORDER, dtype=i32)

    names = jnp.concatenate([block_pair, block_atom], axis=1)
    row_names = spread_names(spread_names(names, shift_z, z), shift_y, y)

    def beside(v):
        v = jnp.broadcast_to(v, (2,) + v.shape[-2:]).transpose(0, 2, 1).astype(jnp.bfloat16)
        v = jnp.broadcast_to(v[..., None], v.shape + (b // 2 // v.shape[2],)).reshape(2, b, 1)
        return jnp.broadcast_to(v, (2, b, BESIDE))

    start = jnp.concatenate([blocks[:, :, :FIRST], beside(names[:, None, :])], axis=2)
    where = jnp.stack([r, r + 1 - 2 * k, x, k]).astype(i32)
    near = relay(start, shift_row_x)
    mine, theirs = sort_tiles(where, near, near)
    part1 = mine + swap_core(theirs)
    table = row_names.transpose(1, 0, 2, 3).reshape(32, 2)
    rest = jnp.concatenate([blocks[:, :, FIRST:], beside(table)], axis=2)
    rest, mine, theirs = after((rest, mine, theirs))
    part1 = mine + swap_core(theirs)
    near2 = relay(rest, shift_row_x)
    mine, theirs = sort_tiles(where, near, near2)
    part2 = mine + swap_core(theirs)

    far = jnp.arange(4, dtype=i32)
    from_x = (x + offsets) % 4
    found = jnp.stack([piece[0, :, width - FIRST] for piece in near2]).astype(i32).reshape(4, 2, 32)
    found = found[:, 0] * 256 + found[:, 1]
    found = jnp.sum(jnp.where(far[:, None, None] == from_x[:, None], found, 0), axis=1).reshape(4, 16, 2)
    found2 = swap_core(found)
    code = jnp.where(k == 0, jnp.stack([found, found2], 1), jnp.stack([found2, found], 1))
    code = code.transpose(2, 0, 1, 3)

    def slots_of(code, pair):
        spot = 4 * jnp.arange(4, dtype=i32)[:, None] + jnp.arange(2, dtype=i32)
        lows, highs = [], []
        for core in range(2):
            match = (code[..., core, :] // 256) == pair[..., None, None]
            low = jnp.min(jnp.where(match, spot, 99), axis=(-2, -1))
            high = jnp.max(jnp.where(match, spot, -1), axis=(-2, -1))
            lows.append(jnp.where(low < 99, low + 2 * core, -1))
            highs.append(jnp.where(high > low, high + 2 * core, -1))
        return jnp.stack([jnp.where(lows[0] >= 0, lows[0], highs[1]), jnp.where(lows[1] >= 0, lows[1], highs[0])], -1)

    two = lax.dynamic_slice_in_dim(code, 2 * r, 2)
    pairs = (2 * ((x + far) % 4)[:, None] + (k + jnp.arange(2, dtype=i32)) % 2).reshape(8)
    source = slots_of(two[None], jnp.broadcast_to(pairs[:, None], (8, 2)))
    hit = source[..., None] == jnp.arange(16, dtype=i32)
    atom = jnp.sum(jnp.where(hit, (two % 256).reshape(2, 1, 16), 0), axis=-1)
    atom = jnp.where(source >= 0, atom - 16 * r, -1).reshape(1, 32)
    sizes_here = lax.dynamic_slice_in_dim(atom_sizes, 16 * r, 16)
    pattern_hit = jnp.arange(16, dtype=i32)[:, None] == atom
    size = jnp.sum(jnp.where(pattern_hit, sizes_here[:, None], 0), axis=0)[:, None]
    unit = jnp.arange(b, dtype=i32)
    columns = atom.reshape(32, 1)
    rows = jnp.where((unit < size) & (columns >= 0), columns * b + unit, -1).reshape(1, 32 * b)
    chosen_pattern = jnp.sum(jnp.where(pattern_hit, density_pattern[:, :, None], 0), axis=1)
    chosen_pattern = jnp.broadcast_to(chosen_pattern[:, :, None], (8, 32, b)).reshape(8, 32 * b)
    lam_sizes = lax.dynamic_slice_in_dim(atom_sizes, 8 * c, 8)
    lam = jnp.arange(8 * b, dtype=i32)[:, None]
    inside = (lam // b == jnp.arange(8, dtype=i32)) & (lam % b < lam_sizes[None, :])
    chosen = choose_columns(density, rows, chosen_pattern.astype(jnp.bfloat16), inside.astype(jnp.bfloat16))
    chosen = chosen.reshape(4, 2, 8 * b, 4 * b)
    own = [chosen[0]] + [shift_row_x(chosen[d], d) for d in (1, 2, 3)]
    other = swap_core(jnp.stack([piece[1] for piece in own]))

    from_y = jnp.repeat((y + offsets) % 4, 4)
    from_z = jnp.tile((z + offsets) % 4, 4)
    place = (x - from_z) % 4 + jnp.where(from_y // 2 == k, 0, 4)
    left1, left2 = order_columns(place.astype(i32), (from_y % 2).astype(i32), own, other)

    def spread(part, how):
        half = part.shape[2] // 2
        return how(part[:, :, :half], shift_z), how(part[:, :, half:], shift_y)

    def relay_joined(v, shift):
        return jnp.concatenate(relay(v, shift), axis=0)

    def send(g1, g2):
        return (shift_y(g1, 1), shift_y(g1, -1)), (shift_z(g2, 1), shift_z(g2, -1))

    def forward(sides):
        (minus1, plus1), (minus2, plus2) = sides
        return (
            [shift_y(minus1[:4], 1), shift_y(plus1[4:], -1)],
            [shift_z(minus2[:4], 1), shift_z(plus2[4:], -1)],
        )

    def multiply(g, sides, last, out, at):
        half = g[0].shape[2]
        totals = [product(left, 0, [v, *pair]) for left, v, pair in zip((left1, left2), g, sides)]
        for left, total, pieces in zip((left1, left2), totals, last):
            out = product(left, 24 * b, pieces, total, out, at, width)
            at += half
        return out

    g = spread(part1, around)
    sides = send(*g)
    last = forward(sides)
    part2, last = after((part2, last))
    h = spread(part2, relay_joined)
    h, _ = after((h, own))
    sides2 = send(*h)
    out = multiply(g, sides, last, None, 0)
    sides2, out = after((sides2, out))
    out = multiply(h, sides2, forward(sides2), out, FIRST)
    return out[None]


def solution(mesh):
    placed = (
        P("row", "col", None),
        P("row", "col"),
        P("row", "col"),
        P(),
        P("col", "row"),
        P("col", "row"),
    )
    return jax.shard_map(
        per_device, mesh=mesh, in_specs=placed, out_specs=P("row", "col", None), check_vma=False
    )
```

time: 248 us -> 199 us (0.80); the launches traced: 247 us -> 195 us
  waiting for transfers between devices: 157 us -> 50.1 us
  starting transfers between devices: 0.08 us -> 63.2 us
  Pallas kernels: 0 us -> 38.9 us
  blocking collectives: 36.6 us -> 0 us
  local copies, waits for them, and re-layouts: 14.8 us -> 36.2 us
  matrix products: 14.1 us -> 0 us
  between operations: 14.5 us -> 0.85 us
  other arithmetic: 10.2 us -> 5.99 us
    all_gather x3 -> x0, waiting for transfers between devices: 156 us -> none  [the longest x1 104 us: per_device(): lax.all_gather(own_tiles, 'col', axis=0, tiled=True)]
    ppermute x0 -> x51, starting transfers between devices: none -> 63.2 us  [the longest x18 24.5 us: shift_z(): lax.ppermute(v, 'col', [(4 * z + y, 4 * ((z + d) % 4) + y) for z in range...]
    ppermute x0 -> x51, waiting for transfers between devices: none -> 50.1 us  [the longest x18 25.1 us: shift_y(): lax.ppermute(v, 'col', [(4 * z + y, 4 * z + (y + d) % 4) for z in range(4...]
    pallas_call x0 -> x12, Pallas kernels: none -> 38.9 us  [the longest x8 23.3 us: product(): pl.pallas_call(kernel, grid=(n // BN,), in_specs=specs, out_specs=pl.Bloc...]
    unnamed x2 -> x0, blocking collectives: 23.9 us -> none
    slice x0 -> x31, local copies, waits for them, and re-layouts: none -> 18.4 us  [the longest x2 2.85 us: forward(): plus2[4:]]
    dot_general x1 -> x0, matrix products: 14.1 us -> none  [per_device(): result = jnp.dot(left_side, right_side, preferred_element_type=jnp.float32)]
    all_gather x1 -> x0, blocking collectives: 12.8 us -> none  [per_device(): lax.all_gather(density_pattern, 'row', axis=1, tiled=True)]
  transfers between devices with their start and end apart: 3 -> 51, of which waited for: 3 -> 17; matrix products, arithmetic and copies ran while one was open for 10% -> 16% of each run, Pallas kernels for 0% -> 18%
where the time goes in v1:
time: 199 us; the launch traced here: 195 us
  starting transfers between devices  63.2 us (32%)
  waiting for transfers between devices  50.1 us (25%)
  Pallas kernels  38.9 us (20%)
  local copies, waits for them, and re-layouts  36.2 us (18%)
  other arithmetic  5.99 us (3%)
    ppermute x18, waiting for transfers between devices, shift_y(): lax.ppermute(v, 'col', [(4 * z + y, 4 * z + (y + d) % 4) for z in range(4...  25.1 us
    ppermute x18, starting transfers between devices, shift_z(): lax.ppermute(v, 'col', [(4 * z + y, 4 * ((z + d) % 4) + y) for z in range...  24.5 us
    ppermute x18, starting transfers between devices, shift_y(): lax.ppermute(v, 'col', [(4 * z + y, 4 * z + (y + d) % 4) for z in range(4...  24 us
    pallas_call x8, Pallas kernels, product(): pl.pallas_call(kernel, grid=(n // BN,), in_specs=specs, out_specs=pl.Bloc...  23.3 us
    ppermute x18, waiting for transfers between devices, shift_z(): lax.ppermute(v, 'col', [(4 * z + y, 4 * ((z + d) % 4) + y) for z in range...  17.6 us
    ppermute x11, starting transfers between devices, shift_row_x(): lax.ppermute(v, 'row', [(2 * x + k, 2 * ((x + d) % 4) + k) for x in range...  14 us
    unnamed x53, local copies, waits for them, and re-layouts  12.8 us
    pallas_call x2, Pallas kernels, sort_tiles(): pl.pallas_call(sort_kernel, grid_spec=pltpu.PrefetchScalarGridSpec(num_sc...  8.41 us
  transfers between devices with their start and end apart: 51, of which 17 were waited for; matrix products, arithmetic and copies ran while one was open for 16% of the time, Pallas kernels for 18%

profile of v1, /device:TPU:6, one launch (start us, length us, event | category | flops | bytes accessed | tf_op | source)
XLA Modules:
  0.0 195.3 jit_solution(12400617166967553073)
XLA Ops:
  0.7 3.9 %collective-permute-start.2 = (s32[2,2]{0,1:T(2,128)S(1)}, s32[2,2]{0,1:T(2,128)S(1)}, u32[]{:S(2)}, u32[]{:S(2)}) collective-permute-start(s32[2,2]{0,1:T(2,128)S(1)} %get-tuple-element.72), channel_id=1, source_target_pairs={{0,8},{1,9},{2,10},{3,11},{4,12},{5,13},{6,14},{7,15},{8,0},{9,1},... | collective-permute-start | bytes 56 | tf_op jit(solution)/shard_map/ppermute | solution.py:24
  8.9 2.4 %collective-permute-start.6 = (bf16[2,64,1152]{2,1,0:T(8,128)(2,1)S(1)}, bf16[2,64,1152]{2,1,0:T(8,128)(2,1)S(1)}, u32[]{:S(2)}, u32[]{:S(2)}) collective-permute-start(bf16[2,64,1152]{2,1,0:T(8,128)(2,1)S(1)} %pad_maximum_fusion.5.refs_0_.refs_4_), channel_id=1, source_target_pairs={{0,32},{16,48},{32,64},{48,80},{64,96},{80,112},{96,0},{112,16},{1... | collective-permute-start | bytes 884744 | tf_op jit(solution)/shard_map/ppermute | solution.py:16
  12.5 3.2 %collective-permute-start.5 = (s32[4,2,2]{1,0,2:T(4,128)S(1)}, s32[4,2,2]{1,0,2:T(4,128)S(1)}, u32[]{:S(2)}, u32[]{:S(2)}) collective-permute-start(s32[4,2,2]{1,0,2:T(4,128)S(1)} %select_add_fusion), channel_id=1, source_target_pairs={{0,2},{1,3},{2,0},{3,1},{4,6},{5,7},{6,4},{7,5},{8,10},{9,11},{10,... | collective-permute-start | bytes 200 | tf_op jit(solution)/shard_map/ppermute | solution.py:28
  19.4 2.2 %collective-permute-done.3 = s32[4,2,2]{1,0,2:T(4,128)S(1)} collective-permute-done((s32[4,2,2]{1,0,2:T(4,128)S(1)}, s32[4,2,2]{1,0,2:T(4,128)S(1)}, u32[]{:S(2)}, u32[]{:S(2)}) %collective-permute-start.3) | collective-permute-done | bytes 96 | tf_op jit(solution)/shard_map/ppermute | solution.py:28
  24.1 2.8 %collective-permute-done.8 = bf16[1,64,1152]{2,1,0:T(8,128)(2,1)S(1)} collective-permute-done((bf16[1,64,1152]{2,1,0:T(8,128)(2,1)S(1)}, bf16[1,64,1152]{2,1,0:T(8,128)(2,1)S(1)}, u32[]{:S(2)}, u32[]{:S(2)}) %collective-permute-start.8) | collective-permute-done | bytes 147488 | tf_op jit(solution)/shard_map/ppermute | solution.py:16
  31.8 2.4 %collective-permute-start.10 = (bf16[2,64,3200]{2,1,0:T(8,128)(2,1)S(1)}, bf16[2,64,3200]{2,1,0:T(8,128)(2,1)S(1)}, u32[]{:S(2)}, u32[]{:S(2)}) collective-permute-start(bf16[2,64,3200]{2,1,0:T(8,128)(2,1)S(1)} %pad_maximum_fusion.1.refs_4_), channel_id=1, source_target_pairs={{0,32},{16,48},{32,64},{48,80},{64,96},{80,112},{96,0},{112,16},{1... | collective-permute-start | bytes 2457608 | tf_op jit(solution)/shard_map/ppermute | solution.py:16
  35.5 2.6 %collective-permute-start.22 = (bf16[2,64,512]{2,1,0:T(8,128)(2,1)S(1)}, bf16[2,64,512]{2,1,0:T(8,128)(2,1)S(1)}, u32[]{:S(2)}, u32[]{:S(2)}) collective-permute-start(bf16[2,64,512]{2,1,0:T(8,128)(2,1)S(1)} %get-tuple-element.64), channel_id=1, source_target_pairs={{0,12},{1,13},{2,14},{3,15},{4,0},{5,1},{6,2},{7,3},{8,4},{9,5},{1... | collective-permute-start | bytes 393224 | tf_op jit(solution)/shard_map/ppermute | solution.py:24
  38.1 4.2 %collective-permute-done.23 = bf16[2,64,512]{2,1,0:T(8,128)(2,1)S(1)} collective-permute-done((bf16[2,64,512]{2,1,0:T(8,128)(2,1)S(1)}, bf16[2,64,512]{2,1,0:T(8,128)(2,1)S(1)}, u32[]{:S(2)}, u32[]{:S(2)}) %collective-permute-start.23) | collective-permute-done | bytes 131104 | tf_op jit(solution)/shard_map/ppermute | solution.py:24
  46.0 3.8 %collective-permute-done.30 = bf16[2,64,512]{2,1,0:T(8,128)(2,1)S(1)} collective-permute-done((bf16[2,64,512]{2,1,0:T(8,128)(2,1)S(1)}, bf16[2,64,512]{2,1,0:T(8,128)(2,1)S(1)}, u32[]{:S(2)}, u32[]{:S(2)}) %collective-permute-start.30) | collective-permute-done | bytes 131104 | tf_op jit(solution)/shard_map/ppermute | solution.py:28
  69.6 3.2 %collective-permute-start.34 = (bf16[4,64,512]{2,1,0:T(8,128)(2,1)}, bf16[4,64,512]{2,1,0:T(8,128)(2,1)S(1)}, u32[]{:S(2)}, u32[]{:S(2)}) collective-permute-start(bf16[4,64,512]{2,1,0:T(8,128)(2,1)} %slice.181), channel_id=1, source_target_pairs={{0,12},{1,13},{2,14},{3,15},{4,0},{5,1},{6,2},{7,3},{8,4},{9,5},{1... | collective-permute-start | bytes 786440 | tf_op jit(solution)/shard_map/ppermute | solution.py:24
  79.2 6.4 %sort_tiles.3 = (bf16[2,64,3072]{2,1,0:T(8,128)(2,1)S(1)}, bf16[2,64,3072]{2,1,0:T(8,128)(2,1)}) custom-call(s32[4]{0:T(128)S(1)} %pad_add_fusion.2.where_ref, bf16[2,64,1152]{2,1,0:T(8,128)(2,1)S(1)} %pad_maximum_fusion.5.refs_0_.refs_4_, bf16[2,64,1152]{2,1,0:T(8,128)(2,1)S(1)} %collective-permute-done.6.refs_1_.refs_5_, ...), custom_call_target="tpu_custom_call" | custom-call | bytes 4718592 | tf_op jit(solution)/shard_map/sort_tiles/pallas_call | solution.py:151
  91.6 3.2 %collective-permute-start.40 = (bf16[2,64,1536]{2,1,0:T(8,128)(2,1)S(1)}, bf16[2,64,1536]{2,1,0:T(8,128)(2,1)S(1)}, u32[]{:S(2)}, u32[]{:S(2)}) collective-permute-start(bf16[2,64,1536]{2,1,0:T(8,128)(2,1)S(1)} %get-tuple-element.59), channel_id=1, source_target_pairs={{0,3},{1,0},{2,1},{3,2},{4,7},{5,4},{6,5},{7,6},{8,11},{9,8},{10,9... | collective-permute-start | bytes 1179656 | tf_op jit(solution)/shard_map/ppermute | solution.py:28
  94.8 3.2 %collective-permute-start.36 = (bf16[2,64,1536]{2,1,0:T(8,128)(2,1)S(1)}, bf16[2,64,1536]{2,1,0:T(8,128)(2,1)S(1)}, u32[]{:S(2)}, u32[]{:S(2)}) collective-permute-start(bf16[2,64,1536]{2,1,0:T(8,128)(2,1)S(1)} %get-tuple-element.62), channel_id=1, source_target_pairs={{0,12},{1,13},{2,14},{3,15},{4,0},{5,1},{6,2},{7,3},{8,4},{9,5},{1... | collective-permute-start | bytes 1179656 | tf_op jit(solution)/shard_map/ppermute | solution.py:24
  98.1 4.2 %choose_columns.1 = bf16[8,512,256]{2,1,0:T(8,128)(2,1)S(1)} custom-call(bf16[512,1024]{1,0:T(8,128)(2,1)S(1)} %copy-done.19, s32[1,2048]{1,0:T(1,128)S(1)} %select_n.388.row_ref, bf16[8,2048]{1,0:T(8,128)(2,1)S(1)} %convert_element_type.33.pattern_ref, bf16[512,8]{1,0:T(8,128)(2,1)S(1)} %fusion.1.inside_ref), custom_call_target="tpu_custom_call" | custom-call | flops 2147483648 | bytes 3145728 | tf_op jit(solution)/shard_map/choose_columns/pallas_call | solution.py:64
  103.4 3.2 %collective-permute-start.15 = (bf16[2,512,256]{2,1,0:T(8,128)(2,1)S(1)}, bf16[2,512,256]{2,1,0:T(8,128)(2,1)S(1)}, u32[]{:S(2)}, u32[]{:S(2)}) collective-permute-start(bf16[2,512,256]{2,1,0:T(8,128)(2,1)S(1)} %get-tuple-element.56), channel_id=1, source_target_pairs={{0,64},{16,80},{32,96},{48,112},{64,0},{80,16},{96,32},{112,48},{1... | collective-permute-start | bytes 1572872 | tf_op jit(solution)/shard_map/ppermute | solution.py:16
  107.3 3.1 %collective-permute-start.42 = (bf16[1,64,1536]{2,1,0:T(8,128)(2,1)S(1)}, bf16[1,64,1536]{2,1,0:T(8,128)(2,1)S(1)}, u32[]{:S(2)}, u32[]{:S(2)}) collective-permute-start(bf16[1,64,1536]{2,1,0:T(8,128)(2,1)S(1)} %slice.185), channel_id=1, source_target_pairs={{0,3},{1,0},{2,1},{3,2},{4,7},{5,4},{6,5},{7,6},{8,11},{9,8},{10,9... | collective-permute-start | bytes 589832 | tf_op jit(solution)/shard_map/ppermute | solution.py:28
  112.0 6.9 %collective-permute-done.35 = bf16[2,64,1536]{2,1,0:T(8,128)(2,1)S(1)} collective-permute-done((bf16[2,64,1536]{2,1,0:T(8,128)(2,1)S(1)}, bf16[2,64,1536]{2,1,0:T(8,128)(2,1)S(1)}, u32[]{:S(2)}, u32[]{:S(2)}) %collective-permute-start.35) | collective-permute-done | bytes 393248 | tf_op jit(solution)/shard_map/ppermute | solution.py:24
  120.5 5.3 %collective-permute-done.41 = bf16[1,64,1536]{2,1,0:T(8,128)(2,1)S(1)} collective-permute-done((bf16[1,64,1536]{2,1,0:T(8,128)(2,1)S(1)}, bf16[1,64,1536]{2,1,0:T(8,128)(2,1)S(1)}, u32[]{:S(2)}, u32[]{:S(2)}) %collective-permute-start.41) | collective-permute-done | bytes 196640 | tf_op jit(solution)/shard_map/ppermute | solution.py:28
  129.2 5.9 %collective-permute-done.37 = bf16[1,64,1536]{2,1,0:T(8,128)(2,1)S(1)} collective-permute-done((bf16[1,64,1536]{2,1,0:T(8,128)(2,1)S(1)}, bf16[1,64,1536]{2,1,0:T(8,128)(2,1)S(1)}, u32[]{:S(2)}, u32[]{:S(2)}) %collective-permute-start.37) | collective-permute-done | bytes 196640 | tf_op jit(solution)/shard_map/ppermute | solution.py:24
  143.0 2.7 %collective-permute-done.17.refs_4_ = bf16[4,512,256]{2,1,0:T(8,128)(2,1)} collective-permute-done((bf16[4,512,256]{2,1,0:T(8,128)(2,1)}, bf16[4,512,256]{2,1,0:T(8,128)(2,1)}, u32[]{:S(2)}, u32[]{:S(2)}) %collective-permute-start.17) | collective-permute-done | bytes 1048608 | tf_op jit(solution)/shard_map/ppermute | solution.py:20
  149.9 3.0 %order_columns.1 = (bf16[512,2048]{1,0:T(8,128)(2,1)S(1)}, bf16[512,2048]{1,0:T(8,128)(2,1)S(1)}) custom-call(s32[16]{0:T(128)S(1)} %get-tuple-element.77.place_ref, s32[16]{0:T(128)S(1)} %get-tuple-element.76.half_ref, bf16[2,512,256]{2,1,0:T(8,128)(2,1)S(1)} %copy-done.5, bf16[2,512,256]{2,1,0:T(8,128)(2,1)S(1)} %copy-done.15, ...), custom_call_target="tpu_custom_call" | custom-call | bytes 8388608 | tf_op jit(solution)/shard_map/order_columns/pallas_call | solution.py:107
  152.9 2.2 %product.9.refs_3_ = f32[512,512]{1,0:T(8,128)S(1)} custom-call(bf16[512,2048]{1,0:T(8,128)(2,1)S(1)} %get-tuple-element.39.refs_0_, bf16[8,64,512]{2,1,0:T(8,128)(2,1)S(1)} %copy-done.2, bf16[8,64,512]{2,1,0:T(8,128)(2,1)} %collective-permute-done.24.refs_2_, bf16[8,64,512]{2,1,0:T(8,128)(2,1)} %collective-permute-done.26.refs_3_), custom_call_target="tpu_custom_call" | custom-call | flops 805306368 | bytes 4718592 | tf_op jit(solution)/shard_map/product/pallas_call | solution.py:199
  155.1 2.2 %product.10.refs_4_ = bf16[512,4096]{1,0:T(8,128)(2,1)} custom-call(bf16[512,2048]{1,0:T(8,128)(2,1)S(1)} %get-tuple-element.39.refs_0_, bf16[4,64,512]{2,1,0:T(8,128)(2,1)} %collective-permute-done.25.refs_1_, bf16[4,64,512]{2,1,0:T(8,128)(2,1)S(1)} %collective-permute-done.27.refs_2_, f32[512,512]{1,0:T(8,128)S(1)} %product.9.refs_3_), custom_call_target="tpu_custom_call" | custom-call | flops 268435456 | bytes 3670016 | tf_op jit(solution)/shard_map/product/pallas_call | solution.py:199
  157.4 2.2 %product.8.refs_3_ = f32[512,512]{1,0:T(8,128)S(1)} custom-call(bf16[512,2048]{1,0:T(8,128)(2,1)S(1)} %get-tuple-element.29.refs_0_, bf16[8,64,512]{2,1,0:T(8,128)(2,1)S(1)} %copy-done.4, bf16[8,64,512]{2,1,0:T(8,128)(2,1)} %collective-permute-done.31.refs_2_, bf16[8,64,512]{2,1,0:T(8,128)(2,1)} %collective-permute-done.33.refs_3_), custom_call_target="tpu_custom_call" | custom-call | flops 805306368 | bytes 4718592 | tf_op jit(solution)/shard_map/product/pallas_call | solution.py:199
  159.6 2.2 %product.11.refs_4_ = bf16[512,4096]{1,0:T(8,128)(2,1)} custom-call(bf16[512,2048]{1,0:T(8,128)(2,1)S(1)} %get-tuple-element.29.refs_0_, bf16[4,64,512]{2,1,0:T(8,128)(2,1)} %collective-permute-done.32.refs_1_, bf16[4,64,512]{2,1,0:T(8,128)(2,1)S(1)} %copy-done.18, f32[512,512]{1,0:T(8,128)S(1)} %product.8.refs_3_, ...), custom_call_target="tpu_custom_call", output_to_operand_aliasing={{}: (4, {})} | custom-call | flops 268435456 | bytes 3670016 | tf_op jit(solution)/shard_map/product/pallas_call | solution.py:199
  161.8 7.4 %collective-permute-done.44.refs_3_ = bf16[8,64,1536]{2,1,0:T(8,128)(2,1)S(1)} collective-permute-done((bf16[8,64,1536]{2,1,0:T(8,128)(2,1)}, bf16[8,64,1536]{2,1,0:T(8,128)(2,1)S(1)}, u32[]{:S(2)}, u32[]{:S(2)}) %collective-permute-start.44) | collective-permute-done | bytes 1572896 | tf_op jit(solution)/shard_map/ppermute | solution.py:28
  169.1 2.2 %collective-permute-done.43.refs_2_ = bf16[8,64,1536]{2,1,0:T(8,128)(2,1)S(1)} collective-permute-done((bf16[8,64,1536]{2,1,0:T(8,128)(2,1)}, bf16[8,64,1536]{2,1,0:T(8,128)(2,1)S(1)}, u32[]{:S(2)}, u32[]{:S(2)}) %collective-permute-start.43) | collective-permute-done | bytes 1572896 | tf_op jit(solution)/shard_map/ppermute | solution.py:28
  172.0 2.5 %collective-permute-start.50 = (bf16[4,64,1536]{2,1,0:T(8,128)(2,1)S(1)}, bf16[4,64,1536]{2,1,0:T(8,128)(2,1)S(1)}, u32[]{:S(2)}, u32[]{:S(2)}) collective-permute-start(bf16[4,64,1536]{2,1,0:T(8,128)(2,1)S(1)} %slice.156), channel_id=1, source_target_pairs={{0,3},{1,0},{2,1},{3,2},{4,7},{5,4},{6,5},{7,6},{8,11},{9,8},{10,9... | collective-permute-start | bytes 2359304 | tf_op jit(solution)/shard_map/ppermute | solution.py:28
  179.1 4.8 %product.12.refs_3_ = f32[512,1536]{1,0:T(8,128)S(1)} custom-call(bf16[512,2048]{1,0:T(8,128)(2,1)S(1)} %get-tuple-element.29.refs_0_, bf16[8,64,1536]{2,1,0:T(8,128)(2,1)} %constant_dynamic-update-slice_fusion.7.refs_1_, bf16[8,64,1536]{2,1,0:T(8,128)(2,1)} %collective-permute-done.45.refs_2_, bf16[8,64,1536]{2,1,0:T(8,128)(2,1)} %collective-permute-done.46.refs_3_), custom_call_target="tpu_custom_call" | custom-call | flops 2415919104 | bytes 9961472 | tf_op jit(solution)/shard_map/product/pallas_call | solution.py:199
  183.9 4.3 %product.13.refs_3_ = f32[512,1536]{1,0:T(8,128)S(1)} custom-call(bf16[512,2048]{1,0:T(8,128)(2,1)S(1)} %get-tuple-element.39.refs_0_, bf16[8,64,1536]{2,1,0:T(8,128)(2,1)} %constant_dynamic-update-slice_fusion.2.refs_1_, bf16[8,64,1536]{2,1,0:T(8,128)(2,1)S(1)} %collective-permute-done.43.refs_2_, bf16[8,64,1536]{2,1,0:T(8,128)(2,1)S(1)} %collective-permute-done.44.refs_3_), custom_call_target="tpu_custom_call" | custom-call | flops 2415919104 | bytes 9961472 | tf_op jit(solution)/shard_map/product/pallas_call | solution.py:199
  189.8 2.7 %product.14.refs_4_ = bf16[512,4096]{1,0:T(8,128)(2,1)} custom-call(bf16[512,2048]{1,0:T(8,128)(2,1)S(1)} %get-tuple-element.39.refs_0_, bf16[4,64,1536]{2,1,0:T(8,128)(2,1)S(1)} %collective-permute-done.49.refs_1_, bf16[4,64,1536]{2,1,0:T(8,128)(2,1)S(1)} %collective-permute-done.50.refs_2_, ...), custom_call_target="tpu_custom_call", output_to_operand_aliasing={{}: (4, {})} | custom-call | flops 805306368 | bytes 6815744 | tf_op jit(solution)/shard_map/product/pallas_call | solution.py:199
  192.6 2.7 %product.15 = bf16[512,4096]{1,0:T(8,128)(2,1)} custom-call(bf16[512,2048]{1,0:T(8,128)(2,1)S(1)} %get-tuple-element.29.refs_0_, bf16[4,64,1536]{2,1,0:T(8,128)(2,1)S(1)} %collective-permute-done.47.refs_1_, bf16[4,64,1536]{2,1,0:T(8,128)(2,1)S(1)} %collective-permute-done.48.refs_2_, ...), custom_call_target="tpu_custom_call", output_to_operand_aliasing={{}: (4, {})} | custom-call | flops 805306368 | bytes 6815744 | tf_op jit(solution)/shard_map/product/pallas_call | solution.py:199
  (260 shorter events, 81.1 us)
Async XLA Ops:
  0.7 11.7 %collective-permute-start.2 = (s32[2,2]{0,1:T(2,128)S(1)}, s32[2,2]{0,1:T(2,128)S(1)}, u32[]{:S(2)}, u32[]{:S(2)}) collective-permute-start(s32[2,2]{0,1:T(2,128)S(1)} %get-tuple-element.72), channel_id=1, source_target_pairs={{0,8},{1,9},{2,10},{3,11},{4,12},{5,13},{6,14},{7,15},{8,0},{9,1},... | collective-permute-start | bytes 56 | tf_op jit(solution)/shard_map/ppermute | solution.py:24
  8.0 14.0 %collective-permute-start.7 = (bf16[2,64,1152]{2,1,0:T(8,128)(2,1)S(1)}, bf16[2,64,1152]{2,1,0:T(8,128)(2,1)S(1)}, u32[]{:S(2)}, u32[]{:S(2)}) collective-permute-start(bf16[2,64,1152]{2,1,0:T(8,128)(2,1)S(1)} %pad_maximum_fusion.5.refs_0_.refs_4_), channel_id=1, source_target_pairs={{0,96},{16,112},{32,0},{48,16},{64,32},{80,48},{96,64},{112,80},{1... | collective-permute-start | bytes 884744 | tf_op jit(solution)/shard_map/ppermute | solution.py:16
  8.9 12.8 %collective-permute-start.6 = (bf16[2,64,1152]{2,1,0:T(8,128)(2,1)S(1)}, bf16[2,64,1152]{2,1,0:T(8,128)(2,1)S(1)}, u32[]{:S(2)}, u32[]{:S(2)}) collective-permute-start(bf16[2,64,1152]{2,1,0:T(8,128)(2,1)S(1)} %pad_maximum_fusion.5.refs_0_.refs_4_), channel_id=1, source_target_pairs={{0,32},{16,48},{32,64},{48,80},{64,96},{80,112},{96,0},{112,16},{1... | collective-permute-start | bytes 884744 | tf_op jit(solution)/shard_map/ppermute | solution.py:16
  30.9 24.6 %collective-permute-start.11 = (bf16[2,64,3200]{2,1,0:T(8,128)(2,1)S(1)}, bf16[2,64,3200]{2,1,0:T(8,128)(2,1)S(1)}, u32[]{:S(2)}, u32[]{:S(2)}) collective-permute-start(bf16[2,64,3200]{2,1,0:T(8,128)(2,1)S(1)} %pad_maximum_fusion.1.refs_4_), channel_id=1, source_target_pairs={{0,96},{16,112},{32,0},{48,16},{64,32},{80,48},{96,64},{112,80},{1... | collective-permute-start | bytes 2457608 | tf_op jit(solution)/shard_map/ppermute | solution.py:16
  31.8 22.4 %collective-permute-start.10 = (bf16[2,64,3200]{2,1,0:T(8,128)(2,1)S(1)}, bf16[2,64,3200]{2,1,0:T(8,128)(2,1)S(1)}, u32[]{:S(2)}, u32[]{:S(2)}) collective-permute-start(bf16[2,64,3200]{2,1,0:T(8,128)(2,1)S(1)} %pad_maximum_fusion.1.refs_4_), channel_id=1, source_target_pairs={{0,32},{16,48},{32,64},{48,80},{64,96},{80,112},{96,0},{112,16},{1... | collective-permute-start | bytes 2457608 | tf_op jit(solution)/shard_map/ppermute | solution.py:16
  49.8 12.7 %collective-permute-start.26 = (bf16[8,64,512]{2,1,0:T(8,128)(2,1)S(1)}, bf16[8,64,512]{2,1,0:T(8,128)(2,1)}, u32[]{:S(2)}, u32[]{:S(2)}) collective-permute-start(bf16[8,64,512]{2,1,0:T(8,128)(2,1)S(1)} %pad_maximum_fusion.3.refs_1_), channel_id=1, source_target_pairs={{0,3},{1,0},{2,1},{3,2},{4,7},{5,4},{6,5},{7,6},{8,11},{9,8},{10,9... | collective-permute-start | bytes 1572872 | tf_op jit(solution)/shard_map/ppermute | solution.py:28
  50.5 13.7 %collective-permute-start.24 = (bf16[8,64,512]{2,1,0:T(8,128)(2,1)S(1)}, bf16[8,64,512]{2,1,0:T(8,128)(2,1)}, u32[]{:S(2)}, u32[]{:S(2)}) collective-permute-start(bf16[8,64,512]{2,1,0:T(8,128)(2,1)S(1)} %pad_maximum_fusion.3.refs_1_), channel_id=1, source_target_pairs={{0,1},{1,2},{2,3},{3,0},{4,5},{5,6},{6,7},{7,4},{8,9},{9,10},{10,1... | collective-permute-start | bytes 1572872 | tf_op jit(solution)/shard_map/ppermute | solution.py:28
  52.7 15.3 %collective-permute-start.33 = (bf16[8,64,512]{2,1,0:T(8,128)(2,1)S(1)}, bf16[8,64,512]{2,1,0:T(8,128)(2,1)}, u32[]{:S(2)}, u32[]{:S(2)}) collective-permute-start(bf16[8,64,512]{2,1,0:T(8,128)(2,1)S(1)} %pad_maximum_fusion.4.refs_1_), channel_id=1, source_target_pairs={{0,12},{1,13},{2,14},{3,15},{4,0},{5,1},{6,2},{7,3},{8,4},{9,5},{1... | collective-permute-start | bytes 1572872 | tf_op jit(solution)/shard_map/ppermute | solution.py:24
  54.2 15.5 %collective-permute-start.31 = (bf16[8,64,512]{2,1,0:T(8,128)(2,1)S(1)}, bf16[8,64,512]{2,1,0:T(8,128)(2,1)}, u32[]{:S(2)}, u32[]{:S(2)}) collective-permute-start(bf16[8,64,512]{2,1,0:T(8,128)(2,1)S(1)} %pad_maximum_fusion.4.refs_1_), channel_id=1, source_target_pairs={{0,4},{1,5},{2,6},{3,7},{4,8},{5,9},{6,10},{7,11},{8,12},{9,13},{1... | collective-permute-start | bytes 1572872 | tf_op jit(solution)/shard_map/ppermute | solution.py:24
  56.5 18.0 %collective-permute-start.12 = (bf16[1,64,3200]{2,1,0:T(8,128)(2,1)}, bf16[1,64,3200]{2,1,0:T(8,128)(2,1)}, u32[]{:S(2)}, u32[]{:S(2)}) collective-permute-start(bf16[1,64,3200]{2,1,0:T(8,128)(2,1)} %slice.161), channel_id=1, source_target_pairs={{0,32},{16,48},{32,64},{48,80},{64,96},{80,112},{96,0},{112,16},{1... | collective-permute-start | bytes 1228808 | tf_op jit(solution)/shard_map/ppermute | solution.py:16
  62.5 13.1 %collective-permute-start.18 = (bf16[1,64,3200]{2,1,0:T(8,128)(2,1)}, bf16[1,64,3200]{2,1,0:T(8,128)(2,1)}, u32[]{:S(2)}, u32[]{:S(2)}) collective-permute-start(bf16[1,64,3200]{2,1,0:T(8,128)(2,1)} %slice.175), channel_id=1, source_target_pairs={{0,96},{16,112},{32,0},{48,16},{64,32},{80,48},{96,64},{112,80},{1... | collective-permute-start | bytes 1228808 | tf_op jit(solution)/shard_map/ppermute | solution.py:16
  64.2 26.3 %collective-permute-start.27 = (bf16[4,64,512]{2,1,0:T(8,128)(2,1)}, bf16[4,64,512]{2,1,0:T(8,128)(2,1)S(1)}, u32[]{:S(2)}, u32[]{:S(2)}) collective-permute-start(bf16[4,64,512]{2,1,0:T(8,128)(2,1)} %slice.178), channel_id=1, source_target_pairs={{0,3},{1,0},{2,1},{3,2},{4,7},{5,4},{6,5},{7,6},{8,11},{9,8},{10,9... | collective-permute-start | bytes 786440 | tf_op jit(solution)/shard_map/ppermute | solution.py:28
  68.0 22.6 %collective-permute-start.25 = (bf16[4,64,512]{2,1,0:T(8,128)(2,1)}, bf16[4,64,512]{2,1,0:T(8,128)(2,1)}, u32[]{:S(2)}, u32[]{:S(2)}) collective-permute-start(bf16[4,64,512]{2,1,0:T(8,128)(2,1)} %slice.177), channel_id=1, source_target_pairs={{0,1},{1,2},{2,3},{3,0},{4,5},{5,6},{6,7},{7,4},{8,9},{9,10},{10,1... | collective-permute-start | bytes 786440 | tf_op jit(solution)/shard_map/ppermute | solution.py:28
  69.6 20.9 %collective-permute-start.34 = (bf16[4,64,512]{2,1,0:T(8,128)(2,1)}, bf16[4,64,512]{2,1,0:T(8,128)(2,1)S(1)}, u32[]{:S(2)}, u32[]{:S(2)}) collective-permute-start(bf16[4,64,512]{2,1,0:T(8,128)(2,1)} %slice.181), channel_id=1, source_target_pairs={{0,12},{1,13},{2,14},{3,15},{4,0},{5,1},{6,2},{7,3},{8,4},{9,5},{1... | collective-permute-start | bytes 786440 | tf_op jit(solution)/shard_map/ppermute | solution.py:24
  74.5 16.1 %collective-permute-start.32 = (bf16[4,64,512]{2,1,0:T(8,128)(2,1)}, bf16[4,64,512]{2,1,0:T(8,128)(2,1)}, u32[]{:S(2)}, u32[]{:S(2)}) collective-permute-start(bf16[4,64,512]{2,1,0:T(8,128)(2,1)} %slice.180), channel_id=1, source_target_pairs={{0,4},{1,5},{2,6},{3,7},{4,8},{5,9},{6,10},{7,11},{8,12},{9,13},{1... | collective-permute-start | bytes 786440 | tf_op jit(solution)/shard_map/ppermute | solution.py:24
  75.6 11.0 %collective-permute-start.13 = (s32[4,16,2]{0,2,1:T(2,128)S(1)}, s32[4,16,2]{0,2,1:T(2,128)S(1)}, u32[]{:S(2)}, u32[]{:S(2)}) collective-permute-start(s32[4,16,2]{0,2,1:T(2,128)S(1)} %bitcast.45), channel_id=1, source_target_pairs={{0,16},{16,0},{32,48},{48,32},{64,80},{80,64},{96,112},{112,96},{1... | collective-permute-start | bytes 1544 | tf_op jit(solution)/shard_map/ppermute | solution.py:20
  91.6 15.0 %collective-permute-start.40 = (bf16[2,64,1536]{2,1,0:T(8,128)(2,1)S(1)}, bf16[2,64,1536]{2,1,0:T(8,128)(2,1)S(1)}, u32[]{:S(2)}, u32[]{:S(2)}) collective-permute-start(bf16[2,64,1536]{2,1,0:T(8,128)(2,1)S(1)} %get-tuple-element.59), channel_id=1, source_target_pairs={{0,3},{1,0},{2,1},{3,2},{4,7},{5,4},{6,5},{7,6},{8,11},{9,8},{10,9... | collective-permute-start | bytes 1179656 | tf_op jit(solution)/shard_map/ppermute | solution.py:28
  94.8 12.3 %collective-permute-start.39 = (bf16[2,64,1536]{2,1,0:T(8,128)(2,1)S(1)}, bf16[2,64,1536]{2,1,0:T(8,128)(2,1)S(1)}, u32[]{:S(2)}, u32[]{:S(2)}) collective-permute-start(bf16[2,64,1536]{2,1,0:T(8,128)(2,1)S(1)} %get-tuple-element.59), channel_id=1, source_target_pairs={{0,1},{1,2},{2,3},{3,0},{4,5},{5,6},{6,7},{7,4},{8,9},{9,10},{10,1... | collective-permute-start | bytes 1179656 | tf_op jit(solution)/shard_map/ppermute | solution.py:28
  94.8 12.5 %collective-permute-start.36 = (bf16[2,64,1536]{2,1,0:T(8,128)(2,1)S(1)}, bf16[2,64,1536]{2,1,0:T(8,128)(2,1)S(1)}, u32[]{:S(2)}, u32[]{:S(2)}) collective-permute-start(bf16[2,64,1536]{2,1,0:T(8,128)(2,1)S(1)} %get-tuple-element.62), channel_id=1, source_target_pairs={{0,12},{1,13},{2,14},{3,15},{4,0},{5,1},{6,2},{7,3},{8,4},{9,5},{1... | collective-permute-start | bytes 1179656 | tf_op jit(solution)/shard_map/ppermute | solution.py:24
  103.4 33.1 %collective-permute-start.16 = (bf16[2,512,256]{2,1,0:T(8,128)(2,1)S(1)}, bf16[2,512,256]{2,1,0:T(8,128)(2,1)S(1)}, u32[]{:S(2)}, u32[]{:S(2)}) collective-permute-start(bf16[2,512,256]{2,1,0:T(8,128)(2,1)S(1)} %get-tuple-element.55), channel_id=1, source_target_pairs={{0,96},{16,112},{32,0},{48,16},{64,32},{80,48},{96,64},{112,80},{1... | collective-permute-start | bytes 1572872 | tf_op jit(solution)/shard_map/ppermute | solution.py:16
  103.4 33.1 %collective-permute-start.15 = (bf16[2,512,256]{2,1,0:T(8,128)(2,1)S(1)}, bf16[2,512,256]{2,1,0:T(8,128)(2,1)S(1)}, u32[]{:S(2)}, u32[]{:S(2)}) collective-permute-start(bf16[2,512,256]{2,1,0:T(8,128)(2,1)S(1)} %get-tuple-element.56), channel_id=1, source_target_pairs={{0,64},{16,80},{32,96},{48,112},{64,0},{80,16},{96,32},{112,48},{1... | collective-permute-start | bytes 1572872 | tf_op jit(solution)/shard_map/ppermute | solution.py:16
  106.6 29.9 %collective-permute-start.14 = (bf16[2,512,256]{2,1,0:T(8,128)(2,1)S(1)}, bf16[2,512,256]{2,1,0:T(8,128)(2,1)S(1)}, u32[]{:S(2)}, u32[]{:S(2)}) collective-permute-start(bf16[2,512,256]{2,1,0:T(8,128)(2,1)S(1)} %get-tuple-element.57), channel_id=1, source_target_pairs={{0,32},{16,48},{32,64},{48,80},{64,96},{80,112},{96,0},{112,16},{1... | collective-permute-start | bytes 1572872 | tf_op jit(solution)/shard_map/ppermute | solution.py:16
  107.1 11.7 %collective-permute-start.35 = (bf16[2,64,1536]{2,1,0:T(8,128)(2,1)S(1)}, bf16[2,64,1536]{2,1,0:T(8,128)(2,1)S(1)}, u32[]{:S(2)}, u32[]{:S(2)}) collective-permute-start(bf16[2,64,1536]{2,1,0:T(8,128)(2,1)S(1)} %get-tuple-element.62), channel_id=1, source_target_pairs={{0,4},{1,5},{2,6},{3,7},{4,8},{5,9},{6,10},{7,11},{8,12},{9,13},{1... | collective-permute-start | bytes 1179656 | tf_op jit(solution)/shard_map/ppermute | solution.py:24
  107.3 20.9 %collective-permute-start.42 = (bf16[1,64,1536]{2,1,0:T(8,128)(2,1)S(1)}, bf16[1,64,1536]{2,1,0:T(8,128)(2,1)S(1)}, u32[]{:S(2)}, u32[]{:S(2)}) collective-permute-start(bf16[1,64,1536]{2,1,0:T(8,128)(2,1)S(1)} %slice.185), channel_id=1, source_target_pairs={{0,3},{1,0},{2,1},{3,2},{4,7},{5,4},{6,5},{7,6},{8,11},{9,8},{10,9... | collective-permute-start | bytes 589832 | tf_op jit(solution)/shard_map/ppermute | solution.py:28
  136.5 32.6 %collective-permute-start.44 = (bf16[8,64,1536]{2,1,0:T(8,128)(2,1)}, bf16[8,64,1536]{2,1,0:T(8,128)(2,1)S(1)}, u32[]{:S(2)}, u32[]{:S(2)}) collective-permute-start(bf16[8,64,1536]{2,1,0:T(8,128)(2,1)} %constant_dynamic-update-slice_fusion.2.refs_1_), channel_id=1, source_target_pairs={{0,3},{1,0},{2,1},{3,2},{4,7},{5,4},{6,5},{7,6},{8,11},{9,8},{10,9... | collective-permute-start | bytes 4718600 | tf_op jit(solution)/shard_map/ppermute | solution.py:28
  137.5 33.8 %collective-permute-start.43 = (bf16[8,64,1536]{2,1,0:T(8,128)(2,1)}, bf16[8,64,1536]{2,1,0:T(8,128)(2,1)S(1)}, u32[]{:S(2)}, u32[]{:S(2)}) collective-permute-start(bf16[8,64,1536]{2,1,0:T(8,128)(2,1)} %constant_dynamic-update-slice_fusion.2.refs_1_), channel_id=1, source_target_pairs={{0,1},{1,2},{2,3},{3,0},{4,5},{5,6},{6,7},{7,4},{8,9},{9,10},{10,1... | collective-permute-start | bytes 4718600 | tf_op jit(solution)/shard_map/ppermute | solution.py:28
  138.6 32.7 %collective-permute-start.46 = (bf16[8,64,1536]{2,1,0:T(8,128)(2,1)}, bf16[8,64,1536]{2,1,0:T(8,128)(2,1)}, u32[]{:S(2)}, u32[]{:S(2)}) collective-permute-start(bf16[8,64,1536]{2,1,0:T(8,128)(2,1)} %constant_dynamic-update-slice_fusion.7.refs_1_), channel_id=1, source_target_pairs={{0,12},{1,13},{2,14},{3,15},{4,0},{5,1},{6,2},{7,3},{8,4},{9,5},{1... | collective-permute-start | bytes 4718600 | tf_op jit(solution)/shard_map/ppermute | solution.py:24
  138.6 33.3 %collective-permute-start.45 = (bf16[8,64,1536]{2,1,0:T(8,128)(2,1)}, bf16[8,64,1536]{2,1,0:T(8,128)(2,1)}, u32[]{:S(2)}, u32[]{:S(2)}) collective-permute-start(bf16[8,64,1536]{2,1,0:T(8,128)(2,1)} %constant_dynamic-update-slice_fusion.7.refs_1_), channel_id=1, source_target_pairs={{0,4},{1,5},{2,6},{3,7},{4,8},{5,9},{6,10},{7,11},{8,12},{9,13},{1... | collective-permute-start | bytes 4718600 | tf_op jit(solution)/shard_map/ppermute | solution.py:24
  172.0 16.1 %collective-permute-start.50 = (bf16[4,64,1536]{2,1,0:T(8,128)(2,1)S(1)}, bf16[4,64,1536]{2,1,0:T(8,128)(2,1)S(1)}, u32[]{:S(2)}, u32[]{:S(2)}) collective-permute-start(bf16[4,64,1536]{2,1,0:T(8,128)(2,1)S(1)} %slice.156), channel_id=1, source_target_pairs={{0,3},{1,0},{2,1},{3,2},{4,7},{5,4},{6,5},{7,6},{8,11},{9,8},{10,9... | collective-permute-start | bytes 2359304 | tf_op jit(solution)/shard_map/ppermute | solution.py:28
  174.6 15.3 %collective-permute-start.49 = (bf16[4,64,1536]{2,1,0:T(8,128)(2,1)S(1)}, bf16[4,64,1536]{2,1,0:T(8,128)(2,1)S(1)}, u32[]{:S(2)}, u32[]{:S(2)}) collective-permute-start(bf16[4,64,1536]{2,1,0:T(8,128)(2,1)S(1)} %slice.155), channel_id=1, source_target_pairs={{0,1},{1,2},{2,3},{3,0},{4,5},{5,6},{6,7},{7,4},{8,9},{9,10},{10,1... | collective-permute-start | bytes 2359304 | tf_op jit(solution)/shard_map/ppermute | solution.py:28
  177.0 15.6 %collective-permute-start.48 = (bf16[4,64,1536]{2,1,0:T(8,128)(2,1)S(1)}, bf16[4,64,1536]{2,1,0:T(8,128)(2,1)S(1)}, u32[]{:S(2)}, u32[]{:S(2)}) collective-permute-start(bf16[4,64,1536]{2,1,0:T(8,128)(2,1)S(1)} %slice.154), channel_id=1, source_target_pairs={{0,12},{1,13},{2,14},{3,15},{4,0},{5,1},{6,2},{7,3},{8,4},{9,5},{1... | collective-permute-start | bytes 2359304 | tf_op jit(solution)/shard_map/ppermute | solution.py:24
  177.3 15.3 %collective-permute-start.47 = (bf16[4,64,1536]{2,1,0:T(8,128)(2,1)S(1)}, bf16[4,64,1536]{2,1,0:T(8,128)(2,1)S(1)}, u32[]{:S(2)}, u32[]{:S(2)}) collective-permute-start(bf16[4,64,1536]{2,1,0:T(8,128)(2,1)S(1)} %slice.153), channel_id=1, source_target_pairs={{0,4},{1,5},{2,6},{3,7},{4,8},{5,9},{6,10},{7,11},{8,12},{9,13},{1... | collective-permute-start | bytes 2359304 | tf_op jit(solution)/shard_map/ppermute | solution.py:24
  (44 other events, 285.9 us)

commit v2 on v0

v2 whole, which is shorter than its diff:
```python
import jax
import jax.numpy as jnp
from jax import lax
from jax.experimental import pallas as pl
from jax.experimental.pallas import tpu as pltpu
from jax.sharding import PartitionSpec as P

ORDER = (0, -1, 1, 2)
VMEM = 14 * 1024 * 1024
BESIDE = 128
WEIGHT = 2
PARAMS = pltpu.CompilerParams(vmem_limit_bytes=VMEM)
ANY = pl.BlockSpec(memory_space=pl.ANY)


def shift_row_x(v, d):
    return lax.ppermute(v, "row", [(2 * x + k, 2 * ((x + d) % 4) + k) for x in range(4) for k in range(2)])


def swap_core(v):
    return lax.ppermute(v, "row", [(r, r ^ 1) for r in range(8)])


def shift_z(v, d):
    return lax.ppermute(v, "col", [(4 * z + y, 4 * ((z + d) % 4) + y) for z in range(4) for y in range(4)])


def shift_y(v, d):
    return lax.ppermute(v, "col", [(4 * z + y, 4 * z + (y + d) % 4) for z in range(4) for y in range(4)])


def halves(minus, plus, others=()):
    count, b, n = minus.shape
    half, step = count // 2, min(n, 1024)

    def kernel(*refs):
        refs[-2][...] = refs[0][...]
        refs[-1][...] = refs[1][...]

    spec = pl.BlockSpec((half, b, step), lambda i: (0, 0, i))
    return pl.pallas_call(
        kernel,
        grid=(n // step,),
        in_specs=[spec, pl.BlockSpec((half, b, step), lambda i: (1, 0, i))] + [ANY] * len(others),
        out_specs=[spec, spec],
        out_shape=[jax.ShapeDtypeStruct((half, b, n), jnp.bfloat16)] * 2,
        compiler_params=PARAMS,
        cost_estimate=pl.CostEstimate(flops=0, bytes_accessed=4 * b * n * count, transcendentals=0),
        name="halves",
    )(minus, plus, *others)


def relay(v, shift, others=()):
    minus, plus = shift(v, 1), shift(v, -1)
    first, second = halves(minus, plus, others)
    return [v, minus, plus, shift(first, 1), shift(second, -1)]


def join(pieces):
    _, b, n = pieces[0].shape
    step = 512

    def kernel(*refs):
        at = 0
        for ref in refs[:-1]:
            refs[-1][at : at + ref.shape[0]] = ref[...]
            at += ref.shape[0]

    total = sum(p.shape[0] for p in pieces)
    return pl.pallas_call(
        kernel,
        grid=(n // step,),
        in_specs=[pl.BlockSpec((p.shape[0], b, step), lambda i: (0, 0, i)) for p in pieces],
        out_specs=pl.BlockSpec((total, b, step), lambda i: (0, 0, i)),
        out_shape=jax.ShapeDtypeStruct((total, b, n), jnp.bfloat16),
        compiler_params=PARAMS,
        cost_estimate=pl.CostEstimate(flops=0, bytes_accessed=4 * b * n * total, transcendentals=0),
        name="join",
    )(*pieces)


ROW, OTHER, X, CORE, Z, Y, COL = range(7)


def place_of(distance):
    return jnp.where(distance == 0, 0, jnp.where(distance == 3, 1, jnp.where(distance == 1, 2, 3)))


def choose_kernel(at_ref, size_ref, density_ref, own_ref, other_ref, pattern_ref, out_ref):
    t = pl.program_id(0)
    x, core = at_ref[X], at_ref[CORE]
    pair = 2 * lax.rem(x + t // 2, 4) + lax.rem(core + lax.rem(t, 2), 2)
    i32 = jnp.int32
    sub = lax.broadcasted_iota(i32, (8, BESIDE), 0)
    lane = lax.broadcasted_iota(i32, (1, BESIDE), 1)
    unit = lax.rem(lane, 64)
    spot = jnp.zeros_like(sub)
    for i, d in enumerate(ORDER):
        spot = jnp.where(sub // 2 == i, 2 * lax.rem(x + (d + 4), 4), spot)
    spot = spot + lax.rem(sub, 2)
    rows, patterns = [], []
    for b in range(2):
        away_y = lax.rem(2 * core + b - at_ref[Y] + 4, 4)
        away_z = lax.rem(x - at_ref[Z] + 4, 4)
        piece = 4 * place_of(away_y) + place_of(away_z)
        own, other = own_ref[piece].astype(i32), other_ref[piece].astype(i32)
        atoms = []
        for names in (jnp.where(core == 0, own, other), jnp.where(core == 0, other, own)):
            match = names // 8 == pair
            low = jnp.min(jnp.where(match, spot, 99), axis=0, keepdims=True)
            high = jnp.max(jnp.where(match, spot, -1), axis=0, keepdims=True)
            atom = names - 8 * pair
            one = jnp.max(jnp.where(match & (spot == low), atom, -1), axis=0, keepdims=True)
            two = jnp.max(jnp.where(match & (spot == high) & (high > low), atom, -1), axis=0, keepdims=True)
            atoms.append((one, two))
        slots = [jnp.where(atoms[j][0] >= 0, atoms[j][0], atoms[1 - j][1]) for j in range(2)]
        atom = jnp.where(lane < 64, slots[0], slots[1])
        size = jnp.zeros_like(atom)
        pattern = jnp.zeros((8, BESIDE), jnp.float32)
        for j in range(8):
            size = jnp.where(atom == j, size_ref[16 * at_ref[ROW] + 8 * b + j], size)
            pattern = jnp.where(atom == j, pattern_ref[:, 8 * b + j : 8 * b + j + 1].astype(jnp.float32), pattern)
        rows.append(jnp.where((atom >= 0) & (unit < size), (8 * b + atom) * 64 + unit, -1))
        patterns.append(pattern)
    rows, pattern = jnp.concatenate(rows, axis=1), jnp.concatenate(patterns, axis=1)
    hit = lax.broadcasted_iota(i32, (density_ref.shape[1], rows.shape[1]), 0) == rows
    picked = jnp.dot(density_ref[...], hit.astype(jnp.bfloat16), preferred_element_type=jnp.float32)
    row = lax.broadcasted_iota(i32, (64, rows.shape[1]), 0)
    for j in range(8):
        factor = jnp.where(row < size_ref[8 * at_ref[COL] + j], pattern[j : j + 1], 0.0)
        out_ref[0, 64 * j : 64 * j + 64] = (picked[64 * j : 64 * j + 64] * factor).astype(jnp.bfloat16)


def choose_columns(at, sizes, density, own, other, pattern):
    m, width = density.shape
    names = pl.BlockSpec(own.shape, lambda t, p, q: (0, 0, 0))
    return pl.pallas_call(
        choose_kernel,
        grid_spec=pltpu.PrefetchScalarGridSpec(
            num_scalar_prefetch=2,
            grid=(8,),
            in_specs=[
                pl.BlockSpec((m, width), lambda t, p, q: (0, 0)),
                names,
                names,
                pl.BlockSpec(pattern.shape, lambda t, p, q: (0, 0)),
            ],
            out_specs=pl.BlockSpec((1, m, 256), lambda t, p, q: (t, 0, 0)),
        ),
        out_shape=jax.ShapeDtypeStruct((8, m, 256), jnp.bfloat16),
        compiler_params=PARAMS,
        cost_estimate=pl.CostEstimate(flops=2 * m * width * 2048, bytes_accessed=2 * m * (width + 2048), transcendentals=0),
        name="choose_columns",
    )(at, sizes, density, own, other, pattern)


def order_kernel(at_ref, *refs):
    own, other, (left1, left2), (blocks, sems) = refs[:4], refs[4], refs[5:7], refs[7:]
    copies = [pltpu.make_async_copy(own[d].at[0], blocks.at[d], sems.at[d]) for d in range(4)]
    copies += [pltpu.make_async_copy(other.at[d], blocks.at[4 + d], sems.at[4 + d]) for d in range(4)]
    for copy in copies:
        copy.start()
    for copy in copies:
        copy.wait()
    for i in range(16):
        j = (i % 4) * 4 + i // 4
        from_y = lax.rem(at_ref[Y] + (ORDER[i // 4] + 4), 4)
        from_z = lax.rem(at_ref[Z] + (ORDER[i % 4] + 4), 4)
        place = lax.rem(at_ref[X] - from_z + 4, 4) + jnp.where(from_y // 2 == at_ref[CORE], 0, 4)
        block = blocks[place, :, pl.ds(pl.multiple_of(lax.rem(from_y, 2) * 128, 128), 128)]
        left1[:, i * 128 : (i + 1) * 128] = block
        left2[:, j * 128 : (j + 1) * 128] = block


def order_columns(at, own, other):
    m = other.shape[1]
    return pl.pallas_call(
        order_kernel,
        grid_spec=pltpu.PrefetchScalarGridSpec(
            num_scalar_prefetch=1,
            grid=(1,),
            in_specs=[ANY] * 5,
            out_specs=[pl.BlockSpec((m, 2048), lambda i, p: (0, 0))] * 2,
            scratch_shapes=[pltpu.VMEM((8, m, 256), jnp.bfloat16), pltpu.SemaphoreType.DMA((8,))],
        ),
        out_shape=[jax.ShapeDtypeStruct((m, 2048), jnp.bfloat16)] * 2,
        compiler_params=PARAMS,
        cost_estimate=pl.CostEstimate(flops=0, bytes_accessed=8 * 2 * m * 2048, transcendentals=0),
        name="order_columns",
    )(at, *own, other)


def pick_tiles(at, names, pieces, which):
    _, b, n = pieces[0].shape
    step = 1024

    def kernel(at_ref, name_ref, *refs):
        pieces, out = refs[:5], refs[5]
        spots = [2 * lax.rem(at_ref[X] + (d + 4), 4) + s for d in ORDER for s in range(2)]
        match = [(name_ref[j] // 8 == at_ref[which]).astype(jnp.int32) for j in range(8)]
        slots = []
        for j in range(8):
            before = sum(match[i] * (spots[i] < spots[j]).astype(jnp.int32) for i in range(8) if i != j)
            slots.append(jnp.where(at_ref[CORE] == 1, 1 - before, before))
        for s in range(2):
            there = [match[j] * (slots[j] == s).astype(jnp.int32) for j in range(8)]

            @pl.when(sum(there) == 0)
            def _():
                out[s] = jnp.zeros(out.shape[1:], out.dtype)

            for j in range(8):

                @pl.when(there[j] == 1)
                def _():
                    out[s] = pieces[j // 2][j % 2] if j < 6 else pieces[j - 3][0]

    return pl.pallas_call(
        kernel,
        grid_spec=pltpu.PrefetchScalarGridSpec(
            num_scalar_prefetch=2,
            grid=(n // step,),
            in_specs=[pl.BlockSpec((v.shape[0], b, step), lambda i, p, q: (0, 0, i)) for v in pieces],
            out_specs=pl.BlockSpec((2, b, step), lambda i, p, q: (0, 0, i)),
        ),
        out_shape=jax.ShapeDtypeStruct((2, b, n), jnp.bfloat16),
        compiler_params=PARAMS,
        cost_estimate=pl.CostEstimate(flops=0, bytes_accessed=24 * b * n, transcendentals=0),
        name="pick_tiles",
    )(at, names, *pieces)


def merge_tiles(mine, got, cuts):
    _, b, n = mine.shape
    edges = [0, *cuts, n]

    def kernel(mine_ref, got_ref, *outs):
        for out, low, high in zip(outs, edges, edges[1:]):
            out[...] = mine_ref[:, :, low:high] + got_ref[:, :, low:high]

    return pl.pallas_call(
        kernel,
        out_shape=[jax.ShapeDtypeStruct((2, b, v - u), jnp.bfloat16) for u, v in zip(edges, edges[1:])],
        compiler_params=PARAMS,
        cost_estimate=pl.CostEstimate(flops=0, bytes_accessed=12 * b * n, transcendentals=0),
        name="merge_tiles",
    )(mine, got)


def product_kernel(at, count, started, left_ref, *refs):
    total = refs[count][...] if started else None
    for piece in refs[:count]:
        depth = piece.shape[0] * piece.shape[1]
        right = piece[...].reshape(depth, piece.shape[2])
        term = jnp.dot(left_ref[:, at : at + depth], right, preferred_element_type=jnp.float32)
        total = term if total is None else total + term
        at += depth
    refs[-1][...] = total.astype(refs[-1].dtype)


def product(left, at, pieces, n, total=None, out=None, column=0, width=None):
    m = left.shape[0]
    step = 512
    depth = sum(p.shape[0] * p.shape[1] for p in pieces)
    first = column // step
    specs = [pl.BlockSpec(left.shape, lambda i: (0, 0))]
    specs += [pl.BlockSpec(p.shape[:2] + (step,), lambda i: (0, 0, i)) for p in pieces]
    operands = [left, *pieces]
    if total is not None:
        specs.append(pl.BlockSpec((m, step), lambda i: (0, i)))
        operands.append(total)
    alias = {}
    if out is not None:
        specs.append(pl.BlockSpec(memory_space=pl.ANY))
        alias = {len(operands): 0}
        operands.append(out)

    def kernel(*refs):
        product_kernel(at, len(pieces), total is not None, *refs)

    shape = jax.ShapeDtypeStruct((m, n), jnp.float32) if width is None else jax.ShapeDtypeStruct((m, width), jnp.bfloat16)
    return pl.pallas_call(
        kernel,
        grid=(n // step,),
        in_specs=specs,
        out_specs=pl.BlockSpec((m, step), lambda i: (0, first + i)),
        out_shape=shape,
        input_output_aliases=alias,
        compiler_params=PARAMS,
        cost_estimate=pl.CostEstimate(
            flops=2 * WEIGHT * m * depth * n, bytes_accessed=2 * WEIGHT * (left.size + (depth + 2 * m) * n), transcendentals=0
        ),
        name="product",
    )(*operands)


def per_device(blocks, block_atom, block_pair, atom_sizes, density, density_pattern):
    b, width = blocks.shape[1], blocks.shape[2]
    r, c = lax.axis_index("row"), lax.axis_index("col")
    x, k, z, y = r // 2, r % 2, c // 4, c % 4
    i32 = jnp.int32
    at = jnp.stack([r, r + 1 - 2 * k, x, k, z, y, c]).astype(i32)

    def around(v, shift):
        return [v, shift(v, 1), shift(v, -1), shift(v, 2)]

    def forward(sides, shift):
        first, second = halves(*sides)
        return [shift(first, 1), shift(second, -1)]

    name = (8 * block_pair + jnp.clip(block_atom - 8 * c, 0, 7)).astype(jnp.float32)
    name = jnp.stack(around(jnp.broadcast_to(name, (2, BESIDE)), shift_z))
    near = relay(blocks, shift_row_x, (name,))
    name = jnp.concatenate(around(name, shift_y))
    names = jnp.concatenate(around(name, shift_row_x), axis=1)

    here = names[0, :, 0].astype(i32)
    theirs = swap_core(pick_tiles(at, here, near, OTHER))
    v1, v2 = merge_tiles(pick_tiles(at, here, near, ROW), theirs, [width // 2])
    pieces1, pieces2 = relay(v1, shift_z), relay(v2, shift_y)

    chosen = choose_columns(at, atom_sizes, density, names, swap_core(names), density_pattern)
    chosen = chosen.reshape(4, 2, 8 * b, 4 * b)
    own = [chosen[0]] + [shift_row_x(chosen[d], d) for d in (1, 2, 3)]

    g1, g2 = join(pieces1), join(pieces2)
    sides1, sides2 = [shift_y(g1, 1), shift_y(g1, -1)], [shift_z(g2, 1), shift_z(g2, -1)]
    last1, last2 = forward(sides1, shift_y), forward(sides2, shift_z)

    other = swap_core(jnp.stack([piece[1] for piece in own]))
    left1, left2 = order_columns(at, own, other)

    half = width // 2
    total1 = product(left1, 0, [g1, *sides1], half)
    total2 = product(left2, 0, [g2, *sides2], half)
    out = product(left1, 24 * b, last1, half, total1, None, 0, width)
    out = product(left2, 24 * b, last2, half, total2, out, half, width)
    return out[None]


def solution(mesh):
    placed = (
        P("row", "col", None),
        P("row", "col"),
        P("row", "col"),
        P(),
        P("col", "row"),
        P("col", "row"),
    )
    return jax.shard_map(
        per_device, mesh=mesh, in_specs=placed, out_specs=P("row", "col", None), check_vma=False
    )
```

time: 248 us -> 165 us (0.67)
  waiting for transfers between devices: 157 us -> 82.2 us
  starting transfers between devices: 0.08 us -> 47.4 us
  blocking collectives: 36.6 us -> 0 us
  Pallas kernels: 0 us -> 33 us
  local copies, waits for them, and re-layouts: 14.8 us -> 0.57 us
  between operations: 14.5 us -> 0.32 us
  matrix products: 14.1 us -> 0 us
  other arithmetic: 10.2 us -> 0.97 us
    all_gather x3 -> x0, waiting for transfers between devices: 156 us -> none  [the longest x1 104 us: per_device(): lax.all_gather(own_tiles, 'col', axis=0, tiled=True)]
    ppermute x0 -> x35, waiting for transfers between devices: none -> 82.2 us  [the longest x11 38.7 us: shift_y(): lax.ppermute(v, 'col', [(4 * z + y, 4 * z + (y + d) % 4) for z in range(4...]
    ppermute x0 -> x35, starting transfers between devices: none -> 47.4 us  [the longest x11 19.5 us: shift_z(): lax.ppermute(v, 'col', [(4 * z + y, 4 * ((z + d) % 4) + y) for z in range...]
    pallas_call x0 -> x16, Pallas kernels: none -> 33 us  [the longest x4 15.9 us: product(): pl.pallas_call(kernel, grid=(n // step,), in_specs=specs, out_specs=pl.Bl...]
    unnamed x2 -> x0, blocking collectives: 23.9 us -> none
    dot_general x1 -> x0, matrix products: 14.1 us -> none  [per_device(): result = jnp.dot(left_side, right_side, preferred_element_type=jnp.float32)]
    all_gather x1 -> x0, blocking collectives: 12.8 us -> none  [per_device(): lax.all_gather(density_pattern, 'row', axis=1, tiled=True)]
    gather x3 -> x0, local copies, waits for them, and re-layouts: 8.69 us -> none  [the longest x1 4.06 us: per_device(): jnp.take(masked_density, jnp.minimum(panel_atoms, atom_count - 1), axis=1)]
  transfers between devices with their start and end apart: 3 -> 35, of which waited for: 3 -> 17; matrix products, arithmetic and copies ran while one was open for 10% -> 1% of each run, Pallas kernels for 0% -> 16%
where the time goes in v2:
time: 165 us; the launch traced here: 164 us
  waiting for transfers between devices  82.2 us (50%)
  starting transfers between devices  47.4 us (29%)
  Pallas kernels  33 us (20%)
    ppermute x11, waiting for transfers between devices, shift_y(): lax.ppermute(v, 'col', [(4 * z + y, 4 * z + (y + d) % 4) for z in range(4...  38.7 us
    ppermute x10, waiting for transfers between devices, shift_row_x(): lax.ppermute(v, 'row', [(2 * x + k, 2 * ((x + d) % 4) + k) for x in range...  30.8 us
    ppermute x11, starting transfers between devices, shift_z(): lax.ppermute(v, 'col', [(4 * z + y, 4 * ((z + d) % 4) + y) for z in range...  19.5 us
    pallas_call x4, Pallas kernels, product(): pl.pallas_call(kernel, grid=(n // step,), in_specs=specs, out_specs=pl.Bl...  15.9 us
    ppermute x11, starting transfers between devices, shift_y(): lax.ppermute(v, 'col', [(4 * z + y, 4 * z + (y + d) % 4) for z in range(4...  15.5 us
    ppermute x10, starting transfers between devices, shift_row_x(): lax.ppermute(v, 'row', [(2 * x + k, 2 * ((x + d) % 4) + k) for x in range...  11.7 us
    ppermute x11, waiting for transfers between devices, shift_z(): lax.ppermute(v, 'col', [(4 * z + y, 4 * ((z + d) % 4) + y) for z in range...  10.1 us
    pallas_call x2, Pallas kernels, pick_tiles(): pl.pallas_call(kernel, grid_spec=pltpu.PrefetchScalarGridSpec(num_scalar_...  6.65 us
  transfers between devices with their start and end apart: 35, of which 17 were waited for; matrix products, arithmetic and copies ran while one was open for 1% of the time, Pallas kernels for 16%

profile of v2, /device:TPU:6, one launch (start us, length us, event | category | flops | bytes accessed | tf_op | source)
XLA Modules:
  0.0 164.4 jit_solution(15797503758765351586)
XLA Ops:
  0.8 2.4 %collective-permute-start.14 = (bf16[2,64,4096]{2,1,0:T(8,128)(2,1)}, bf16[2,64,4096]{2,1,0:T(8,128)(2,1)S(1)}, u32[]{:S(2)}, u32[]{:S(2)}) collective-permute-start(bf16[2,64,4096]{2,1,0:T(8,128)(2,1)} %refs_0_.3), channel_id=1, source_target_pairs={{0,32},{16,48},{32,64},{48,80},{64,96},{80,112},{96,0},{112,16},{1... | collective-permute-start | bytes 3145736 | tf_op jit(solution)/shard_map/ppermute | solution.py:17
  4.0 3.9 %collective-permute-start.2 = (f32[2,128]{1,0:T(2,128)S(1)}, f32[2,128]{1,0:T(2,128)S(1)}, u32[]{:S(2)}, u32[]{:S(2)}) collective-permute-start(f32[2,128]{1,0:T(2,128)S(1)} %broadcast_in_dim.8), channel_id=1, source_target_pairs={{0,8},{1,9},{2,10},{3,11},{4,12},{5,13},{6,14},{7,15},{8,0},{9,1},... | collective-permute-start | bytes 3080 | tf_op jit(solution)/shard_map/ppermute | solution.py:25
  11.4 1.9 %collective-permute-done = f32[2,128]{1,0:T(2,128)S(1)} collective-permute-done((f32[2,128]{1,0:T(2,128)S(1)}, f32[2,128]{1,0:T(2,128)S(1)}, u32[]{:S(2)}, u32[]{:S(2)}) %collective-permute-start) | collective-permute-done | bytes 1056 | tf_op jit(solution)/shard_map/ppermute | solution.py:25
  13.4 3.2 %collective-permute-start.5 = (f32[4,2,128]{2,1,0:T(2,128)S(1)}, f32[4,2,128]{2,1,0:T(2,128)S(1)}, u32[]{:S(2)}, u32[]{:S(2)}) collective-permute-start(f32[4,2,128]{2,1,0:T(2,128)S(1)} %pad_maximum_fusion.2.refs_2_), channel_id=1, source_target_pairs={{0,2},{1,3},{2,0},{3,1},{4,6},{5,7},{6,4},{7,5},{8,10},{9,11},{10,... | collective-permute-start | bytes 12296 | tf_op jit(solution)/shard_map/ppermute | solution.py:29
  18.7 7.6 %collective-permute-done.15.refs_1_.refs_2_ = bf16[2,64,4096]{2,1,0:T(8,128)(2,1)S(1)} collective-permute-done((bf16[2,64,4096]{2,1,0:T(8,128)(2,1)}, bf16[2,64,4096]{2,1,0:T(8,128)(2,1)S(1)}, u32[]{:S(2)}, u32[]{:S(2)}) %collective-permute-start.15) | collective-permute-done | bytes 1048608 | tf_op jit(solution)/shard_map/ppermute | solution.py:17
  28.0 3.0 %collective-permute-start.16 = (bf16[1,64,4096]{2,1,0:T(8,128)(2,1)}, bf16[1,64,4096]{2,1,0:T(8,128)(2,1)}, u32[]{:S(2)}, u32[]{:S(2)}) collective-permute-start(bf16[1,64,4096]{2,1,0:T(8,128)(2,1)} %get-tuple-element.20), channel_id=1, source_target_pairs={{0,32},{16,48},{32,64},{48,80},{64,96},{80,112},{96,0},{112,16},{1... | collective-permute-start | bytes 1572872 | tf_op jit(solution)/shard_map/ppermute | solution.py:17
  32.5 2.6 %collective-permute-start.7 = (f32[16,2,128]{2,1,0:T(2,128)S(1)}, f32[16,2,128]{2,1,0:T(2,128)S(1)}, u32[]{:S(2)}, u32[]{:S(2)}) collective-permute-start(f32[16,2,128]{2,1,0:T(2,128)S(1)} %constant_dynamic-update-slice_fusion), channel_id=1, source_target_pairs={{0,96},{16,112},{32,0},{48,16},{64,32},{80,48},{96,64},{112,80},{1... | collective-permute-start | bytes 49160 | tf_op jit(solution)/shard_map/ppermute | solution.py:17
  35.8 7.8 %collective-permute-done.8 = f32[16,2,128]{2,1,0:T(2,128)S(1)} collective-permute-done((f32[16,2,128]{2,1,0:T(2,128)S(1)}, f32[16,2,128]{2,1,0:T(2,128)S(1)}, u32[]{:S(2)}, u32[]{:S(2)}) %collective-permute-start.8) | collective-permute-done | bytes 16416 | tf_op jit(solution)/shard_map/ppermute | solution.py:17
  45.4 3.3 %pick_tiles.3 = bf16[2,64,4096]{2,1,0:T(8,128)(2,1)S(1)} custom-call(s32[7]{0:T(128)S(1)} %stack.46.at_ref, s32[8]{0:T(128)S(1)} %fusion.name_ref, bf16[2,64,4096]{2,1,0:T(8,128)(2,1)S(1)} %copy-done, bf16[2,64,4096]{2,1,0:T(8,128)(2,1)S(1)} %collective-permute-done.14.refs_0_.refs_1_, bf16[2,64,4096]{2,1,0:T(8,128)(2,1)S(1)} %collective-permute-done.15.refs_1_.refs_2_, ...), custom_call_target="tpu_custom_call" | custom-call | bytes 6291456 | tf_op jit(solution)/shard_map/pick_tiles/pallas_call | solution.py:218
  49.3 3.3 %pick_tiles.2.mine_ref = bf16[2,64,4096]{2,1,0:T(8,128)(2,1)S(1)} custom-call(s32[7]{0:T(128)S(1)} %stack.46.at_ref, s32[8]{0:T(128)S(1)} %fusion.name_ref, bf16[2,64,4096]{2,1,0:T(8,128)(2,1)S(1)} %copy-done, bf16[2,64,4096]{2,1,0:T(8,128)(2,1)S(1)} %collective-permute-done.14.refs_0_.refs_1_, ...), custom_call_target="tpu_custom_call" | custom-call | bytes 6291456 | tf_op jit(solution)/shard_map/pick_tiles/pallas_call | solution.py:218
  52.8 4.0 %collective-permute-start.28 = (bf16[2,64,2048]{2,1,0:T(8,128)(2,1)S(1)}, bf16[2,64,2048]{2,1,0:T(8,128)(2,1)S(1)}, u32[]{:S(2)}, u32[]{:S(2)}) collective-permute-start(bf16[2,64,2048]{2,1,0:T(8,128)(2,1)S(1)} %get-tuple-element.28.refs_0_), channel_id=1, source_target_pairs={{0,12},{1,13},{2,14},{3,15},{4,0},{5,1},{6,2},{7,3},{8,4},{9,5},{1... | collective-permute-start | bytes 1572872 | tf_op jit(solution)/shard_map/ppermute | solution.py:25
  56.9 4.8 %choose_columns.1 = bf16[8,512,256]{2,1,0:T(8,128)(2,1)S(1)} custom-call(s32[7]{0:T(128)S(1)} %stack.46.at_ref, s32[128]{0:T(128)S(1)} %copy-done.3, bf16[512,1024]{1,0:T(8,128)(2,1)S(1)} %copy-done.1, f32[16,8,128]{2,1,0:T(8,128)S(1)} %pad_maximum_fusion.1.own_ref, f32[16,8,128]{2,1,0:T(8,128)S(1)} %collective-permute-done.9.other_ref, s32[8,16]{1,0:T(8,128)S(1)} %copy-done.2), custom_call_target="tpu_custom_call" | custom-call | flops 2147483648 | bytes 3145728 | tf_op jit(solution)/shard_map/choose_columns/pallas_call | solution.py:137
  61.7 3.2 %collective-permute-start.20 = (bf16[2,64,2048]{2,1,0:T(8,128)(2,1)S(1)}, bf16[2,64,2048]{2,1,0:T(8,128)(2,1)S(1)}, u32[]{:S(2)}, u32[]{:S(2)}) collective-permute-start(bf16[2,64,2048]{2,1,0:T(8,128)(2,1)S(1)} %get-tuple-element.22.refs_0_), channel_id=1, source_target_pairs={{0,3},{1,0},{2,1},{3,2},{4,7},{5,4},{6,5},{7,6},{8,11},{9,8},{10,9... | collective-permute-start | bytes 1572872 | tf_op jit(solution)/shard_map/ppermute | solution.py:29
  65.1 3.3 %collective-permute-done.28.refs_1_.refs_2_ = bf16[2,64,2048]{2,1,0:T(8,128)(2,1)S(1)} collective-permute-done((bf16[2,64,2048]{2,1,0:T(8,128)(2,1)S(1)}, bf16[2,64,2048]{2,1,0:T(8,128)(2,1)S(1)}, u32[]{:S(2)}, u32[]{:S(2)}) %collective-permute-start.28) | collective-permute-done | bytes 524320 | tf_op jit(solution)/shard_map/ppermute | solution.py:25
  68.4 3.4 %collective-permute-done.27.refs_0_.refs_1_ = bf16[2,64,2048]{2,1,0:T(8,128)(2,1)S(1)} collective-permute-done((bf16[2,64,2048]{2,1,0:T(8,128)(2,1)S(1)}, bf16[2,64,2048]{2,1,0:T(8,128)(2,1)S(1)}, u32[]{:S(2)}, u32[]{:S(2)}) %collective-permute-start.27) | collective-permute-done | bytes 524320 | tf_op jit(solution)/shard_map/ppermute | solution.py:25
  72.0 3.2 %collective-permute-start.30 = (bf16[1,64,2048]{2,1,0:T(8,128)(2,1)S(1)}, bf16[1,64,2048]{2,1,0:T(8,128)(2,1)S(1)}, u32[]{:S(2)}, u32[]{:S(2)}) collective-permute-start(bf16[1,64,2048]{2,1,0:T(8,128)(2,1)S(1)} %get-tuple-element.30), channel_id=1, source_target_pairs={{0,12},{1,13},{2,14},{3,15},{4,0},{5,1},{6,2},{7,3},{8,4},{9,5},{1... | collective-permute-start | bytes 786440 | tf_op jit(solution)/shard_map/ppermute | solution.py:25
  76.1 3.4 %collective-permute-done.19.refs_0_.refs_1_ = bf16[2,64,2048]{2,1,0:T(8,128)(2,1)S(1)} collective-permute-done((bf16[2,64,2048]{2,1,0:T(8,128)(2,1)S(1)}, bf16[2,64,2048]{2,1,0:T(8,128)(2,1)S(1)}, u32[]{:S(2)}, u32[]{:S(2)}) %collective-permute-start.19) | collective-permute-done | bytes 524320 | tf_op jit(solution)/shard_map/ppermute | solution.py:29
  79.7 3.2 %collective-permute-start.22 = (bf16[1,64,2048]{2,1,0:T(8,128)(2,1)S(1)}, bf16[1,64,2048]{2,1,0:T(8,128)(2,1)S(1)}, u32[]{:S(2)}, u32[]{:S(2)}) collective-permute-start(bf16[1,64,2048]{2,1,0:T(8,128)(2,1)S(1)} %get-tuple-element.24), channel_id=1, source_target_pairs={{0,3},{1,0},{2,1},{3,2},{4,7},{5,4},{6,5},{7,6},{8,11},{9,8},{10,9... | collective-permute-start | bytes 786440 | tf_op jit(solution)/shard_map/ppermute | solution.py:29
  84.4 3.4 %collective-permute-done.21.refs_3_ = bf16[1,64,2048]{2,1,0:T(8,128)(2,1)S(1)} collective-permute-done((bf16[1,64,2048]{2,1,0:T(8,128)(2,1)S(1)}, bf16[1,64,2048]{2,1,0:T(8,128)(2,1)S(1)}, u32[]{:S(2)}, u32[]{:S(2)}) %collective-permute-start.21) | collective-permute-done | bytes 262176 | tf_op jit(solution)/shard_map/ppermute | solution.py:29
  90.3 3.0 %collective-permute-start.24 = (bf16[8,64,2048]{2,1,0:T(8,128)(2,1)S(1)}, bf16[8,64,2048]{2,1,0:T(8,128)(2,1)S(1)}, u32[]{:S(2)}, u32[]{:S(2)}) collective-permute-start(bf16[8,64,2048]{2,1,0:T(8,128)(2,1)S(1)} %join.2.refs_1_), channel_id=1, source_target_pairs={{0,12},{1,13},{2,14},{3,15},{4,0},{5,1},{6,2},{7,3},{8,4},{9,5},{1... | collective-permute-start | bytes 6291464 | tf_op jit(solution)/shard_map/ppermute | solution.py:25
  93.3 3.1 %collective-permute-done.11.refs_2_ = bf16[2,512,256]{2,1,0:T(8,128)(2,1)S(1)} collective-permute-done((bf16[2,512,256]{2,1,0:T(8,128)(2,1)S(1)}, bf16[2,512,256]{2,1,0:T(8,128)(2,1)S(1)}, u32[]{:S(2)}, u32[]{:S(2)}) %collective-permute-start.11) | collective-permute-done | bytes 524320 | tf_op jit(solution)/shard_map/ppermute | solution.py:17
  96.7 10.6 %collective-permute-done.10.refs_1_ = bf16[2,512,256]{2,1,0:T(8,128)(2,1)S(1)} collective-permute-done((bf16[2,512,256]{2,1,0:T(8,128)(2,1)S(1)}, bf16[2,512,256]{2,1,0:T(8,128)(2,1)S(1)}, u32[]{:S(2)}, u32[]{:S(2)}) %collective-permute-start.10) | collective-permute-done | bytes 524320 | tf_op jit(solution)/shard_map/ppermute | solution.py:17
  107.6 2.6 %collective-permute-done.13.refs_4_ = bf16[4,512,256]{2,1,0:T(8,128)(2,1)S(1)} collective-permute-done((bf16[4,512,256]{2,1,0:T(8,128)(2,1)S(1)}, bf16[4,512,256]{2,1,0:T(8,128)(2,1)S(1)}, u32[]{:S(2)}, u32[]{:S(2)}) %collective-permute-start.13) | collective-permute-done | bytes 1048608 | tf_op jit(solution)/shard_map/ppermute | solution.py:21
  111.8 20.2 %collective-permute-done.32.refs_1_.refs_3_ = bf16[8,64,2048]{2,1,0:T(8,128)(2,1)S(1)} collective-permute-done((bf16[8,64,2048]{2,1,0:T(8,128)(2,1)S(1)}, bf16[8,64,2048]{2,1,0:T(8,128)(2,1)S(1)}, u32[]{:S(2)}, u32[]{:S(2)}) %collective-permute-start.32) | collective-permute-done | bytes 2097184 | tf_op jit(solution)/shard_map/ppermute | solution.py:29
  132.0 2.3 %collective-permute-done.31.refs_0_.refs_2_ = bf16[8,64,2048]{2,1,0:T(8,128)(2,1)S(1)} collective-permute-done((bf16[8,64,2048]{2,1,0:T(8,128)(2,1)S(1)}, bf16[8,64,2048]{2,1,0:T(8,128)(2,1)S(1)}, u32[]{:S(2)}, u32[]{:S(2)}) %collective-permute-start.31) | collective-permute-done | bytes 2097184 | tf_op jit(solution)/shard_map/ppermute | solution.py:29
  134.8 3.2 %collective-permute-start.34 = (bf16[4,64,2048]{2,1,0:T(8,128)(2,1)S(1)}, bf16[4,64,2048]{2,1,0:T(8,128)(2,1)S(1)}, u32[]{:S(2)}, u32[]{:S(2)}) collective-permute-start(bf16[4,64,2048]{2,1,0:T(8,128)(2,1)S(1)} %get-tuple-element.32), channel_id=1, source_target_pairs={{0,3},{1,0},{2,1},{3,2},{4,7},{5,4},{6,5},{7,6},{8,11},{9,8},{10,9... | collective-permute-start | bytes 3145736 | tf_op jit(solution)/shard_map/ppermute | solution.py:29
  138.6 3.2 %collective-permute-start.26 = (bf16[4,64,2048]{2,1,0:T(8,128)(2,1)S(1)}, bf16[4,64,2048]{2,1,0:T(8,128)(2,1)S(1)}, u32[]{:S(2)}, u32[]{:S(2)}) collective-permute-start(bf16[4,64,2048]{2,1,0:T(8,128)(2,1)S(1)} %get-tuple-element.26), channel_id=1, source_target_pairs={{0,12},{1,13},{2,14},{3,15},{4,0},{5,1},{6,2},{7,3},{8,4},{9,5},{1... | collective-permute-start | bytes 3145736 | tf_op jit(solution)/shard_map/ppermute | solution.py:25
  141.8 4.7 %product.5.refs_3_ = f32[512,2048]{1,0:T(8,128)S(1)} custom-call(bf16[512,2048]{1,0:T(8,128)(2,1)S(1)} %get-tuple-element.27.refs_0_, bf16[8,64,2048]{2,1,0:T(8,128)(2,1)S(1)} %join.3.refs_1_, bf16[8,64,2048]{2,1,0:T(8,128)(2,1)S(1)} %collective-permute-done.31.refs_0_.refs_2_, bf16[8,64,2048]{2,1,0:T(8,128)(2,1)S(1)} %collective-permute-done.32.refs_1_.refs_3_), custom_call_target="tpu_custom_call" | custom-call | flops 6442450944 | bytes 25165824 | tf_op jit(solution)/shard_map/product/pallas_call | solution.py:282
  146.5 4.7 %product.4.refs_3_ = f32[512,2048]{1,0:T(8,128)S(1)} custom-call(bf16[512,2048]{1,0:T(8,128)(2,1)S(1)} %get-tuple-element.19.refs_0_, bf16[8,64,2048]{2,1,0:T(8,128)(2,1)S(1)} %join.2.refs_1_, bf16[8,64,2048]{2,1,0:T(8,128)(2,1)S(1)} %collective-permute-done.23.refs_0_.refs_2_, bf16[8,64,2048]{2,1,0:T(8,128)(2,1)S(1)} %collective-permute-done.24.refs_1_.refs_3_), custom_call_target="tpu_custom_call" | custom-call | flops 6442450944 | bytes 25165824 | tf_op jit(solution)/shard_map/product/pallas_call | solution.py:282
  151.2 6.7 %collective-permute-done.33.refs_1_ = bf16[4,64,2048]{2,1,0:T(8,128)(2,1)S(1)} collective-permute-done((bf16[4,64,2048]{2,1,0:T(8,128)(2,1)S(1)}, bf16[4,64,2048]{2,1,0:T(8,128)(2,1)S(1)}, u32[]{:S(2)}, u32[]{:S(2)}) %collective-permute-start.33) | collective-permute-done | bytes 1048608 | tf_op jit(solution)/shard_map/ppermute | solution.py:29
  157.9 3.3 %product.6.refs_4_ = bf16[512,4096]{1,0:T(8,128)(2,1)} custom-call(bf16[512,2048]{1,0:T(8,128)(2,1)S(1)} %get-tuple-element.27.refs_0_, bf16[4,64,2048]{2,1,0:T(8,128)(2,1)S(1)} %collective-permute-done.33.refs_1_, bf16[4,64,2048]{2,1,0:T(8,128)(2,1)S(1)} %collective-permute-done.34.refs_2_, f32[512,2048]{1,0:T(8,128)S(1)} %product.5.refs_3_), custom_call_target="tpu_custom_call" | custom-call | flops 2147483648 | bytes 16777216 | tf_op jit(solution)/shard_map/product/pallas_call | solution.py:282
  161.2 3.3 %product.7 = bf16[512,4096]{1,0:T(8,128)(2,1)} custom-call(bf16[512,2048]{1,0:T(8,128)(2,1)S(1)} %get-tuple-element.19.refs_0_, bf16[4,64,2048]{2,1,0:T(8,128)(2,1)S(1)} %collective-permute-done.25.refs_1_, bf16[4,64,2048]{2,1,0:T(8,128)(2,1)S(1)} %collective-permute-done.26.refs_2_, ...), custom_call_target="tpu_custom_call", output_to_operand_aliasing={{}: (4, {})} | custom-call | flops 2147483648 | bytes 16777216 | tf_op jit(solution)/shard_map/product/pallas_call | solution.py:282
  (82 shorter events, 22.2 us)
Async XLA Ops:
  0.0 26.3 %collective-permute-start.15 = (bf16[2,64,4096]{2,1,0:T(8,128)(2,1)}, bf16[2,64,4096]{2,1,0:T(8,128)(2,1)S(1)}, u32[]{:S(2)}, u32[]{:S(2)}) collective-permute-start(bf16[2,64,4096]{2,1,0:T(8,128)(2,1)} %refs_0_.3), channel_id=1, source_target_pairs={{0,96},{16,112},{32,0},{48,16},{64,32},{80,48},{96,64},{112,80},{1... | collective-permute-start | bytes 3145736 | tf_op jit(solution)/shard_map/ppermute | solution.py:17
  0.8 25.5 %collective-permute-start.14 = (bf16[2,64,4096]{2,1,0:T(8,128)(2,1)}, bf16[2,64,4096]{2,1,0:T(8,128)(2,1)S(1)}, u32[]{:S(2)}, u32[]{:S(2)}) collective-permute-start(bf16[2,64,4096]{2,1,0:T(8,128)(2,1)} %refs_0_.3), channel_id=1, source_target_pairs={{0,32},{16,48},{32,64},{48,80},{64,96},{80,112},{96,0},{112,16},{1... | collective-permute-start | bytes 3145736 | tf_op jit(solution)/shard_map/ppermute | solution.py:17
  4.0 6.0 %collective-permute-start.2 = (f32[2,128]{1,0:T(2,128)S(1)}, f32[2,128]{1,0:T(2,128)S(1)}, u32[]{:S(2)}, u32[]{:S(2)}) collective-permute-start(f32[2,128]{1,0:T(2,128)S(1)} %broadcast_in_dim.8), channel_id=1, source_target_pairs={{0,8},{1,9},{2,10},{3,11},{4,12},{5,13},{6,14},{7,15},{8,0},{9,1},... | collective-permute-start | bytes 3080 | tf_op jit(solution)/shard_map/ppermute | solution.py:25
  8.6 4.8 %collective-permute-start = (f32[2,128]{1,0:T(2,128)S(1)}, f32[2,128]{1,0:T(2,128)S(1)}, u32[]{:S(2)}, u32[]{:S(2)}) collective-permute-start(f32[2,128]{1,0:T(2,128)S(1)} %broadcast_in_dim.8), channel_id=1, source_target_pairs={{0,4},{1,5},{2,6},{3,7},{4,8},{5,9},{6,10},{7,11},{8,12},{9,13},{1... | collective-permute-start | bytes 3080 | tf_op jit(solution)/shard_map/ppermute | solution.py:25
  13.4 17.5 %collective-permute-start.5 = (f32[4,2,128]{2,1,0:T(2,128)S(1)}, f32[4,2,128]{2,1,0:T(2,128)S(1)}, u32[]{:S(2)}, u32[]{:S(2)}) collective-permute-start(f32[4,2,128]{2,1,0:T(2,128)S(1)} %pad_maximum_fusion.2.refs_2_), channel_id=1, source_target_pairs={{0,2},{1,3},{2,0},{3,1},{4,6},{5,7},{6,4},{7,5},{8,10},{9,11},{10,... | collective-permute-start | bytes 12296 | tf_op jit(solution)/shard_map/ppermute | solution.py:29
  16.7 14.3 %collective-permute-start.4 = (f32[4,2,128]{2,1,0:T(2,128)S(1)}, f32[4,2,128]{2,1,0:T(2,128)S(1)}, u32[]{:S(2)}, u32[]{:S(2)}) collective-permute-start(f32[4,2,128]{2,1,0:T(2,128)S(1)} %pad_maximum_fusion.2.refs_2_), channel_id=1, source_target_pairs={{0,3},{1,0},{2,1},{3,2},{4,7},{5,4},{6,5},{7,6},{8,11},{9,8},{10,9... | collective-permute-start | bytes 12296 | tf_op jit(solution)/shard_map/ppermute | solution.py:29
  17.7 13.2 %collective-permute-start.3 = (f32[4,2,128]{2,1,0:T(2,128)S(1)}, f32[4,2,128]{2,1,0:T(2,128)S(1)}, u32[]{:S(2)}, u32[]{:S(2)}) collective-permute-start(f32[4,2,128]{2,1,0:T(2,128)S(1)} %pad_maximum_fusion.2.refs_2_), channel_id=1, source_target_pairs={{0,1},{1,2},{2,3},{3,0},{4,5},{5,6},{6,7},{7,4},{8,9},{9,10},{10,1... | collective-permute-start | bytes 12296 | tf_op jit(solution)/shard_map/ppermute | solution.py:29
  28.0 17.4 %collective-permute-start.16 = (bf16[1,64,4096]{2,1,0:T(8,128)(2,1)}, bf16[1,64,4096]{2,1,0:T(8,128)(2,1)}, u32[]{:S(2)}, u32[]{:S(2)}) collective-permute-start(bf16[1,64,4096]{2,1,0:T(8,128)(2,1)} %get-tuple-element.20), channel_id=1, source_target_pairs={{0,32},{16,48},{32,64},{48,80},{64,96},{80,112},{96,0},{112,16},{1... | collective-permute-start | bytes 1572872 | tf_op jit(solution)/shard_map/ppermute | solution.py:17
  30.9 14.5 %collective-permute-start.17 = (bf16[1,64,4096]{2,1,0:T(8,128)(2,1)}, bf16[1,64,4096]{2,1,0:T(8,128)(2,1)}, u32[]{:S(2)}, u32[]{:S(2)}) collective-permute-start(bf16[1,64,4096]{2,1,0:T(8,128)(2,1)} %get-tuple-element.21), channel_id=1, source_target_pairs={{0,96},{16,112},{32,0},{48,16},{64,32},{80,48},{96,64},{112,80},{1... | collective-permute-start | bytes 1572872 | tf_op jit(solution)/shard_map/ppermute | solution.py:17
  31.0 12.7 %collective-permute-start.8 = (f32[16,2,128]{2,1,0:T(2,128)S(1)}, f32[16,2,128]{2,1,0:T(2,128)S(1)}, u32[]{:S(2)}, u32[]{:S(2)}) collective-permute-start(f32[16,2,128]{2,1,0:T(2,128)S(1)} %constant_dynamic-update-slice_fusion), channel_id=1, source_target_pairs={{0,64},{16,80},{32,96},{48,112},{64,0},{80,16},{96,32},{112,48},{1... | collective-permute-start | bytes 49160 | tf_op jit(solution)/shard_map/ppermute | solution.py:17
  32.5 12.7 %collective-permute-start.7 = (f32[16,2,128]{2,1,0:T(2,128)S(1)}, f32[16,2,128]{2,1,0:T(2,128)S(1)}, u32[]{:S(2)}, u32[]{:S(2)}) collective-permute-start(f32[16,2,128]{2,1,0:T(2,128)S(1)} %constant_dynamic-update-slice_fusion), channel_id=1, source_target_pairs={{0,96},{16,112},{32,0},{48,16},{64,32},{80,48},{96,64},{112,80},{1... | collective-permute-start | bytes 49160 | tf_op jit(solution)/shard_map/ppermute | solution.py:17
  35.1 10.1 %collective-permute-start.6 = (f32[16,2,128]{2,1,0:T(2,128)S(1)}, f32[16,2,128]{2,1,0:T(2,128)S(1)}, u32[]{:S(2)}, u32[]{:S(2)}) collective-permute-start(f32[16,2,128]{2,1,0:T(2,128)S(1)} %constant_dynamic-update-slice_fusion), channel_id=1, source_target_pairs={{0,32},{16,48},{32,64},{48,80},{64,96},{80,112},{96,0},{112,16},{1... | collective-permute-start | bytes 49160 | tf_op jit(solution)/shard_map/ppermute | solution.py:17
  48.9 8.0 %collective-permute-start.9 = (f32[16,8,128]{2,1,0:T(8,128)S(1)}, f32[16,8,128]{2,1,0:T(8,128)S(1)}, u32[]{:S(2)}, u32[]{:S(2)}) collective-permute-start(f32[16,8,128]{2,1,0:T(8,128)S(1)} %pad_maximum_fusion.1.own_ref), channel_id=1, source_target_pairs={{0,16},{16,0},{32,48},{48,32},{64,80},{80,64},{96,112},{112,96},{1... | collective-permute-start | bytes 196616 | tf_op jit(solution)/shard_map/ppermute | solution.py:21
  52.8 15.5 %collective-permute-start.28 = (bf16[2,64,2048]{2,1,0:T(8,128)(2,1)S(1)}, bf16[2,64,2048]{2,1,0:T(8,128)(2,1)S(1)}, u32[]{:S(2)}, u32[]{:S(2)}) collective-permute-start(bf16[2,64,2048]{2,1,0:T(8,128)(2,1)S(1)} %get-tuple-element.28.refs_0_), channel_id=1, source_target_pairs={{0,12},{1,13},{2,14},{3,15},{4,0},{5,1},{6,2},{7,3},{8,4},{9,5},{1... | collective-permute-start | bytes 1572872 | tf_op jit(solution)/shard_map/ppermute | solution.py:25
  56.8 14.9 %collective-permute-start.27 = (bf16[2,64,2048]{2,1,0:T(8,128)(2,1)S(1)}, bf16[2,64,2048]{2,1,0:T(8,128)(2,1)S(1)}, u32[]{:S(2)}, u32[]{:S(2)}) collective-permute-start(bf16[2,64,2048]{2,1,0:T(8,128)(2,1)S(1)} %get-tuple-element.28.refs_0_), channel_id=1, source_target_pairs={{0,4},{1,5},{2,6},{3,7},{4,8},{5,9},{6,10},{7,11},{8,12},{9,13},{1... | collective-permute-start | bytes 1572872 | tf_op jit(solution)/shard_map/ppermute | solution.py:25
  61.7 14.4 %collective-permute-start.20 = (bf16[2,64,2048]{2,1,0:T(8,128)(2,1)S(1)}, bf16[2,64,2048]{2,1,0:T(8,128)(2,1)S(1)}, u32[]{:S(2)}, u32[]{:S(2)}) collective-permute-start(bf16[2,64,2048]{2,1,0:T(8,128)(2,1)S(1)} %get-tuple-element.22.refs_0_), channel_id=1, source_target_pairs={{0,3},{1,0},{2,1},{3,2},{4,7},{5,4},{6,5},{7,6},{8,11},{9,8},{10,9... | collective-permute-start | bytes 1572872 | tf_op jit(solution)/shard_map/ppermute | solution.py:29
  64.9 14.6 %collective-permute-start.19 = (bf16[2,64,2048]{2,1,0:T(8,128)(2,1)S(1)}, bf16[2,64,2048]{2,1,0:T(8,128)(2,1)S(1)}, u32[]{:S(2)}, u32[]{:S(2)}) collective-permute-start(bf16[2,64,2048]{2,1,0:T(8,128)(2,1)S(1)} %get-tuple-element.22.refs_0_), channel_id=1, source_target_pairs={{0,1},{1,2},{2,3},{3,0},{4,5},{5,6},{6,7},{7,4},{8,9},{9,10},{10,1... | collective-permute-start | bytes 1572872 | tf_op jit(solution)/shard_map/ppermute | solution.py:29
  65.0 28.3 %collective-permute-start.12 = (bf16[2,512,256]{2,1,0:T(8,128)(2,1)S(1)}, bf16[2,512,256]{2,1,0:T(8,128)(2,1)S(1)}, u32[]{:S(2)}, u32[]{:S(2)}) collective-permute-start(bf16[2,512,256]{2,1,0:T(8,128)(2,1)S(1)} %get-tuple-element.33), channel_id=1, source_target_pairs={{0,96},{16,112},{32,0},{48,16},{64,32},{80,48},{96,64},{112,80},{1... | collective-permute-start | bytes 1572872 | tf_op jit(solution)/shard_map/ppermute | solution.py:17
  71.9 11.0 %collective-permute-start.29 = (bf16[1,64,2048]{2,1,0:T(8,128)(2,1)S(1)}, bf16[1,64,2048]{2,1,0:T(8,128)(2,1)S(1)}, u32[]{:S(2)}, u32[]{:S(2)}) collective-permute-start(bf16[1,64,2048]{2,1,0:T(8,128)(2,1)S(1)} %get-tuple-element.29), channel_id=1, source_target_pairs={{0,4},{1,5},{2,6},{3,7},{4,8},{5,9},{6,10},{7,11},{8,12},{9,13},{1... | collective-permute-start | bytes 786440 | tf_op jit(solution)/shard_map/ppermute | solution.py:25
  72.0 11.3 %collective-permute-start.30 = (bf16[1,64,2048]{2,1,0:T(8,128)(2,1)S(1)}, bf16[1,64,2048]{2,1,0:T(8,128)(2,1)S(1)}, u32[]{:S(2)}, u32[]{:S(2)}) collective-permute-start(bf16[1,64,2048]{2,1,0:T(8,128)(2,1)S(1)} %get-tuple-element.30), channel_id=1, source_target_pairs={{0,12},{1,13},{2,14},{3,15},{4,0},{5,1},{6,2},{7,3},{8,4},{9,5},{1... | collective-permute-start | bytes 786440 | tf_op jit(solution)/shard_map/ppermute | solution.py:25
  79.7 8.1 %collective-permute-start.21 = (bf16[1,64,2048]{2,1,0:T(8,128)(2,1)S(1)}, bf16[1,64,2048]{2,1,0:T(8,128)(2,1)S(1)}, u32[]{:S(2)}, u32[]{:S(2)}) collective-permute-start(bf16[1,64,2048]{2,1,0:T(8,128)(2,1)S(1)} %get-tuple-element.23), channel_id=1, source_target_pairs={{0,1},{1,2},{2,3},{3,0},{4,5},{5,6},{6,7},{7,4},{8,9},{9,10},{10,1... | collective-permute-start | bytes 786440 | tf_op jit(solution)/shard_map/ppermute | solution.py:29
  79.7 10.0 %collective-permute-start.22 = (bf16[1,64,2048]{2,1,0:T(8,128)(2,1)S(1)}, bf16[1,64,2048]{2,1,0:T(8,128)(2,1)S(1)}, u32[]{:S(2)}, u32[]{:S(2)}) collective-permute-start(bf16[1,64,2048]{2,1,0:T(8,128)(2,1)S(1)} %get-tuple-element.24), channel_id=1, source_target_pairs={{0,3},{1,0},{2,1},{3,2},{4,7},{5,4},{6,5},{7,6},{8,11},{9,8},{10,9... | collective-permute-start | bytes 786440 | tf_op jit(solution)/shard_map/ppermute | solution.py:29
  83.0 13.4 %collective-permute-start.11 = (bf16[2,512,256]{2,1,0:T(8,128)(2,1)S(1)}, bf16[2,512,256]{2,1,0:T(8,128)(2,1)S(1)}, u32[]{:S(2)}, u32[]{:S(2)}) collective-permute-start(bf16[2,512,256]{2,1,0:T(8,128)(2,1)S(1)} %get-tuple-element.34), channel_id=1, source_target_pairs={{0,64},{16,80},{32,96},{48,112},{64,0},{80,16},{96,32},{112,48},{1... | collective-permute-start | bytes 1572872 | tf_op jit(solution)/shard_map/ppermute | solution.py:17
  83.9 48.1 %collective-permute-start.32 = (bf16[8,64,2048]{2,1,0:T(8,128)(2,1)S(1)}, bf16[8,64,2048]{2,1,0:T(8,128)(2,1)S(1)}, u32[]{:S(2)}, u32[]{:S(2)}) collective-permute-start(bf16[8,64,2048]{2,1,0:T(8,128)(2,1)S(1)} %join.3.refs_1_), channel_id=1, source_target_pairs={{0,3},{1,0},{2,1},{3,2},{4,7},{5,4},{6,5},{7,6},{8,11},{9,8},{10,9... | collective-permute-start | bytes 6291464 | tf_op jit(solution)/shard_map/ppermute | solution.py:29
  87.8 46.5 %collective-permute-start.31 = (bf16[8,64,2048]{2,1,0:T(8,128)(2,1)S(1)}, bf16[8,64,2048]{2,1,0:T(8,128)(2,1)S(1)}, u32[]{:S(2)}, u32[]{:S(2)}) collective-permute-start(bf16[8,64,2048]{2,1,0:T(8,128)(2,1)S(1)} %join.3.refs_1_), channel_id=1, source_target_pairs={{0,1},{1,2},{2,3},{3,0},{4,5},{5,6},{6,7},{7,4},{8,9},{9,10},{10,1... | collective-permute-start | bytes 6291464 | tf_op jit(solution)/shard_map/ppermute | solution.py:29
  90.3 47.8 %collective-permute-start.24 = (bf16[8,64,2048]{2,1,0:T(8,128)(2,1)S(1)}, bf16[8,64,2048]{2,1,0:T(8,128)(2,1)S(1)}, u32[]{:S(2)}, u32[]{:S(2)}) collective-permute-start(bf16[8,64,2048]{2,1,0:T(8,128)(2,1)S(1)} %join.2.refs_1_), channel_id=1, source_target_pairs={{0,12},{1,13},{2,14},{3,15},{4,0},{5,1},{6,2},{7,3},{8,4},{9,5},{1... | collective-permute-start | bytes 6291464 | tf_op jit(solution)/shard_map/ppermute | solution.py:25
  93.3 44.8 %collective-permute-start.23 = (bf16[8,64,2048]{2,1,0:T(8,128)(2,1)S(1)}, bf16[8,64,2048]{2,1,0:T(8,128)(2,1)S(1)}, u32[]{:S(2)}, u32[]{:S(2)}) collective-permute-start(bf16[8,64,2048]{2,1,0:T(8,128)(2,1)S(1)} %join.2.refs_1_), channel_id=1, source_target_pairs={{0,4},{1,5},{2,6},{3,7},{4,8},{5,9},{6,10},{7,11},{8,12},{9,13},{1... | collective-permute-start | bytes 6291464 | tf_op jit(solution)/shard_map/ppermute | solution.py:25
  96.4 11.0 %collective-permute-start.10 = (bf16[2,512,256]{2,1,0:T(8,128)(2,1)S(1)}, bf16[2,512,256]{2,1,0:T(8,128)(2,1)S(1)}, u32[]{:S(2)}, u32[]{:S(2)}) collective-permute-start(bf16[2,512,256]{2,1,0:T(8,128)(2,1)S(1)} %get-tuple-element.35), channel_id=1, source_target_pairs={{0,32},{16,48},{32,64},{48,80},{64,96},{80,112},{96,0},{112,16},{1... | collective-permute-start | bytes 1572872 | tf_op jit(solution)/shard_map/ppermute | solution.py:17
  134.7 23.2 %collective-permute-start.33 = (bf16[4,64,2048]{2,1,0:T(8,128)(2,1)S(1)}, bf16[4,64,2048]{2,1,0:T(8,128)(2,1)S(1)}, u32[]{:S(2)}, u32[]{:S(2)}) collective-permute-start(bf16[4,64,2048]{2,1,0:T(8,128)(2,1)S(1)} %get-tuple-element.31), channel_id=1, source_target_pairs={{0,1},{1,2},{2,3},{3,0},{4,5},{5,6},{6,7},{7,4},{8,9},{9,10},{10,1... | collective-permute-start | bytes 3145736 | tf_op jit(solution)/shard_map/ppermute | solution.py:29
  134.8 23.1 %collective-permute-start.34 = (bf16[4,64,2048]{2,1,0:T(8,128)(2,1)S(1)}, bf16[4,64,2048]{2,1,0:T(8,128)(2,1)S(1)}, u32[]{:S(2)}, u32[]{:S(2)}) collective-permute-start(bf16[4,64,2048]{2,1,0:T(8,128)(2,1)S(1)} %get-tuple-element.32), channel_id=1, source_target_pairs={{0,3},{1,0},{2,1},{3,2},{4,7},{5,4},{6,5},{7,6},{8,11},{9,8},{10,9... | collective-permute-start | bytes 3145736 | tf_op jit(solution)/shard_map/ppermute | solution.py:29
  138.5 22.6 %collective-permute-start.25 = (bf16[4,64,2048]{2,1,0:T(8,128)(2,1)S(1)}, bf16[4,64,2048]{2,1,0:T(8,128)(2,1)S(1)}, u32[]{:S(2)}, u32[]{:S(2)}) collective-permute-start(bf16[4,64,2048]{2,1,0:T(8,128)(2,1)S(1)} %get-tuple-element.25), channel_id=1, source_target_pairs={{0,4},{1,5},{2,6},{3,7},{4,8},{5,9},{6,10},{7,11},{8,12},{9,13},{1... | collective-permute-start | bytes 3145736 | tf_op jit(solution)/shard_map/ppermute | solution.py:25
  138.6 22.5 %collective-permute-start.26 = (bf16[4,64,2048]{2,1,0:T(8,128)(2,1)S(1)}, bf16[4,64,2048]{2,1,0:T(8,128)(2,1)S(1)}, u32[]{:S(2)}, u32[]{:S(2)}) collective-permute-start(bf16[4,64,2048]{2,1,0:T(8,128)(2,1)S(1)} %get-tuple-element.26), channel_id=1, source_target_pairs={{0,12},{1,13},{2,14},{3,15},{4,0},{5,1},{6,2},{7,3},{8,4},{9,5},{1... | collective-permute-start | bytes 3145736 | tf_op jit(solution)/shard_map/ppermute | solution.py:25
  (7 other events, 68.2 us)

commit v3 on v2

--- a/solution.py
+++ b/solution.py
@@ -192,10 +192,9 @@
 
 def pick_tiles(at, names, pieces, which):
     _, b, n = pieces[0].shape
-    step = 1024
 
     def kernel(at_ref, name_ref, *refs):
-        pieces, out = refs[:5], refs[5]
+        pieces, (out, zeros, sems) = refs[:5], refs[5:]
         spots = [2 * lax.rem(at_ref[X] + (d + 4), 4) + s for d in ORDER for s in range(2)]
         match = [(name_ref[j] // 8 == at_ref[which]).astype(jnp.int32) for j in range(8)]
         slots = []
@@ -207,25 +206,31 @@
 
             @pl.when(sum(there) == 0)
             def _():
-                out[s] = jnp.zeros(out.shape[1:], out.dtype)
+                zeros[...] = jnp.zeros_like(zeros)
+                pltpu.make_async_copy(zeros, out.at[s], sems.at[s]).start()
 
             for j in range(8):
 
                 @pl.when(there[j] == 1)
                 def _():
-                    out[s] = pieces[j // 2][j % 2] if j < 6 else pieces[j - 3][0]
+                    source = pieces[j // 2].at[j % 2] if j < 6 else pieces[j - 3].at[0]
+                    pltpu.make_async_copy(source, out.at[s], sems.at[s]).start()
+
+        for s in range(2):
+            pltpu.make_async_copy(zeros, out.at[s], sems.at[s]).wait()
 
     return pl.pallas_call(
         kernel,
         grid_spec=pltpu.PrefetchScalarGridSpec(
             num_scalar_prefetch=2,
-            grid=(n // step,),
-            in_specs=[pl.BlockSpec((v.shape[0], b, step), lambda i, p, q: (0, 0, i)) for v in pieces],
-            out_specs=pl.BlockSpec((2, b, step), lambda i, p, q: (0, 0, i)),
+            grid=(1,),
+            in_specs=[ANY] * 5,
+            out_specs=ANY,
+            scratch_shapes=[pltpu.VMEM((b, n), jnp.bfloat16), pltpu.SemaphoreType.DMA((2,))],
         ),
         out_shape=jax.ShapeDtypeStruct((2, b, n), jnp.bfloat16),
         compiler_params=PARAMS,
-        cost_estimate=pl.CostEstimate(flops=0, bytes_accessed=24 * b * n, transcendentals=0),
+        cost_estimate=pl.CostEstimate(flops=0, bytes_accessed=8 * b * n, transcendentals=0),
         name="pick_tiles",
     )(at, names, *pieces)
 

time: 165 us -> 161 us (0.976)
  Pallas kernels: 33 us -> 28.2 us
    pallas_call x2, Pallas kernels: 6.65 us -> 1.89 us  [pick_tiles(): pl.pallas_call(kernel, grid_spec=pltpu.PrefetchScalarGridSpec(num_scalar_...]
  transfers between devices with their start and end apart: 35 -> 35, of which waited for: 17 -> 18; matrix products, arithmetic and copies ran while one was open for 1% -> 1% of each run, Pallas kernels for 16% -> 15%
where the time goes in v3:
time: 161 us
  waiting for transfers between devices  83.4 us (52%)
  starting transfers between devices  47.5 us (30%)
  Pallas kernels  28.2 us (18%)
    ppermute x11, waiting for transfers between devices, shift_y(): lax.ppermute(v, 'col', [(4 * z + y, 4 * z + (y + d) % 4) for z in range(4...  38.7 us
    ppermute x10, waiting for transfers between devices, shift_row_x(): lax.ppermute(v, 'row', [(2 * x + k, 2 * ((x + d) % 4) + k) for x in range...  30.8 us
    ppermute x11, starting transfers between devices, shift_z(): lax.ppermute(v, 'col', [(4 * z + y, 4 * ((z + d) % 4) + y) for z in range...  19.6 us
    pallas_call x4, Pallas kernels, product(): pl.pallas_call(kernel, grid=(n // step,), in_specs=specs, out_specs=pl.Bl...  15.9 us
    ppermute x11, starting transfers between devices, shift_y(): lax.ppermute(v, 'col', [(4 * z + y, 4 * z + (y + d) % 4) for z in range(4...  15.6 us
    ppermute x10, starting transfers between devices, shift_row_x(): lax.ppermute(v, 'row', [(2 * x + k, 2 * ((x + d) % 4) + k) for x in range...  11.6 us
    ppermute x11, waiting for transfers between devices, shift_z(): lax.ppermute(v, 'col', [(4 * z + y, 4 * ((z + d) % 4) + y) for z in range...  10 us
    pallas_call x1, Pallas kernels, choose_columns(): pl.pallas_call(choose_kernel, grid_spec=pltpu.PrefetchScalarGridSpec(num_...  4.84 us
  transfers between devices with their start and end apart: 35, of which 18 were waited for; matrix products, arithmetic and copies ran while one was open for 1% of the time, Pallas kernels for 15%

profile of v3, /device:TPU:6, one launch (start us, length us, event | category | flops | bytes accessed | tf_op | source)
XLA Modules:
  0.0 160.9 jit_solution(780211234962220361)
XLA Ops:
  0.8 2.4 %collective-permute-start.14 = (bf16[2,64,4096]{2,1,0:T(8,128)(2,1)}, bf16[2,64,4096]{2,1,0:T(8,128)(2,1)S(1)}, u32[]{:S(2)}, u32[]{:S(2)}) collective-permute-start(bf16[2,64,4096]{2,1,0:T(8,128)(2,1)} %refs_0_.3), channel_id=1, source_target_pairs={{0,32},{16,48},{32,64},{48,80},{64,96},{80,112},{96,0},{112,16},{1... | collective-permute-start | bytes 3145736 | tf_op jit(solution)/shard_map/ppermute | solution.py:17
  4.0 3.9 %collective-permute-start.2 = (f32[2,128]{1,0:T(2,128)S(1)}, f32[2,128]{1,0:T(2,128)S(1)}, u32[]{:S(2)}, u32[]{:S(2)}) collective-permute-start(f32[2,128]{1,0:T(2,128)S(1)} %broadcast_in_dim.8), channel_id=1, source_target_pairs={{0,8},{1,9},{2,10},{3,11},{4,12},{5,13},{6,14},{7,15},{8,0},{9,1},... | collective-permute-start | bytes 3080 | tf_op jit(solution)/shard_map/ppermute | solution.py:25
  11.4 1.9 %collective-permute-done = f32[2,128]{1,0:T(2,128)S(1)} collective-permute-done((f32[2,128]{1,0:T(2,128)S(1)}, f32[2,128]{1,0:T(2,128)S(1)}, u32[]{:S(2)}, u32[]{:S(2)}) %collective-permute-start) | collective-permute-done | bytes 1056 | tf_op jit(solution)/shard_map/ppermute | solution.py:25
  13.4 3.2 %collective-permute-start.5 = (f32[4,2,128]{2,1,0:T(2,128)S(1)}, f32[4,2,128]{2,1,0:T(2,128)S(1)}, u32[]{:S(2)}, u32[]{:S(2)}) collective-permute-start(f32[4,2,128]{2,1,0:T(2,128)S(1)} %pad_maximum_fusion.2.refs_2_), channel_id=1, source_target_pairs={{0,2},{1,3},{2,0},{3,1},{4,6},{5,7},{6,4},{7,5},{8,10},{9,11},{10,... | collective-permute-start | bytes 12296 | tf_op jit(solution)/shard_map/ppermute | solution.py:29
  18.7 7.6 %collective-permute-done.15.refs_1_.refs_2_ = bf16[2,64,4096]{2,1,0:T(8,128)(2,1)S(1)} collective-permute-done((bf16[2,64,4096]{2,1,0:T(8,128)(2,1)}, bf16[2,64,4096]{2,1,0:T(8,128)(2,1)S(1)}, u32[]{:S(2)}, u32[]{:S(2)}) %collective-permute-start.15) | collective-permute-done | bytes 1048608 | tf_op jit(solution)/shard_map/ppermute | solution.py:17
  26.3 1.6 %halves.5 = (bf16[1,64,4096]{2,1,0:T(8,128)(2,1)}, bf16[1,64,4096]{2,1,0:T(8,128)(2,1)}) custom-call(bf16[2,64,4096]{2,1,0:T(8,128)(2,1)S(1)} %collective-permute-done.14.refs_0_.refs_1_, bf16[2,64,4096]{2,1,0:T(8,128)(2,1)S(1)} %collective-permute-done.15.refs_1_.refs_2_, f32[4,2,128]{2,1,0:T(2,128)S(1)} %pad_maximum_fusion.2.refs_2_), custom_call_target="tpu_custom_call" | custom-call | bytes 2097152 | tf_op jit(solution)/shard_map/halves/pallas_call | solution.py:41
  28.0 3.0 %collective-permute-start.16 = (bf16[1,64,4096]{2,1,0:T(8,128)(2,1)}, bf16[1,64,4096]{2,1,0:T(8,128)(2,1)}, u32[]{:S(2)}, u32[]{:S(2)}) collective-permute-start(bf16[1,64,4096]{2,1,0:T(8,128)(2,1)} %get-tuple-element.20), channel_id=1, source_target_pairs={{0,32},{16,48},{32,64},{48,80},{64,96},{80,112},{96,0},{112,16},{1... | collective-permute-start | bytes 1572872 | tf_op jit(solution)/shard_map/ppermute | solution.py:17
  32.5 2.6 %collective-permute-start.7 = (f32[16,2,128]{2,1,0:T(2,128)S(1)}, f32[16,2,128]{2,1,0:T(2,128)S(1)}, u32[]{:S(2)}, u32[]{:S(2)}) collective-permute-start(f32[16,2,128]{2,1,0:T(2,128)S(1)} %constant_dynamic-update-slice_fusion), channel_id=1, source_target_pairs={{0,96},{16,112},{32,0},{48,16},{64,32},{80,48},{96,64},{112,80},{1... | collective-permute-start | bytes 49160 | tf_op jit(solution)/shard_map/ppermute | solution.py:17
  35.8 7.8 %collective-permute-done.8 = f32[16,2,128]{2,1,0:T(2,128)S(1)} collective-permute-done((f32[16,2,128]{2,1,0:T(2,128)S(1)}, f32[16,2,128]{2,1,0:T(2,128)S(1)}, u32[]{:S(2)}, u32[]{:S(2)}) %collective-permute-start.8) | collective-permute-done | bytes 16416 | tf_op jit(solution)/shard_map/ppermute | solution.py:17
  49.2 4.1 %collective-permute-start.28 = (bf16[2,64,2048]{2,1,0:T(8,128)(2,1)S(1)}, bf16[2,64,2048]{2,1,0:T(8,128)(2,1)S(1)}, u32[]{:S(2)}, u32[]{:S(2)}) collective-permute-start(bf16[2,64,2048]{2,1,0:T(8,128)(2,1)S(1)} %get-tuple-element.28.refs_0_), channel_id=1, source_target_pairs={{0,12},{1,13},{2,14},{3,15},{4,0},{5,1},{6,2},{7,3},{8,4},{9,5},{1... | collective-permute-start | bytes 1572872 | tf_op jit(solution)/shard_map/ppermute | solution.py:25
  53.3 4.8 %choose_columns.1 = bf16[8,512,256]{2,1,0:T(8,128)(2,1)S(1)} custom-call(s32[7]{0:T(128)S(1)} %stack.46.at_ref, s32[128]{0:T(128)S(1)} %copy-done.3, bf16[512,1024]{1,0:T(8,128)(2,1)S(1)} %copy-done.1, f32[16,8,128]{2,1,0:T(8,128)S(1)} %pad_maximum_fusion.1.own_ref, f32[16,8,128]{2,1,0:T(8,128)S(1)} %collective-permute-done.9.other_ref, s32[8,16]{1,0:T(8,128)S(1)} %copy-done.2), custom_call_target="tpu_custom_call" | custom-call | flops 2147483648 | bytes 3145728 | tf_op jit(solution)/shard_map/choose_columns/pallas_call | solution.py:137
  58.1 3.2 %collective-permute-start.20 = (bf16[2,64,2048]{2,1,0:T(8,128)(2,1)S(1)}, bf16[2,64,2048]{2,1,0:T(8,128)(2,1)S(1)}, u32[]{:S(2)}, u32[]{:S(2)}) collective-permute-start(bf16[2,64,2048]{2,1,0:T(8,128)(2,1)S(1)} %get-tuple-element.22.refs_0_), channel_id=1, source_target_pairs={{0,3},{1,0},{2,1},{3,2},{4,7},{5,4},{6,5},{7,6},{8,11},{9,8},{10,9... | collective-permute-start | bytes 1572872 | tf_op jit(solution)/shard_map/ppermute | solution.py:29
  61.5 3.2 %collective-permute-done.28.refs_1_.refs_2_ = bf16[2,64,2048]{2,1,0:T(8,128)(2,1)S(1)} collective-permute-done((bf16[2,64,2048]{2,1,0:T(8,128)(2,1)S(1)}, bf16[2,64,2048]{2,1,0:T(8,128)(2,1)S(1)}, u32[]{:S(2)}, u32[]{:S(2)}) %collective-permute-start.28) | collective-permute-done | bytes 524320 | tf_op jit(solution)/shard_map/ppermute | solution.py:25
  64.7 3.4 %collective-permute-done.27.refs_0_.refs_1_ = bf16[2,64,2048]{2,1,0:T(8,128)(2,1)S(1)} collective-permute-done((bf16[2,64,2048]{2,1,0:T(8,128)(2,1)S(1)}, bf16[2,64,2048]{2,1,0:T(8,128)(2,1)S(1)}, u32[]{:S(2)}, u32[]{:S(2)}) %collective-permute-start.27) | collective-permute-done | bytes 524320 | tf_op jit(solution)/shard_map/ppermute | solution.py:25
  68.4 3.2 %collective-permute-start.30 = (bf16[1,64,2048]{2,1,0:T(8,128)(2,1)S(1)}, bf16[1,64,2048]{2,1,0:T(8,128)(2,1)S(1)}, u32[]{:S(2)}, u32[]{:S(2)}) collective-permute-start(bf16[1,64,2048]{2,1,0:T(8,128)(2,1)S(1)} %get-tuple-element.30), channel_id=1, source_target_pairs={{0,12},{1,13},{2,14},{3,15},{4,0},{5,1},{6,2},{7,3},{8,4},{9,5},{1... | collective-permute-start | bytes 786440 | tf_op jit(solution)/shard_map/ppermute | solution.py:25
  72.6 3.3 %collective-permute-done.19.refs_0_.refs_1_ = bf16[2,64,2048]{2,1,0:T(8,128)(2,1)S(1)} collective-permute-done((bf16[2,64,2048]{2,1,0:T(8,128)(2,1)S(1)}, bf16[2,64,2048]{2,1,0:T(8,128)(2,1)S(1)}, u32[]{:S(2)}, u32[]{:S(2)}) %collective-permute-start.19) | collective-permute-done | bytes 524320 | tf_op jit(solution)/shard_map/ppermute | solution.py:29
  76.2 3.2 %collective-permute-start.22 = (bf16[1,64,2048]{2,1,0:T(8,128)(2,1)S(1)}, bf16[1,64,2048]{2,1,0:T(8,128)(2,1)S(1)}, u32[]{:S(2)}, u32[]{:S(2)}) collective-permute-start(bf16[1,64,2048]{2,1,0:T(8,128)(2,1)S(1)} %get-tuple-element.24), channel_id=1, source_target_pairs={{0,3},{1,0},{2,1},{3,2},{4,7},{5,4},{6,5},{7,6},{8,11},{9,8},{10,9... | collective-permute-start | bytes 786440 | tf_op jit(solution)/shard_map/ppermute | solution.py:29
  80.9 3.4 %collective-permute-done.21.refs_3_ = bf16[1,64,2048]{2,1,0:T(8,128)(2,1)S(1)} collective-permute-done((bf16[1,64,2048]{2,1,0:T(8,128)(2,1)S(1)}, bf16[1,64,2048]{2,1,0:T(8,128)(2,1)S(1)}, u32[]{:S(2)}, u32[]{:S(2)}) %collective-permute-start.21) | collective-permute-done | bytes 262176 | tf_op jit(solution)/shard_map/ppermute | solution.py:29
  84.2 1.9 %collective-permute-done.22.refs_4_ = bf16[1,64,2048]{2,1,0:T(8,128)(2,1)S(1)} collective-permute-done((bf16[1,64,2048]{2,1,0:T(8,128)(2,1)S(1)}, bf16[1,64,2048]{2,1,0:T(8,128)(2,1)S(1)}, u32[]{:S(2)}, u32[]{:S(2)}) %collective-permute-start.22) | collective-permute-done | bytes 262176 | tf_op jit(solution)/shard_map/ppermute | solution.py:29
  86.7 3.0 %collective-permute-start.24 = (bf16[8,64,2048]{2,1,0:T(8,128)(2,1)S(1)}, bf16[8,64,2048]{2,1,0:T(8,128)(2,1)S(1)}, u32[]{:S(2)}, u32[]{:S(2)}) collective-permute-start(bf16[8,64,2048]{2,1,0:T(8,128)(2,1)S(1)} %join.2.refs_1_), channel_id=1, source_target_pairs={{0,12},{1,13},{2,14},{3,15},{4,0},{5,1},{6,2},{7,3},{8,4},{9,5},{1... | collective-permute-start | bytes 6291464 | tf_op jit(solution)/shard_map/ppermute | solution.py:25
  89.7 3.1 %collective-permute-done.11.refs_2_ = bf16[2,512,256]{2,1,0:T(8,128)(2,1)S(1)} collective-permute-done((bf16[2,512,256]{2,1,0:T(8,128)(2,1)S(1)}, bf16[2,512,256]{2,1,0:T(8,128)(2,1)S(1)}, u32[]{:S(2)}, u32[]{:S(2)}) %collective-permute-start.11) | collective-permute-done | bytes 524320 | tf_op jit(solution)/shard_map/ppermute | solution.py:17
  93.2 10.7 %collective-permute-done.10.refs_1_ = bf16[2,512,256]{2,1,0:T(8,128)(2,1)S(1)} collective-permute-done((bf16[2,512,256]{2,1,0:T(8,128)(2,1)S(1)}, bf16[2,512,256]{2,1,0:T(8,128)(2,1)S(1)}, u32[]{:S(2)}, u32[]{:S(2)}) %collective-permute-start.10) | collective-permute-done | bytes 524320 | tf_op jit(solution)/shard_map/ppermute | solution.py:17
  104.1 2.6 %collective-permute-done.13.refs_4_ = bf16[4,512,256]{2,1,0:T(8,128)(2,1)S(1)} collective-permute-done((bf16[4,512,256]{2,1,0:T(8,128)(2,1)S(1)}, bf16[4,512,256]{2,1,0:T(8,128)(2,1)S(1)}, u32[]{:S(2)}, u32[]{:S(2)}) %collective-permute-start.13) | collective-permute-done | bytes 1048608 | tf_op jit(solution)/shard_map/ppermute | solution.py:21
  108.3 20.1 %collective-permute-done.32.refs_1_.refs_3_ = bf16[8,64,2048]{2,1,0:T(8,128)(2,1)S(1)} collective-permute-done((bf16[8,64,2048]{2,1,0:T(8,128)(2,1)S(1)}, bf16[8,64,2048]{2,1,0:T(8,128)(2,1)S(1)}, u32[]{:S(2)}, u32[]{:S(2)}) %collective-permute-start.32) | collective-permute-done | bytes 2097184 | tf_op jit(solution)/shard_map/ppermute | solution.py:29
  128.4 2.3 %collective-permute-done.31.refs_0_.refs_2_ = bf16[8,64,2048]{2,1,0:T(8,128)(2,1)S(1)} collective-permute-done((bf16[8,64,2048]{2,1,0:T(8,128)(2,1)S(1)}, bf16[8,64,2048]{2,1,0:T(8,128)(2,1)S(1)}, u32[]{:S(2)}, u32[]{:S(2)}) %collective-permute-start.31) | collective-permute-done | bytes 2097184 | tf_op jit(solution)/shard_map/ppermute | solution.py:29
  131.3 3.2 %collective-permute-start.34 = (bf16[4,64,2048]{2,1,0:T(8,128)(2,1)S(1)}, bf16[4,64,2048]{2,1,0:T(8,128)(2,1)S(1)}, u32[]{:S(2)}, u32[]{:S(2)}) collective-permute-start(bf16[4,64,2048]{2,1,0:T(8,128)(2,1)S(1)} %get-tuple-element.32), channel_id=1, source_target_pairs={{0,3},{1,0},{2,1},{3,2},{4,7},{5,4},{6,5},{7,6},{8,11},{9,8},{10,9... | collective-permute-start | bytes 3145736 | tf_op jit(solution)/shard_map/ppermute | solution.py:29
  135.1 3.2 %collective-permute-start.26 = (bf16[4,64,2048]{2,1,0:T(8,128)(2,1)S(1)}, bf16[4,64,2048]{2,1,0:T(8,128)(2,1)S(1)}, u32[]{:S(2)}, u32[]{:S(2)}) collective-permute-start(bf16[4,64,2048]{2,1,0:T(8,128)(2,1)S(1)} %get-tuple-element.26), channel_id=1, source_target_pairs={{0,12},{1,13},{2,14},{3,15},{4,0},{5,1},{6,2},{7,3},{8,4},{9,5},{1... | collective-permute-start | bytes 3145736 | tf_op jit(solution)/shard_map/ppermute | solution.py:25
  138.3 4.7 %product.5.refs_3_ = f32[512,2048]{1,0:T(8,128)S(1)} custom-call(bf16[512,2048]{1,0:T(8,128)(2,1)S(1)} %get-tuple-element.27.refs_0_, bf16[8,64,2048]{2,1,0:T(8,128)(2,1)S(1)} %join.3.refs_1_, bf16[8,64,2048]{2,1,0:T(8,128)(2,1)S(1)} %collective-permute-done.31.refs_0_.refs_2_, bf16[8,64,2048]{2,1,0:T(8,128)(2,1)S(1)} %collective-permute-done.32.refs_1_.refs_3_), custom_call_target="tpu_custom_call" | custom-call | flops 6442450944 | bytes 25165824 | tf_op jit(solution)/shard_map/product/pallas_call | solution.py:287
  143.0 4.7 %product.4.refs_3_ = f32[512,2048]{1,0:T(8,128)S(1)} custom-call(bf16[512,2048]{1,0:T(8,128)(2,1)S(1)} %get-tuple-element.19.refs_0_, bf16[8,64,2048]{2,1,0:T(8,128)(2,1)S(1)} %join.2.refs_1_, bf16[8,64,2048]{2,1,0:T(8,128)(2,1)S(1)} %collective-permute-done.23.refs_0_.refs_2_, bf16[8,64,2048]{2,1,0:T(8,128)(2,1)S(1)} %collective-permute-done.24.refs_1_.refs_3_), custom_call_target="tpu_custom_call" | custom-call | flops 6442450944 | bytes 25165824 | tf_op jit(solution)/shard_map/product/pallas_call | solution.py:287
  147.7 6.7 %collective-permute-done.33.refs_1_ = bf16[4,64,2048]{2,1,0:T(8,128)(2,1)S(1)} collective-permute-done((bf16[4,64,2048]{2,1,0:T(8,128)(2,1)S(1)}, bf16[4,64,2048]{2,1,0:T(8,128)(2,1)S(1)}, u32[]{:S(2)}, u32[]{:S(2)}) %collective-permute-start.33) | collective-permute-done | bytes 1048608 | tf_op jit(solution)/shard_map/ppermute | solution.py:29
  154.4 3.3 %product.6.refs_4_ = bf16[512,4096]{1,0:T(8,128)(2,1)} custom-call(bf16[512,2048]{1,0:T(8,128)(2,1)S(1)} %get-tuple-element.27.refs_0_, bf16[4,64,2048]{2,1,0:T(8,128)(2,1)S(1)} %collective-permute-done.33.refs_1_, bf16[4,64,2048]{2,1,0:T(8,128)(2,1)S(1)} %collective-permute-done.34.refs_2_, f32[512,2048]{1,0:T(8,128)S(1)} %product.5.refs_3_), custom_call_target="tpu_custom_call" | custom-call | flops 2147483648 | bytes 16777216 | tf_op jit(solution)/shard_map/product/pallas_call | solution.py:287
  157.6 3.3 %product.7 = bf16[512,4096]{1,0:T(8,128)(2,1)} custom-call(bf16[512,2048]{1,0:T(8,128)(2,1)S(1)} %get-tuple-element.19.refs_0_, bf16[4,64,2048]{2,1,0:T(8,128)(2,1)S(1)} %collective-permute-done.25.refs_1_, bf16[4,64,2048]{2,1,0:T(8,128)(2,1)S(1)} %collective-permute-done.26.refs_2_, ...), custom_call_target="tpu_custom_call", output_to_operand_aliasing={{}: (4, {})} | custom-call | flops 2147483648 | bytes 16777216 | tf_op jit(solution)/shard_map/product/pallas_call | solution.py:287
  (82 shorter events, 21.9 us)
Async XLA Ops:
  0.0 26.3 %collective-permute-start.15 = (bf16[2,64,4096]{2,1,0:T(8,128)(2,1)}, bf16[2,64,4096]{2,1,0:T(8,128)(2,1)S(1)}, u32[]{:S(2)}, u32[]{:S(2)}) collective-permute-start(bf16[2,64,4096]{2,1,0:T(8,128)(2,1)} %refs_0_.3), channel_id=1, source_target_pairs={{0,96},{16,112},{32,0},{48,16},{64,32},{80,48},{96,64},{112,80},{1... | collective-permute-start | bytes 3145736 | tf_op jit(solution)/shard_map/ppermute | solution.py:17
  0.8 25.5 %collective-permute-start.14 = (bf16[2,64,4096]{2,1,0:T(8,128)(2,1)}, bf16[2,64,4096]{2,1,0:T(8,128)(2,1)S(1)}, u32[]{:S(2)}, u32[]{:S(2)}) collective-permute-start(bf16[2,64,4096]{2,1,0:T(8,128)(2,1)} %refs_0_.3), channel_id=1, source_target_pairs={{0,32},{16,48},{32,64},{48,80},{64,96},{80,112},{96,0},{112,16},{1... | collective-permute-start | bytes 3145736 | tf_op jit(solution)/shard_map/ppermute | solution.py:17
  4.0 6.0 %collective-permute-start.2 = (f32[2,128]{1,0:T(2,128)S(1)}, f32[2,128]{1,0:T(2,128)S(1)}, u32[]{:S(2)}, u32[]{:S(2)}) collective-permute-start(f32[2,128]{1,0:T(2,128)S(1)} %broadcast_in_dim.8), channel_id=1, source_target_pairs={{0,8},{1,9},{2,10},{3,11},{4,12},{5,13},{6,14},{7,15},{8,0},{9,1},... | collective-permute-start | bytes 3080 | tf_op jit(solution)/shard_map/ppermute | solution.py:25
  8.6 4.8 %collective-permute-start = (f32[2,128]{1,0:T(2,128)S(1)}, f32[2,128]{1,0:T(2,128)S(1)}, u32[]{:S(2)}, u32[]{:S(2)}) collective-permute-start(f32[2,128]{1,0:T(2,128)S(1)} %broadcast_in_dim.8), channel_id=1, source_target_pairs={{0,4},{1,5},{2,6},{3,7},{4,8},{5,9},{6,10},{7,11},{8,12},{9,13},{1... | collective-permute-start | bytes 3080 | tf_op jit(solution)/shard_map/ppermute | solution.py:25
  13.4 17.5 %collective-permute-start.5 = (f32[4,2,128]{2,1,0:T(2,128)S(1)}, f32[4,2,128]{2,1,0:T(2,128)S(1)}, u32[]{:S(2)}, u32[]{:S(2)}) collective-permute-start(f32[4,2,128]{2,1,0:T(2,128)S(1)} %pad_maximum_fusion.2.refs_2_), channel_id=1, source_target_pairs={{0,2},{1,3},{2,0},{3,1},{4,6},{5,7},{6,4},{7,5},{8,10},{9,11},{10,... | collective-permute-start | bytes 12296 | tf_op jit(solution)/shard_map/ppermute | solution.py:29
  16.7 14.3 %collective-permute-start.4 = (f32[4,2,128]{2,1,0:T(2,128)S(1)}, f32[4,2,128]{2,1,0:T(2,128)S(1)}, u32[]{:S(2)}, u32[]{:S(2)}) collective-permute-start(f32[4,2,128]{2,1,0:T(2,128)S(1)} %pad_maximum_fusion.2.refs_2_), channel_id=1, source_target_pairs={{0,3},{1,0},{2,1},{3,2},{4,7},{5,4},{6,5},{7,6},{8,11},{9,8},{10,9... | collective-permute-start | bytes 12296 | tf_op jit(solution)/shard_map/ppermute | solution.py:29
  17.7 13.2 %collective-permute-start.3 = (f32[4,2,128]{2,1,0:T(2,128)S(1)}, f32[4,2,128]{2,1,0:T(2,128)S(1)}, u32[]{:S(2)}, u32[]{:S(2)}) collective-permute-start(f32[4,2,128]{2,1,0:T(2,128)S(1)} %pad_maximum_fusion.2.refs_2_), channel_id=1, source_target_pairs={{0,1},{1,2},{2,3},{3,0},{4,5},{5,6},{6,7},{7,4},{8,9},{9,10},{10,1... | collective-permute-start | bytes 12296 | tf_op jit(solution)/shard_map/ppermute | solution.py:29
  28.0 17.4 %collective-permute-start.16 = (bf16[1,64,4096]{2,1,0:T(8,128)(2,1)}, bf16[1,64,4096]{2,1,0:T(8,128)(2,1)}, u32[]{:S(2)}, u32[]{:S(2)}) collective-permute-start(bf16[1,64,4096]{2,1,0:T(8,128)(2,1)} %get-tuple-element.20), channel_id=1, source_target_pairs={{0,32},{16,48},{32,64},{48,80},{64,96},{80,112},{96,0},{112,16},{1... | collective-permute-start | bytes 1572872 | tf_op jit(solution)/shard_map/ppermute | solution.py:17
  30.9 14.5 %collective-permute-start.17 = (bf16[1,64,4096]{2,1,0:T(8,128)(2,1)}, bf16[1,64,4096]{2,1,0:T(8,128)(2,1)}, u32[]{:S(2)}, u32[]{:S(2)}) collective-permute-start(bf16[1,64,4096]{2,1,0:T(8,128)(2,1)} %get-tuple-element.21), channel_id=1, source_target_pairs={{0,96},{16,112},{32,0},{48,16},{64,32},{80,48},{96,64},{112,80},{1... | collective-permute-start | bytes 1572872 | tf_op jit(solution)/shard_map/ppermute | solution.py:17
  31.0 12.7 %collective-permute-start.8 = (f32[16,2,128]{2,1,0:T(2,128)S(1)}, f32[16,2,128]{2,1,0:T(2,128)S(1)}, u32[]{:S(2)}, u32[]{:S(2)}) collective-permute-start(f32[16,2,128]{2,1,0:T(2,128)S(1)} %constant_dynamic-update-slice_fusion), channel_id=1, source_target_pairs={{0,64},{16,80},{32,96},{48,112},{64,0},{80,16},{96,32},{112,48},{1... | collective-permute-start | bytes 49160 | tf_op jit(solution)/shard_map/ppermute | solution.py:17
  32.5 12.7 %collective-permute-start.7 = (f32[16,2,128]{2,1,0:T(2,128)S(1)}, f32[16,2,128]{2,1,0:T(2,128)S(1)}, u32[]{:S(2)}, u32[]{:S(2)}) collective-permute-start(f32[16,2,128]{2,1,0:T(2,128)S(1)} %constant_dynamic-update-slice_fusion), channel_id=1, source_target_pairs={{0,96},{16,112},{32,0},{48,16},{64,32},{80,48},{96,64},{112,80},{1... | collective-permute-start | bytes 49160 | tf_op jit(solution)/shard_map/ppermute | solution.py:17
  35.1 10.1 %collective-permute-start.6 = (f32[16,2,128]{2,1,0:T(2,128)S(1)}, f32[16,2,128]{2,1,0:T(2,128)S(1)}, u32[]{:S(2)}, u32[]{:S(2)}) collective-permute-start(f32[16,2,128]{2,1,0:T(2,128)S(1)} %constant_dynamic-update-slice_fusion), channel_id=1, source_target_pairs={{0,32},{16,48},{32,64},{48,80},{64,96},{80,112},{96,0},{112,16},{1... | collective-permute-start | bytes 49160 | tf_op jit(solution)/shard_map/ppermute | solution.py:17
  46.4 6.8 %collective-permute-start.9 = (f32[16,8,128]{2,1,0:T(8,128)S(1)}, f32[16,8,128]{2,1,0:T(8,128)S(1)}, u32[]{:S(2)}, u32[]{:S(2)}) collective-permute-start(f32[16,8,128]{2,1,0:T(8,128)S(1)} %pad_maximum_fusion.1.own_ref), channel_id=1, source_target_pairs={{0,16},{16,0},{32,48},{48,32},{64,80},{80,64},{96,112},{112,96},{1... | collective-permute-start | bytes 196616 | tf_op jit(solution)/shard_map/ppermute | solution.py:21
  49.2 15.6 %collective-permute-start.28 = (bf16[2,64,2048]{2,1,0:T(8,128)(2,1)S(1)}, bf16[2,64,2048]{2,1,0:T(8,128)(2,1)S(1)}, u32[]{:S(2)}, u32[]{:S(2)}) collective-permute-start(bf16[2,64,2048]{2,1,0:T(8,128)(2,1)S(1)} %get-tuple-element.28.refs_0_), channel_id=1, source_target_pairs={{0,12},{1,13},{2,14},{3,15},{4,0},{5,1},{6,2},{7,3},{8,4},{9,5},{1... | collective-permute-start | bytes 1572872 | tf_op jit(solution)/shard_map/ppermute | solution.py:25
  53.3 14.9 %collective-permute-start.27 = (bf16[2,64,2048]{2,1,0:T(8,128)(2,1)S(1)}, bf16[2,64,2048]{2,1,0:T(8,128)(2,1)S(1)}, u32[]{:S(2)}, u32[]{:S(2)}) collective-permute-start(bf16[2,64,2048]{2,1,0:T(8,128)(2,1)S(1)} %get-tuple-element.28.refs_0_), channel_id=1, source_target_pairs={{0,4},{1,5},{2,6},{3,7},{4,8},{5,9},{6,10},{7,11},{8,12},{9,13},{1... | collective-permute-start | bytes 1572872 | tf_op jit(solution)/shard_map/ppermute | solution.py:25
  58.1 14.5 %collective-permute-start.20 = (bf16[2,64,2048]{2,1,0:T(8,128)(2,1)S(1)}, bf16[2,64,2048]{2,1,0:T(8,128)(2,1)S(1)}, u32[]{:S(2)}, u32[]{:S(2)}) collective-permute-start(bf16[2,64,2048]{2,1,0:T(8,128)(2,1)S(1)} %get-tuple-element.22.refs_0_), channel_id=1, source_target_pairs={{0,3},{1,0},{2,1},{3,2},{4,7},{5,4},{6,5},{7,6},{8,11},{9,8},{10,9... | collective-permute-start | bytes 1572872 | tf_op jit(solution)/shard_map/ppermute | solution.py:29
  61.3 14.6 %collective-permute-start.19 = (bf16[2,64,2048]{2,1,0:T(8,128)(2,1)S(1)}, bf16[2,64,2048]{2,1,0:T(8,128)(2,1)S(1)}, u32[]{:S(2)}, u32[]{:S(2)}) collective-permute-start(bf16[2,64,2048]{2,1,0:T(8,128)(2,1)S(1)} %get-tuple-element.22.refs_0_), channel_id=1, source_target_pairs={{0,1},{1,2},{2,3},{3,0},{4,5},{5,6},{6,7},{7,4},{8,9},{9,10},{10,1... | collective-permute-start | bytes 1572872 | tf_op jit(solution)/shard_map/ppermute | solution.py:29
  61.4 28.3 %collective-permute-start.12 = (bf16[2,512,256]{2,1,0:T(8,128)(2,1)S(1)}, bf16[2,512,256]{2,1,0:T(8,128)(2,1)S(1)}, u32[]{:S(2)}, u32[]{:S(2)}) collective-permute-start(bf16[2,512,256]{2,1,0:T(8,128)(2,1)S(1)} %get-tuple-element.33), channel_id=1, source_target_pairs={{0,96},{16,112},{32,0},{48,16},{64,32},{80,48},{96,64},{112,80},{1... | collective-permute-start | bytes 1572872 | tf_op jit(solution)/shard_map/ppermute | solution.py:17
  68.3 11.1 %collective-permute-start.29 = (bf16[1,64,2048]{2,1,0:T(8,128)(2,1)S(1)}, bf16[1,64,2048]{2,1,0:T(8,128)(2,1)S(1)}, u32[]{:S(2)}, u32[]{:S(2)}) collective-permute-start(bf16[1,64,2048]{2,1,0:T(8,128)(2,1)S(1)} %get-tuple-element.29), channel_id=1, source_target_pairs={{0,4},{1,5},{2,6},{3,7},{4,8},{5,9},{6,10},{7,11},{8,12},{9,13},{1... | collective-permute-start | bytes 786440 | tf_op jit(solution)/shard_map/ppermute | solution.py:25
  68.4 11.4 %collective-permute-start.30 = (bf16[1,64,2048]{2,1,0:T(8,128)(2,1)S(1)}, bf16[1,64,2048]{2,1,0:T(8,128)(2,1)S(1)}, u32[]{:S(2)}, u32[]{:S(2)}) collective-permute-start(bf16[1,64,2048]{2,1,0:T(8,128)(2,1)S(1)} %get-tuple-element.30), channel_id=1, source_target_pairs={{0,12},{1,13},{2,14},{3,15},{4,0},{5,1},{6,2},{7,3},{8,4},{9,5},{1... | collective-permute-start | bytes 786440 | tf_op jit(solution)/shard_map/ppermute | solution.py:25
  76.1 8.2 %collective-permute-start.21 = (bf16[1,64,2048]{2,1,0:T(8,128)(2,1)S(1)}, bf16[1,64,2048]{2,1,0:T(8,128)(2,1)S(1)}, u32[]{:S(2)}, u32[]{:S(2)}) collective-permute-start(bf16[1,64,2048]{2,1,0:T(8,128)(2,1)S(1)} %get-tuple-element.23), channel_id=1, source_target_pairs={{0,1},{1,2},{2,3},{3,0},{4,5},{5,6},{6,7},{7,4},{8,9},{9,10},{10,1... | collective-permute-start | bytes 786440 | tf_op jit(solution)/shard_map/ppermute | solution.py:29
  76.2 10.0 %collective-permute-start.22 = (bf16[1,64,2048]{2,1,0:T(8,128)(2,1)S(1)}, bf16[1,64,2048]{2,1,0:T(8,128)(2,1)S(1)}, u32[]{:S(2)}, u32[]{:S(2)}) collective-permute-start(bf16[1,64,2048]{2,1,0:T(8,128)(2,1)S(1)} %get-tuple-element.24), channel_id=1, source_target_pairs={{0,3},{1,0},{2,1},{3,2},{4,7},{5,4},{6,5},{7,6},{8,11},{9,8},{10,9... | collective-permute-start | bytes 786440 | tf_op jit(solution)/shard_map/ppermute | solution.py:29
  79.4 13.4 %collective-permute-start.11 = (bf16[2,512,256]{2,1,0:T(8,128)(2,1)S(1)}, bf16[2,512,256]{2,1,0:T(8,128)(2,1)S(1)}, u32[]{:S(2)}, u32[]{:S(2)}) collective-permute-start(bf16[2,512,256]{2,1,0:T(8,128)(2,1)S(1)} %get-tuple-element.34), channel_id=1, source_target_pairs={{0,64},{16,80},{32,96},{48,112},{64,0},{80,16},{96,32},{112,48},{1... | collective-permute-start | bytes 1572872 | tf_op jit(solution)/shard_map/ppermute | solution.py:17
  80.3 48.1 %collective-permute-start.32 = (bf16[8,64,2048]{2,1,0:T(8,128)(2,1)S(1)}, bf16[8,64,2048]{2,1,0:T(8,128)(2,1)S(1)}, u32[]{:S(2)}, u32[]{:S(2)}) collective-permute-start(bf16[8,64,2048]{2,1,0:T(8,128)(2,1)S(1)} %join.3.refs_1_), channel_id=1, source_target_pairs={{0,3},{1,0},{2,1},{3,2},{4,7},{5,4},{6,5},{7,6},{8,11},{9,8},{10,9... | collective-permute-start | bytes 6291464 | tf_op jit(solution)/shard_map/ppermute | solution.py:29
  84.2 46.5 %collective-permute-start.31 = (bf16[8,64,2048]{2,1,0:T(8,128)(2,1)S(1)}, bf16[8,64,2048]{2,1,0:T(8,128)(2,1)S(1)}, u32[]{:S(2)}, u32[]{:S(2)}) collective-permute-start(bf16[8,64,2048]{2,1,0:T(8,128)(2,1)S(1)} %join.3.refs_1_), channel_id=1, source_target_pairs={{0,1},{1,2},{2,3},{3,0},{4,5},{5,6},{6,7},{7,4},{8,9},{9,10},{10,1... | collective-permute-start | bytes 6291464 | tf_op jit(solution)/shard_map/ppermute | solution.py:29
  86.7 47.8 %collective-permute-start.24 = (bf16[8,64,2048]{2,1,0:T(8,128)(2,1)S(1)}, bf16[8,64,2048]{2,1,0:T(8,128)(2,1)S(1)}, u32[]{:S(2)}, u32[]{:S(2)}) collective-permute-start(bf16[8,64,2048]{2,1,0:T(8,128)(2,1)S(1)} %join.2.refs_1_), channel_id=1, source_target_pairs={{0,12},{1,13},{2,14},{3,15},{4,0},{5,1},{6,2},{7,3},{8,4},{9,5},{1... | collective-permute-start | bytes 6291464 | tf_op jit(solution)/shard_map/ppermute | solution.py:25
  89.7 44.8 %collective-permute-start.23 = (bf16[8,64,2048]{2,1,0:T(8,128)(2,1)S(1)}, bf16[8,64,2048]{2,1,0:T(8,128)(2,1)S(1)}, u32[]{:S(2)}, u32[]{:S(2)}) collective-permute-start(bf16[8,64,2048]{2,1,0:T(8,128)(2,1)S(1)} %join.2.refs_1_), channel_id=1, source_target_pairs={{0,4},{1,5},{2,6},{3,7},{4,8},{5,9},{6,10},{7,11},{8,12},{9,13},{1... | collective-permute-start | bytes 6291464 | tf_op jit(solution)/shard_map/ppermute | solution.py:25
  92.8 11.0 %collective-permute-start.10 = (bf16[2,512,256]{2,1,0:T(8,128)(2,1)S(1)}, bf16[2,512,256]{2,1,0:T(8,128)(2,1)S(1)}, u32[]{:S(2)}, u32[]{:S(2)}) collective-permute-start(bf16[2,512,256]{2,1,0:T(8,128)(2,1)S(1)} %get-tuple-element.35), channel_id=1, source_target_pairs={{0,32},{16,48},{32,64},{48,80},{64,96},{80,112},{96,0},{112,16},{1... | collective-permute-start | bytes 1572872 | tf_op jit(solution)/shard_map/ppermute | solution.py:17
  131.2 23.2 %collective-permute-start.33 = (bf16[4,64,2048]{2,1,0:T(8,128)(2,1)S(1)}, bf16[4,64,2048]{2,1,0:T(8,128)(2,1)S(1)}, u32[]{:S(2)}, u32[]{:S(2)}) collective-permute-start(bf16[4,64,2048]{2,1,0:T(8,128)(2,1)S(1)} %get-tuple-element.31), channel_id=1, source_target_pairs={{0,1},{1,2},{2,3},{3,0},{4,5},{5,6},{6,7},{7,4},{8,9},{9,10},{10,1... | collective-permute-start | bytes 3145736 | tf_op jit(solution)/shard_map/ppermute | solution.py:29
  131.3 23.1 %collective-permute-start.34 = (bf16[4,64,2048]{2,1,0:T(8,128)(2,1)S(1)}, bf16[4,64,2048]{2,1,0:T(8,128)(2,1)S(1)}, u32[]{:S(2)}, u32[]{:S(2)}) collective-permute-start(bf16[4,64,2048]{2,1,0:T(8,128)(2,1)S(1)} %get-tuple-element.32), channel_id=1, source_target_pairs={{0,3},{1,0},{2,1},{3,2},{4,7},{5,4},{6,5},{7,6},{8,11},{9,8},{10,9... | collective-permute-start | bytes 3145736 | tf_op jit(solution)/shard_map/ppermute | solution.py:29
  135.0 22.6 %collective-permute-start.25 = (bf16[4,64,2048]{2,1,0:T(8,128)(2,1)S(1)}, bf16[4,64,2048]{2,1,0:T(8,128)(2,1)S(1)}, u32[]{:S(2)}, u32[]{:S(2)}) collective-permute-start(bf16[4,64,2048]{2,1,0:T(8,128)(2,1)S(1)} %get-tuple-element.25), channel_id=1, source_target_pairs={{0,4},{1,5},{2,6},{3,7},{4,8},{5,9},{6,10},{7,11},{8,12},{9,13},{1... | collective-permute-start | bytes 3145736 | tf_op jit(solution)/shard_map/ppermute | solution.py:25
  135.1 22.6 %collective-permute-start.26 = (bf16[4,64,2048]{2,1,0:T(8,128)(2,1)S(1)}, bf16[4,64,2048]{2,1,0:T(8,128)(2,1)S(1)}, u32[]{:S(2)}, u32[]{:S(2)}) collective-permute-start(bf16[4,64,2048]{2,1,0:T(8,128)(2,1)S(1)} %get-tuple-element.26), channel_id=1, source_target_pairs={{0,12},{1,13},{2,14},{3,15},{4,0},{5,1},{6,2},{7,3},{8,4},{9,5},{1... | collective-permute-start | bytes 3145736 | tf_op jit(solution)/shard_map/ppermute | solution.py:25
  (7 other events, 70.5 us)

commit v4 on v3

--- a/solution.py
+++ b/solution.py
@@ -1,3 +1,5 @@
+import functools
+
 import jax
 import jax.numpy as jnp
 from jax import lax
@@ -86,10 +88,9 @@
     return jnp.where(distance == 0, 0, jnp.where(distance == 3, 1, jnp.where(distance == 1, 2, 3)))
 
 
-def choose_kernel(at_ref, size_ref, density_ref, own_ref, other_ref, pattern_ref, out_ref):
-    t = pl.program_id(0)
+def choose_kernel(d, at_ref, size_ref, density_ref, own_ref, other_ref, pattern_ref, out_ref):
     x, core = at_ref[X], at_ref[CORE]
-    pair = 2 * lax.rem(x + t // 2, 4) + lax.rem(core + lax.rem(t, 2), 2)
+    pair = 2 * lax.rem(x + d, 4) + lax.rem(core + pl.program_id(0), 2)
     i32 = jnp.int32
     sub = lax.broadcasted_iota(i32, (8, BESIDE), 0)
     lane = lax.broadcasted_iota(i32, (1, BESIDE), 1)
@@ -131,14 +132,14 @@
         out_ref[0, 64 * j : 64 * j + 64] = (picked[64 * j : 64 * j + 64] * factor).astype(jnp.bfloat16)
 
 
-def choose_columns(at, sizes, density, own, other, pattern):
+def choose_columns(at, sizes, density, own, other, pattern, d):
     m, width = density.shape
     names = pl.BlockSpec(own.shape, lambda t, p, q: (0, 0, 0))
     return pl.pallas_call(
-        choose_kernel,
+        functools.partial(choose_kernel, d),
         grid_spec=pltpu.PrefetchScalarGridSpec(
             num_scalar_prefetch=2,
-            grid=(8,),
+            grid=(2,),
             in_specs=[
                 pl.BlockSpec((m, width), lambda t, p, q: (0, 0)),
                 names,
@@ -147,9 +148,9 @@
             ],
             out_specs=pl.BlockSpec((1, m, 256), lambda t, p, q: (t, 0, 0)),
         ),
-        out_shape=jax.ShapeDtypeStruct((8, m, 256), jnp.bfloat16),
-        compiler_params=PARAMS,
-        cost_estimate=pl.CostEstimate(flops=2 * m * width * 2048, bytes_accessed=2 * m * (width + 2048), transcendentals=0),
+        out_shape=jax.ShapeDtypeStruct((2, m, 256), jnp.bfloat16),
+        compiler_params=PARAMS,
+        cost_estimate=pl.CostEstimate(flops=2 * m * width * 512, bytes_accessed=2 * m * (width + 512), transcendentals=0),
         name="choose_columns",
     )(at, sizes, density, own, other, pattern)
 
@@ -252,36 +253,33 @@
     )(mine, got)
 
 
-def product_kernel(at, count, started, left_ref, *refs):
-    total = refs[count][...] if started else None
-    for piece in refs[:count]:
-        depth = piece.shape[0] * piece.shape[1]
-        right = piece[...].reshape(depth, piece.shape[2])
-        term = jnp.dot(left_ref[:, at : at + depth], right, preferred_element_type=jnp.float32)
-        total = term if total is None else total + term
-        at += depth
-    refs[-1][...] = total.astype(refs[-1].dtype)
-
-
 def product(left, at, pieces, n, total=None, out=None, column=0, width=None):
     m = left.shape[0]
     step = 512
     depth = sum(p.shape[0] * p.shape[1] for p in pieces)
-    first = column // step
-    specs = [pl.BlockSpec(left.shape, lambda i: (0, 0))]
+    first, count = column // step, len(pieces)
+    specs = [pl.BlockSpec((m, depth), lambda i: (0, at // depth))]
     specs += [pl.BlockSpec(p.shape[:2] + (step,), lambda i: (0, 0, i)) for p in pieces]
     operands = [left, *pieces]
     if total is not None:
-        specs.append(pl.BlockSpec((m, step), lambda i: (0, i)))
+        specs.append(pl.BlockSpec(memory_space=pltpu.VMEM))
         operands.append(total)
     alias = {}
     if out is not None:
-        specs.append(pl.BlockSpec(memory_space=pl.ANY))
+        specs.append(ANY)
         alias = {len(operands): 0}
         operands.append(out)
 
-    def kernel(*refs):
-        product_kernel(at, len(pieces), total is not None, *refs)
+    def kernel(left_ref, *refs):
+        result = None if total is None else refs[count][:, pl.ds(pl.multiple_of(pl.program_id(0) * step, step), step)]
+        low = 0
+        for piece in refs[:count]:
+            high = low + piece.shape[0] * piece.shape[1]
+            right = piece[...].reshape(high - low, step)
+            term = jnp.dot(left_ref[:, low:high], right, preferred_element_type=jnp.float32)
+            result = term if result is None else result + term
+            low = high
+        refs[-1][...] = result.astype(refs[-1].dtype)
 
     shape = jax.ShapeDtypeStruct((m, n), jnp.float32) if width is None else jax.ShapeDtypeStruct((m, width), jnp.bfloat16)
     return pl.pallas_call(
@@ -293,7 +291,7 @@
         input_output_aliases=alias,
         compiler_params=PARAMS,
         cost_estimate=pl.CostEstimate(
-            flops=2 * WEIGHT * m * depth * n, bytes_accessed=2 * WEIGHT * (left.size + (depth + 2 * m) * n), transcendentals=0
+            flops=2 * WEIGHT * m * depth * n, bytes_accessed=2 * WEIGHT * (m * depth + (depth + 2 * m) * n), transcendentals=0
         ),
         name="product",
     )(*operands)
@@ -324,8 +322,8 @@
     v1, v2 = merge_tiles(pick_tiles(at, here, near, ROW), theirs, [width // 2])
     pieces1, pieces2 = relay(v1, shift_z), relay(v2, shift_y)
 
-    chosen = choose_columns(at, atom_sizes, density, names, swap_core(names), density_pattern)
-    chosen = chosen.reshape(4, 2, 8 * b, 4 * b)
+    others = swap_core(names)
+    chosen = [choose_columns(at, atom_sizes, density, names, others, density_pattern, d) for d in range(4)]
     own = [chosen[0]] + [shift_row_x(chosen[d], d) for d in (1, 2, 3)]
 
     g1, g2 = join(pieces1), join(pieces2)

time: 161 us -> 159 us (0.988); the launches traced: 161 us -> 157 us
  waiting for transfers between devices: 83.4 us -> 76.6 us
    ppermute x11, waiting for transfers between devices: 38.7 us -> 27 us  [shift_y(): lax.ppermute(v, 'col', [(4 * z + y, 4 * z + (y + d) % 4) for z in range(4...]
    ppermute x11, starting transfers between devices: 15.6 us -> 18.1 us  [shift_y(): lax.ppermute(v, 'col', [(4 * z + y, 4 * z + (y + d) % 4) for z in range(4...]
    ppermute x11, waiting for transfers between devices: 10 us -> 12.2 us  [shift_z(): lax.ppermute(v, 'col', [(4 * z + y, 4 * ((z + d) % 4) + y) for z in range...]
    ppermute x3, waiting for transfers between devices: 3.79 us -> 5.57 us  [swap_core(): return lax.ppermute(v, 'row', [(r, r ^ 1) for r in range(8)])]
    pallas_call x1 -> x4, Pallas kernels: 4.84 us -> 6.47 us  [choose_columns(): pl.pallas_call(functools.partial(choose_kernel, d), grid_spec=pltpu.Prefe...]
  transfers between devices with their start and end apart: 35 -> 35, of which waited for: 18 -> 18; matrix products, arithmetic and copies ran while one was open for 1% -> 1% of each run, Pallas kernels for 15% -> 16%
where the time goes in v4:
time: 159 us; the launch traced here: 157 us
  waiting for transfers between devices  76.6 us (48%)
  starting transfers between devices  49 us (31%)
  Pallas kernels  29.8 us (19%)
    ppermute x10, waiting for transfers between devices, shift_row_x(): lax.ppermute(v, 'row', [(2 * x + k, 2 * ((x + d) % 4) + k) for x in range...  31.8 us
    ppermute x11, waiting for transfers between devices, shift_y(): lax.ppermute(v, 'col', [(4 * z + y, 4 * z + (y + d) % 4) for z in range(4...  27 us
    ppermute x11, starting transfers between devices, shift_z(): lax.ppermute(v, 'col', [(4 * z + y, 4 * ((z + d) % 4) + y) for z in range...  18.9 us
    ppermute x11, starting transfers between devices, shift_y(): lax.ppermute(v, 'col', [(4 * z + y, 4 * z + (y + d) % 4) for z in range(4...  18.1 us
    pallas_call x4, Pallas kernels, product(): pl.pallas_call(kernel, grid=(n // step,), in_specs=specs, out_specs=pl.Bl...  15.8 us
    ppermute x11, waiting for transfers between devices, shift_z(): lax.ppermute(v, 'col', [(4 * z + y, 4 * ((z + d) % 4) + y) for z in range...  12.2 us
    ppermute x10, starting transfers between devices, shift_row_x(): lax.ppermute(v, 'row', [(2 * x + k, 2 * ((x + d) % 4) + k) for x in range...  11.7 us
    pallas_call x4, Pallas kernels, choose_columns(): pl.pallas_call(functools.partial(choose_kernel, d), grid_spec=pltpu.Prefe...  6.47 us
  transfers between devices with their start and end apart: 35, of which 18 were waited for; matrix products, arithmetic and copies ran while one was open for 1% of the time, Pallas kernels for 16%

profile of v4, /device:TPU:6, one launch (start us, length us, event | category | flops | bytes accessed | tf_op | source)
XLA Modules:
  0.0 157.1 jit_solution(14350453124084252168)
XLA Ops:
  0.8 2.4 %collective-permute-start.14 = (bf16[2,64,4096]{2,1,0:T(8,128)(2,1)}, bf16[2,64,4096]{2,1,0:T(8,128)(2,1)S(1)}, u32[]{:S(2)}, u32[]{:S(2)}) collective-permute-start(bf16[2,64,4096]{2,1,0:T(8,128)(2,1)} %refs_0_.3), channel_id=1, source_target_pairs={{0,32},{16,48},{32,64},{48,80},{64,96},{80,112},{96,0},{112,16},{1... | collective-permute-start | bytes 3145736 | tf_op jit(solution)/shard_map/ppermute | solution.py:19
  4.0 3.9 %collective-permute-start.2 = (f32[2,128]{1,0:T(2,128)S(1)}, f32[2,128]{1,0:T(2,128)S(1)}, u32[]{:S(2)}, u32[]{:S(2)}) collective-permute-start(f32[2,128]{1,0:T(2,128)S(1)} %broadcast_in_dim.8), channel_id=1, source_target_pairs={{0,8},{1,9},{2,10},{3,11},{4,12},{5,13},{6,14},{7,15},{8,0},{9,1},... | collective-permute-start | bytes 3080 | tf_op jit(solution)/shard_map/ppermute | solution.py:27
  11.4 1.9 %collective-permute-done = f32[2,128]{1,0:T(2,128)S(1)} collective-permute-done((f32[2,128]{1,0:T(2,128)S(1)}, f32[2,128]{1,0:T(2,128)S(1)}, u32[]{:S(2)}, u32[]{:S(2)}) %collective-permute-start) | collective-permute-done | bytes 1056 | tf_op jit(solution)/shard_map/ppermute | solution.py:27
  13.4 3.2 %collective-permute-start.5 = (f32[4,2,128]{2,1,0:T(2,128)S(1)}, f32[4,2,128]{2,1,0:T(2,128)S(1)}, u32[]{:S(2)}, u32[]{:S(2)}) collective-permute-start(f32[4,2,128]{2,1,0:T(2,128)S(1)} %pad_maximum_fusion.2.refs_2_), channel_id=1, source_target_pairs={{0,2},{1,3},{2,0},{3,1},{4,6},{5,7},{6,4},{7,5},{8,10},{9,11},{10,... | collective-permute-start | bytes 12296 | tf_op jit(solution)/shard_map/ppermute | solution.py:31
  18.7 7.6 %collective-permute-done.15.refs_1_.refs_2_ = bf16[2,64,4096]{2,1,0:T(8,128)(2,1)S(1)} collective-permute-done((bf16[2,64,4096]{2,1,0:T(8,128)(2,1)}, bf16[2,64,4096]{2,1,0:T(8,128)(2,1)S(1)}, u32[]{:S(2)}, u32[]{:S(2)}) %collective-permute-start.15) | collective-permute-done | bytes 1048608 | tf_op jit(solution)/shard_map/ppermute | solution.py:19
  26.3 1.6 %halves.5 = (bf16[1,64,4096]{2,1,0:T(8,128)(2,1)}, bf16[1,64,4096]{2,1,0:T(8,128)(2,1)}) custom-call(bf16[2,64,4096]{2,1,0:T(8,128)(2,1)S(1)} %collective-permute-done.14.refs_0_.refs_1_, bf16[2,64,4096]{2,1,0:T(8,128)(2,1)S(1)} %collective-permute-done.15.refs_1_.refs_2_, f32[4,2,128]{2,1,0:T(2,128)S(1)} %pad_maximum_fusion.2.refs_2_), custom_call_target="tpu_custom_call" | custom-call | bytes 2097152 | tf_op jit(solution)/shard_map/halves/pallas_call | solution.py:43
  27.9 3.0 %collective-permute-start.16 = (bf16[1,64,4096]{2,1,0:T(8,128)(2,1)}, bf16[1,64,4096]{2,1,0:T(8,128)(2,1)}, u32[]{:S(2)}, u32[]{:S(2)}) collective-permute-start(bf16[1,64,4096]{2,1,0:T(8,128)(2,1)} %get-tuple-element.20), channel_id=1, source_target_pairs={{0,32},{16,48},{32,64},{48,80},{64,96},{80,112},{96,0},{112,16},{1... | collective-permute-start | bytes 1572872 | tf_op jit(solution)/shard_map/ppermute | solution.py:19
  32.5 2.6 %collective-permute-start.7 = (f32[16,2,128]{2,1,0:T(2,128)S(1)}, f32[16,2,128]{2,1,0:T(2,128)S(1)}, u32[]{:S(2)}, u32[]{:S(2)}) collective-permute-start(f32[16,2,128]{2,1,0:T(2,128)S(1)} %constant_dynamic-update-slice_fusion), channel_id=1, source_target_pairs={{0,96},{16,112},{32,0},{48,16},{64,32},{80,48},{96,64},{112,80},{1... | collective-permute-start | bytes 49160 | tf_op jit(solution)/shard_map/ppermute | solution.py:19
  35.8 7.8 %collective-permute-done.8 = f32[16,2,128]{2,1,0:T(2,128)S(1)} collective-permute-done((f32[16,2,128]{2,1,0:T(2,128)S(1)}, f32[16,2,128]{2,1,0:T(2,128)S(1)}, u32[]{:S(2)}, u32[]{:S(2)}) %collective-permute-start.8) | collective-permute-done | bytes 16416 | tf_op jit(solution)/shard_map/ppermute | solution.py:19
  47.4 1.7 %collective-permute-done.18.got_ref = bf16[2,64,4096]{2,1,0:T(8,128)(2,1)S(1)} collective-permute-done((bf16[2,64,4096]{2,1,0:T(8,128)(2,1)S(1)}, bf16[2,64,4096]{2,1,0:T(8,128)(2,1)S(1)}, u32[]{:S(2)}, u32[]{:S(2)}) %collective-permute-start.18) | collective-permute-done | bytes 1048608 | tf_op jit(solution)/shard_map/ppermute | solution.py:23
  49.2 4.1 %collective-permute-start.28 = (bf16[2,64,2048]{2,1,0:T(8,128)(2,1)S(1)}, bf16[2,64,2048]{2,1,0:T(8,128)(2,1)S(1)}, u32[]{:S(2)}, u32[]{:S(2)}) collective-permute-start(bf16[2,64,2048]{2,1,0:T(8,128)(2,1)S(1)} %get-tuple-element.28.refs_0_), channel_id=1, source_target_pairs={{0,12},{1,13},{2,14},{3,15},{4,0},{5,1},{6,2},{7,3},{8,4},{9,5},{1... | collective-permute-start | bytes 1572872 | tf_op jit(solution)/shard_map/ppermute | solution.py:27
  53.3 3.0 %collective-permute-start.20 = (bf16[2,64,2048]{2,1,0:T(8,128)(2,1)S(1)}, bf16[2,64,2048]{2,1,0:T(8,128)(2,1)S(1)}, u32[]{:S(2)}, u32[]{:S(2)}) collective-permute-start(bf16[2,64,2048]{2,1,0:T(8,128)(2,1)S(1)} %get-tuple-element.22.refs_0_), channel_id=1, source_target_pairs={{0,3},{1,0},{2,1},{3,2},{4,7},{5,4},{6,5},{7,6},{8,11},{9,8},{10,9... | collective-permute-start | bytes 1572872 | tf_op jit(solution)/shard_map/ppermute | solution.py:31
  57.6 1.6 %choose_columns.5 = bf16[2,512,256]{2,1,0:T(8,128)(2,1)S(1)} custom-call(s32[7]{0:T(128)S(1)} %stack.46.at_ref, s32[128]{0:T(128)S(1)} %copy-done.3, bf16[512,1024]{1,0:T(8,128)(2,1)S(1)} %copy-done.1, f32[16,8,128]{2,1,0:T(8,128)S(1)} %pad_maximum_fusion.1.own_ref, f32[16,8,128]{2,1,0:T(8,128)S(1)} %collective-permute-done.9.other_ref, s32[8,16]{1,0:T(8,128)S(1)} %copy-done.2), custom_call_target="tpu_custom_call" | custom-call | flops 536870912 | bytes 1572864 | tf_op jit(solution)/shard_map/choose_columns/pallas_call | solution.py:138
  59.6 5.2 %collective-permute-done.28.refs_1_.refs_2_ = bf16[2,64,2048]{2,1,0:T(8,128)(2,1)S(1)} collective-permute-done((bf16[2,64,2048]{2,1,0:T(8,128)(2,1)S(1)}, bf16[2,64,2048]{2,1,0:T(8,128)(2,1)S(1)}, u32[]{:S(2)}, u32[]{:S(2)}) %collective-permute-start.28) | collective-permute-done | bytes 524320 | tf_op jit(solution)/shard_map/ppermute | solution.py:27
  64.8 3.4 %collective-permute-done.27.refs_0_.refs_1_ = bf16[2,64,2048]{2,1,0:T(8,128)(2,1)S(1)} collective-permute-done((bf16[2,64,2048]{2,1,0:T(8,128)(2,1)S(1)}, bf16[2,64,2048]{2,1,0:T(8,128)(2,1)S(1)}, u32[]{:S(2)}, u32[]{:S(2)}) %collective-permute-start.27) | collective-permute-done | bytes 524320 | tf_op jit(solution)/shard_map/ppermute | solution.py:27
  68.4 3.2 %collective-permute-start.30 = (bf16[1,64,2048]{2,1,0:T(8,128)(2,1)S(1)}, bf16[1,64,2048]{2,1,0:T(8,128)(2,1)S(1)}, u32[]{:S(2)}, u32[]{:S(2)}) collective-permute-start(bf16[1,64,2048]{2,1,0:T(8,128)(2,1)S(1)} %get-tuple-element.30), channel_id=1, source_target_pairs={{0,12},{1,13},{2,14},{3,15},{4,0},{5,1},{6,2},{7,3},{8,4},{9,5},{1... | collective-permute-start | bytes 786440 | tf_op jit(solution)/shard_map/ppermute | solution.py:27
  71.9 1.7 %collective-permute-start.21 = (bf16[1,64,2048]{2,1,0:T(8,128)(2,1)S(1)}, bf16[1,64,2048]{2,1,0:T(8,128)(2,1)S(1)}, u32[]{:S(2)}, u32[]{:S(2)}) collective-permute-start(bf16[1,64,2048]{2,1,0:T(8,128)(2,1)S(1)} %get-tuple-element.23), channel_id=1, source_target_pairs={{0,1},{1,2},{2,3},{3,0},{4,5},{5,6},{6,7},{7,4},{8,9},{9,10},{10,1... | collective-permute-start | bytes 786440 | tf_op jit(solution)/shard_map/ppermute | solution.py:31
  73.5 1.6 %collective-permute-start.22 = (bf16[1,64,2048]{2,1,0:T(8,128)(2,1)S(1)}, bf16[1,64,2048]{2,1,0:T(8,128)(2,1)S(1)}, u32[]{:S(2)}, u32[]{:S(2)}) collective-permute-start(bf16[1,64,2048]{2,1,0:T(8,128)(2,1)S(1)} %get-tuple-element.24), channel_id=1, source_target_pairs={{0,3},{1,0},{2,1},{3,2},{4,7},{5,4},{6,5},{7,6},{8,11},{9,8},{10,9... | collective-permute-start | bytes 786440 | tf_op jit(solution)/shard_map/ppermute | solution.py:31
  77.8 3.2 %collective-permute-start.32 = (bf16[8,64,2048]{2,1,0:T(8,128)(2,1)S(1)}, bf16[8,64,2048]{2,1,0:T(8,128)(2,1)S(1)}, u32[]{:S(2)}, u32[]{:S(2)}) collective-permute-start(bf16[8,64,2048]{2,1,0:T(8,128)(2,1)S(1)} %join.3.refs_0_), channel_id=1, source_target_pairs={{0,3},{1,0},{2,1},{3,2},{4,7},{5,4},{6,5},{7,6},{8,11},{9,8},{10,9... | collective-permute-start | bytes 6291464 | tf_op jit(solution)/shard_map/ppermute | solution.py:31
  81.9 2.3 %collective-permute-start.24 = (bf16[8,64,2048]{2,1,0:T(8,128)(2,1)S(1)}, bf16[8,64,2048]{2,1,0:T(8,128)(2,1)S(1)}, u32[]{:S(2)}, u32[]{:S(2)}) collective-permute-start(bf16[8,64,2048]{2,1,0:T(8,128)(2,1)S(1)} %join.2.refs_0_), channel_id=1, source_target_pairs={{0,12},{1,13},{2,14},{3,15},{4,0},{5,1},{6,2},{7,3},{8,4},{9,5},{1... | collective-permute-start | bytes 6291464 | tf_op jit(solution)/shard_map/ppermute | solution.py:27
  85.9 4.9 %collective-permute-done.11.refs_2_ = bf16[2,512,256]{2,1,0:T(8,128)(2,1)S(1)} collective-permute-done((bf16[2,512,256]{2,1,0:T(8,128)(2,1)S(1)}, bf16[2,512,256]{2,1,0:T(8,128)(2,1)S(1)}, u32[]{:S(2)}, u32[]{:S(2)}) %collective-permute-start.11) | collective-permute-done | bytes 524320 | tf_op jit(solution)/shard_map/ppermute | solution.py:19
  92.5 9.9 %collective-permute-done.12.refs_3_ = bf16[2,512,256]{2,1,0:T(8,128)(2,1)S(1)} collective-permute-done((bf16[2,512,256]{2,1,0:T(8,128)(2,1)S(1)}, bf16[2,512,256]{2,1,0:T(8,128)(2,1)S(1)}, u32[]{:S(2)}, u32[]{:S(2)}) %collective-permute-start.12) | collective-permute-done | bytes 524320 | tf_op jit(solution)/shard_map/ppermute | solution.py:19
  102.6 2.6 %collective-permute-done.13.refs_4_ = bf16[4,512,256]{2,1,0:T(8,128)(2,1)S(1)} collective-permute-done((bf16[4,512,256]{2,1,0:T(8,128)(2,1)S(1)}, bf16[4,512,256]{2,1,0:T(8,128)(2,1)S(1)}, u32[]{:S(2)}, u32[]{:S(2)}) %collective-permute-start.13) | collective-permute-done | bytes 1048608 | tf_op jit(solution)/shard_map/ppermute | solution.py:23
  106.8 18.0 %collective-permute-done.32.refs_1_.refs_2_ = bf16[8,64,2048]{2,1,0:T(8,128)(2,1)S(1)} collective-permute-done((bf16[8,64,2048]{2,1,0:T(8,128)(2,1)S(1)}, bf16[8,64,2048]{2,1,0:T(8,128)(2,1)S(1)}, u32[]{:S(2)}, u32[]{:S(2)}) %collective-permute-start.32) | collective-permute-done | bytes 2097184 | tf_op jit(solution)/shard_map/ppermute | solution.py:31
  124.9 2.5 %collective-permute-done.31.refs_0_.refs_1_ = bf16[8,64,2048]{2,1,0:T(8,128)(2,1)S(1)} collective-permute-done((bf16[8,64,2048]{2,1,0:T(8,128)(2,1)S(1)}, bf16[8,64,2048]{2,1,0:T(8,128)(2,1)S(1)}, u32[]{:S(2)}, u32[]{:S(2)}) %collective-permute-start.31) | collective-permute-done | bytes 2097184 | tf_op jit(solution)/shard_map/ppermute | solution.py:31
  127.9 3.2 %collective-permute-start.34 = (bf16[4,64,2048]{2,1,0:T(8,128)(2,1)S(1)}, bf16[4,64,2048]{2,1,0:T(8,128)(2,1)S(1)}, u32[]{:S(2)}, u32[]{:S(2)}) collective-permute-start(bf16[4,64,2048]{2,1,0:T(8,128)(2,1)S(1)} %get-tuple-element.32), channel_id=1, source_target_pairs={{0,3},{1,0},{2,1},{3,2},{4,7},{5,4},{6,5},{7,6},{8,11},{9,8},{10,9... | collective-permute-start | bytes 3145736 | tf_op jit(solution)/shard_map/ppermute | solution.py:31
  131.7 3.2 %collective-permute-start.26 = (bf16[4,64,2048]{2,1,0:T(8,128)(2,1)S(1)}, bf16[4,64,2048]{2,1,0:T(8,128)(2,1)S(1)}, u32[]{:S(2)}, u32[]{:S(2)}) collective-permute-start(bf16[4,64,2048]{2,1,0:T(8,128)(2,1)S(1)} %get-tuple-element.26), channel_id=1, source_target_pairs={{0,12},{1,13},{2,14},{3,15},{4,0},{5,1},{6,2},{7,3},{8,4},{9,5},{1... | collective-permute-start | bytes 3145736 | tf_op jit(solution)/shard_map/ppermute | solution.py:27
  134.9 4.8 %product.5.refs_2_ = f32[512,2048]{1,0:T(8,128)S(1)} custom-call(bf16[512,2048]{1,0:T(8,128)(2,1)S(1)} %get-tuple-element.27.left_ref, bf16[8,64,2048]{2,1,0:T(8,128)(2,1)S(1)} %join.3.refs_0_, bf16[8,64,2048]{2,1,0:T(8,128)(2,1)S(1)} %collective-permute-done.31.refs_0_.refs_1_, bf16[8,64,2048]{2,1,0:T(8,128)(2,1)S(1)} %collective-permute-done.32.refs_1_.refs_2_), custom_call_target="tpu_custom_call" | custom-call | flops 6442450944 | bytes 24117248 | tf_op jit(solution)/shard_map/product/pallas_call | solution.py:285
  139.7 4.8 %product.4.refs_2_ = f32[512,2048]{1,0:T(8,128)S(1)} custom-call(bf16[512,2048]{1,0:T(8,128)(2,1)S(1)} %get-tuple-element.19.left_ref, bf16[8,64,2048]{2,1,0:T(8,128)(2,1)S(1)} %join.2.refs_0_, bf16[8,64,2048]{2,1,0:T(8,128)(2,1)S(1)} %collective-permute-done.23.refs_0_.refs_1_, bf16[8,64,2048]{2,1,0:T(8,128)(2,1)S(1)} %collective-permute-done.24.refs_1_.refs_2_), custom_call_target="tpu_custom_call" | custom-call | flops 6442450944 | bytes 24117248 | tf_op jit(solution)/shard_map/product/pallas_call | solution.py:285
  144.5 6.2 %collective-permute-done.33.refs_0_ = bf16[4,64,2048]{2,1,0:T(8,128)(2,1)S(1)} collective-permute-done((bf16[4,64,2048]{2,1,0:T(8,128)(2,1)S(1)}, bf16[4,64,2048]{2,1,0:T(8,128)(2,1)S(1)}, u32[]{:S(2)}, u32[]{:S(2)}) %collective-permute-start.33) | collective-permute-done | bytes 1048608 | tf_op jit(solution)/shard_map/ppermute | solution.py:31
  150.7 3.1 %product.6.refs_3_ = bf16[512,4096]{1,0:T(8,128)(2,1)} custom-call(bf16[512,2048]{1,0:T(8,128)(2,1)S(1)} %get-tuple-element.27.left_ref, bf16[4,64,2048]{2,1,0:T(8,128)(2,1)S(1)} %collective-permute-done.33.refs_0_, bf16[4,64,2048]{2,1,0:T(8,128)(2,1)S(1)} %collective-permute-done.34.refs_1_, f32[512,2048]{1,0:T(8,128)S(1)} %product.5.refs_2_), custom_call_target="tpu_custom_call" | custom-call | flops 2147483648 | bytes 13631488 | tf_op jit(solution)/shard_map/product/pallas_call | solution.py:285
  153.9 3.1 %product.7 = bf16[512,4096]{1,0:T(8,128)(2,1)} custom-call(bf16[512,2048]{1,0:T(8,128)(2,1)S(1)} %get-tuple-element.19.left_ref, bf16[4,64,2048]{2,1,0:T(8,128)(2,1)S(1)} %collective-permute-done.25.refs_0_, bf16[4,64,2048]{2,1,0:T(8,128)(2,1)S(1)} %collective-permute-done.26.refs_1_, ...), custom_call_target="tpu_custom_call", output_to_operand_aliasing={{}: (4, {})} | custom-call | flops 2147483648 | bytes 13631488 | tf_op jit(solution)/shard_map/product/pallas_call | solution.py:285
  (84 shorter events, 25.1 us)
Async XLA Ops:
  0.0 26.3 %collective-permute-start.15 = (bf16[2,64,4096]{2,1,0:T(8,128)(2,1)}, bf16[2,64,4096]{2,1,0:T(8,128)(2,1)S(1)}, u32[]{:S(2)}, u32[]{:S(2)}) collective-permute-start(bf16[2,64,4096]{2,1,0:T(8,128)(2,1)} %refs_0_.3), channel_id=1, source_target_pairs={{0,96},{16,112},{32,0},{48,16},{64,32},{80,48},{96,64},{112,80},{1... | collective-permute-start | bytes 3145736 | tf_op jit(solution)/shard_map/ppermute | solution.py:19
  0.8 25.5 %collective-permute-start.14 = (bf16[2,64,4096]{2,1,0:T(8,128)(2,1)}, bf16[2,64,4096]{2,1,0:T(8,128)(2,1)S(1)}, u32[]{:S(2)}, u32[]{:S(2)}) collective-permute-start(bf16[2,64,4096]{2,1,0:T(8,128)(2,1)} %refs_0_.3), channel_id=1, source_target_pairs={{0,32},{16,48},{32,64},{48,80},{64,96},{80,112},{96,0},{112,16},{1... | collective-permute-start | bytes 3145736 | tf_op jit(solution)/shard_map/ppermute | solution.py:19
  4.0 6.0 %collective-permute-start.2 = (f32[2,128]{1,0:T(2,128)S(1)}, f32[2,128]{1,0:T(2,128)S(1)}, u32[]{:S(2)}, u32[]{:S(2)}) collective-permute-start(f32[2,128]{1,0:T(2,128)S(1)} %broadcast_in_dim.8), channel_id=1, source_target_pairs={{0,8},{1,9},{2,10},{3,11},{4,12},{5,13},{6,14},{7,15},{8,0},{9,1},... | collective-permute-start | bytes 3080 | tf_op jit(solution)/shard_map/ppermute | solution.py:27
  7.9 3.6 %collective-permute-start.1 = (f32[2,128]{1,0:T(2,128)S(1)}, f32[2,128]{1,0:T(2,128)S(1)}, u32[]{:S(2)}, u32[]{:S(2)}) collective-permute-start(f32[2,128]{1,0:T(2,128)S(1)} %broadcast_in_dim.8), channel_id=1, source_target_pairs={{0,12},{1,13},{2,14},{3,15},{4,0},{5,1},{6,2},{7,3},{8,4},{9,5},{1... | collective-permute-start | bytes 3080 | tf_op jit(solution)/shard_map/ppermute | solution.py:27
  8.6 4.8 %collective-permute-start = (f32[2,128]{1,0:T(2,128)S(1)}, f32[2,128]{1,0:T(2,128)S(1)}, u32[]{:S(2)}, u32[]{:S(2)}) collective-permute-start(f32[2,128]{1,0:T(2,128)S(1)} %broadcast_in_dim.8), channel_id=1, source_target_pairs={{0,4},{1,5},{2,6},{3,7},{4,8},{5,9},{6,10},{7,11},{8,12},{9,13},{1... | collective-permute-start | bytes 3080 | tf_op jit(solution)/shard_map/ppermute | solution.py:27
  13.4 17.5 %collective-permute-start.5 = (f32[4,2,128]{2,1,0:T(2,128)S(1)}, f32[4,2,128]{2,1,0:T(2,128)S(1)}, u32[]{:S(2)}, u32[]{:S(2)}) collective-permute-start(f32[4,2,128]{2,1,0:T(2,128)S(1)} %pad_maximum_fusion.2.refs_2_), channel_id=1, source_target_pairs={{0,2},{1,3},{2,0},{3,1},{4,6},{5,7},{6,4},{7,5},{8,10},{9,11},{10,... | collective-permute-start | bytes 12296 | tf_op jit(solution)/shard_map/ppermute | solution.py:31
  16.7 14.3 %collective-permute-start.4 = (f32[4,2,128]{2,1,0:T(2,128)S(1)}, f32[4,2,128]{2,1,0:T(2,128)S(1)}, u32[]{:S(2)}, u32[]{:S(2)}) collective-permute-start(f32[4,2,128]{2,1,0:T(2,128)S(1)} %pad_maximum_fusion.2.refs_2_), channel_id=1, source_target_pairs={{0,3},{1,0},{2,1},{3,2},{4,7},{5,4},{6,5},{7,6},{8,11},{9,8},{10,9... | collective-permute-start | bytes 12296 | tf_op jit(solution)/shard_map/ppermute | solution.py:31
  17.7 13.2 %collective-permute-start.3 = (f32[4,2,128]{2,1,0:T(2,128)S(1)}, f32[4,2,128]{2,1,0:T(2,128)S(1)}, u32[]{:S(2)}, u32[]{:S(2)}) collective-permute-start(f32[4,2,128]{2,1,0:T(2,128)S(1)} %pad_maximum_fusion.2.refs_2_), channel_id=1, source_target_pairs={{0,1},{1,2},{2,3},{3,0},{4,5},{5,6},{6,7},{7,4},{8,9},{9,10},{10,1... | collective-permute-start | bytes 12296 | tf_op jit(solution)/shard_map/ppermute | solution.py:31
  27.9 17.4 %collective-permute-start.16 = (bf16[1,64,4096]{2,1,0:T(8,128)(2,1)}, bf16[1,64,4096]{2,1,0:T(8,128)(2,1)}, u32[]{:S(2)}, u32[]{:S(2)}) collective-permute-start(bf16[1,64,4096]{2,1,0:T(8,128)(2,1)} %get-tuple-element.20), channel_id=1, source_target_pairs={{0,32},{16,48},{32,64},{48,80},{64,96},{80,112},{96,0},{112,16},{1... | collective-permute-start | bytes 1572872 | tf_op jit(solution)/shard_map/ppermute | solution.py:19
  30.9 14.5 %collective-permute-start.17 = (bf16[1,64,4096]{2,1,0:T(8,128)(2,1)}, bf16[1,64,4096]{2,1,0:T(8,128)(2,1)}, u32[]{:S(2)}, u32[]{:S(2)}) collective-permute-start(bf16[1,64,4096]{2,1,0:T(8,128)(2,1)} %get-tuple-element.21), channel_id=1, source_target_pairs={{0,96},{16,112},{32,0},{48,16},{64,32},{80,48},{96,64},{112,80},{1... | collective-permute-start | bytes 1572872 | tf_op jit(solution)/shard_map/ppermute | solution.py:19
  31.0 12.7 %collective-permute-start.8 = (f32[16,2,128]{2,1,0:T(2,128)S(1)}, f32[16,2,128]{2,1,0:T(2,128)S(1)}, u32[]{:S(2)}, u32[]{:S(2)}) collective-permute-start(f32[16,2,128]{2,1,0:T(2,128)S(1)} %constant_dynamic-update-slice_fusion), channel_id=1, source_target_pairs={{0,64},{16,80},{32,96},{48,112},{64,0},{80,16},{96,32},{112,48},{1... | collective-permute-start | bytes 49160 | tf_op jit(solution)/shard_map/ppermute | solution.py:19
  32.5 12.7 %collective-permute-start.7 = (f32[16,2,128]{2,1,0:T(2,128)S(1)}, f32[16,2,128]{2,1,0:T(2,128)S(1)}, u32[]{:S(2)}, u32[]{:S(2)}) collective-permute-start(f32[16,2,128]{2,1,0:T(2,128)S(1)} %constant_dynamic-update-slice_fusion), channel_id=1, source_target_pairs={{0,96},{16,112},{32,0},{48,16},{64,32},{80,48},{96,64},{112,80},{1... | collective-permute-start | bytes 49160 | tf_op jit(solution)/shard_map/ppermute | solution.py:19
  35.1 10.1 %collective-permute-start.6 = (f32[16,2,128]{2,1,0:T(2,128)S(1)}, f32[16,2,128]{2,1,0:T(2,128)S(1)}, u32[]{:S(2)}, u32[]{:S(2)}) collective-permute-start(f32[16,2,128]{2,1,0:T(2,128)S(1)} %constant_dynamic-update-slice_fusion), channel_id=1, source_target_pairs={{0,32},{16,48},{32,64},{48,80},{64,96},{80,112},{96,0},{112,16},{1... | collective-permute-start | bytes 49160 | tf_op jit(solution)/shard_map/ppermute | solution.py:19
  49.2 15.6 %collective-permute-start.28 = (bf16[2,64,2048]{2,1,0:T(8,128)(2,1)S(1)}, bf16[2,64,2048]{2,1,0:T(8,128)(2,1)S(1)}, u32[]{:S(2)}, u32[]{:S(2)}) collective-permute-start(bf16[2,64,2048]{2,1,0:T(8,128)(2,1)S(1)} %get-tuple-element.28.refs_0_), channel_id=1, source_target_pairs={{0,12},{1,13},{2,14},{3,15},{4,0},{5,1},{6,2},{7,3},{8,4},{9,5},{1... | collective-permute-start | bytes 1572872 | tf_op jit(solution)/shard_map/ppermute | solution.py:27
  53.3 14.9 %collective-permute-start.27 = (bf16[2,64,2048]{2,1,0:T(8,128)(2,1)S(1)}, bf16[2,64,2048]{2,1,0:T(8,128)(2,1)S(1)}, u32[]{:S(2)}, u32[]{:S(2)}) collective-permute-start(bf16[2,64,2048]{2,1,0:T(8,128)(2,1)S(1)} %get-tuple-element.28.refs_0_), channel_id=1, source_target_pairs={{0,4},{1,5},{2,6},{3,7},{4,8},{5,9},{6,10},{7,11},{8,12},{9,13},{1... | collective-permute-start | bytes 1572872 | tf_op jit(solution)/shard_map/ppermute | solution.py:27
  53.3 18.4 %collective-permute-start.20 = (bf16[2,64,2048]{2,1,0:T(8,128)(2,1)S(1)}, bf16[2,64,2048]{2,1,0:T(8,128)(2,1)S(1)}, u32[]{:S(2)}, u32[]{:S(2)}) collective-permute-start(bf16[2,64,2048]{2,1,0:T(8,128)(2,1)S(1)} %get-tuple-element.22.refs_0_), channel_id=1, source_target_pairs={{0,3},{1,0},{2,1},{3,2},{4,7},{5,4},{6,5},{7,6},{8,11},{9,8},{10,9... | collective-permute-start | bytes 1572872 | tf_op jit(solution)/shard_map/ppermute | solution.py:31
  56.3 15.4 %collective-permute-start.19 = (bf16[2,64,2048]{2,1,0:T(8,128)(2,1)S(1)}, bf16[2,64,2048]{2,1,0:T(8,128)(2,1)S(1)}, u32[]{:S(2)}, u32[]{:S(2)}) collective-permute-start(bf16[2,64,2048]{2,1,0:T(8,128)(2,1)S(1)} %get-tuple-element.22.refs_0_), channel_id=1, source_target_pairs={{0,1},{1,2},{2,3},{3,0},{4,5},{5,6},{6,7},{7,4},{8,9},{9,10},{10,1... | collective-permute-start | bytes 1572872 | tf_op jit(solution)/shard_map/ppermute | solution.py:31
  59.2 25.0 %collective-permute-start.10 = (bf16[2,512,256]{2,1,0:T(8,128)(2,1)S(1)}, bf16[2,512,256]{2,1,0:T(8,128)(2,1)S(1)}, u32[]{:S(2)}, u32[]{:S(2)}) collective-permute-start(bf16[2,512,256]{2,1,0:T(8,128)(2,1)S(1)} %choose_columns.5), channel_id=1, source_target_pairs={{0,32},{16,48},{32,64},{48,80},{64,96},{80,112},{96,0},{112,16},{1... | collective-permute-start | bytes 1572872 | tf_op jit(solution)/shard_map/ppermute | solution.py:19
  68.4 8.5 %collective-permute-start.29 = (bf16[1,64,2048]{2,1,0:T(8,128)(2,1)S(1)}, bf16[1,64,2048]{2,1,0:T(8,128)(2,1)S(1)}, u32[]{:S(2)}, u32[]{:S(2)}) collective-permute-start(bf16[1,64,2048]{2,1,0:T(8,128)(2,1)S(1)} %get-tuple-element.29), channel_id=1, source_target_pairs={{0,4},{1,5},{2,6},{3,7},{4,8},{5,9},{6,10},{7,11},{8,12},{9,13},{1... | collective-permute-start | bytes 786440 | tf_op jit(solution)/shard_map/ppermute | solution.py:27
  68.4 8.8 %collective-permute-start.30 = (bf16[1,64,2048]{2,1,0:T(8,128)(2,1)S(1)}, bf16[1,64,2048]{2,1,0:T(8,128)(2,1)S(1)}, u32[]{:S(2)}, u32[]{:S(2)}) collective-permute-start(bf16[1,64,2048]{2,1,0:T(8,128)(2,1)S(1)} %get-tuple-element.30), channel_id=1, source_target_pairs={{0,12},{1,13},{2,14},{3,15},{4,0},{5,1},{6,2},{7,3},{8,4},{9,5},{1... | collective-permute-start | bytes 786440 | tf_op jit(solution)/shard_map/ppermute | solution.py:27
  71.9 9.2 %collective-permute-start.21 = (bf16[1,64,2048]{2,1,0:T(8,128)(2,1)S(1)}, bf16[1,64,2048]{2,1,0:T(8,128)(2,1)S(1)}, u32[]{:S(2)}, u32[]{:S(2)}) collective-permute-start(bf16[1,64,2048]{2,1,0:T(8,128)(2,1)S(1)} %get-tuple-element.23), channel_id=1, source_target_pairs={{0,1},{1,2},{2,3},{3,0},{4,5},{5,6},{6,7},{7,4},{8,9},{9,10},{10,1... | collective-permute-start | bytes 786440 | tf_op jit(solution)/shard_map/ppermute | solution.py:31
  73.5 7.8 %collective-permute-start.22 = (bf16[1,64,2048]{2,1,0:T(8,128)(2,1)S(1)}, bf16[1,64,2048]{2,1,0:T(8,128)(2,1)S(1)}, u32[]{:S(2)}, u32[]{:S(2)}) collective-permute-start(bf16[1,64,2048]{2,1,0:T(8,128)(2,1)S(1)} %get-tuple-element.24), channel_id=1, source_target_pairs={{0,3},{1,0},{2,1},{3,2},{4,7},{5,4},{6,5},{7,6},{8,11},{9,8},{10,9... | collective-permute-start | bytes 786440 | tf_op jit(solution)/shard_map/ppermute | solution.py:31
  76.8 13.9 %collective-permute-start.11 = (bf16[2,512,256]{2,1,0:T(8,128)(2,1)S(1)}, bf16[2,512,256]{2,1,0:T(8,128)(2,1)S(1)}, u32[]{:S(2)}, u32[]{:S(2)}) collective-permute-start(bf16[2,512,256]{2,1,0:T(8,128)(2,1)S(1)} %choose_columns.6), channel_id=1, source_target_pairs={{0,64},{16,80},{32,96},{48,112},{64,0},{80,16},{96,32},{112,48},{1... | collective-permute-start | bytes 1572872 | tf_op jit(solution)/shard_map/ppermute | solution.py:19
  77.8 47.0 %collective-permute-start.32 = (bf16[8,64,2048]{2,1,0:T(8,128)(2,1)S(1)}, bf16[8,64,2048]{2,1,0:T(8,128)(2,1)S(1)}, u32[]{:S(2)}, u32[]{:S(2)}) collective-permute-start(bf16[8,64,2048]{2,1,0:T(8,128)(2,1)S(1)} %join.3.refs_0_), channel_id=1, source_target_pairs={{0,3},{1,0},{2,1},{3,2},{4,7},{5,4},{6,5},{7,6},{8,11},{9,8},{10,9... | collective-permute-start | bytes 6291464 | tf_op jit(solution)/shard_map/ppermute | solution.py:31
  81.1 46.2 %collective-permute-start.31 = (bf16[8,64,2048]{2,1,0:T(8,128)(2,1)S(1)}, bf16[8,64,2048]{2,1,0:T(8,128)(2,1)S(1)}, u32[]{:S(2)}, u32[]{:S(2)}) collective-permute-start(bf16[8,64,2048]{2,1,0:T(8,128)(2,1)S(1)} %join.3.refs_0_), channel_id=1, source_target_pairs={{0,1},{1,2},{2,3},{3,0},{4,5},{5,6},{6,7},{7,4},{8,9},{9,10},{10,1... | collective-permute-start | bytes 6291464 | tf_op jit(solution)/shard_map/ppermute | solution.py:31
  81.9 49.2 %collective-permute-start.24 = (bf16[8,64,2048]{2,1,0:T(8,128)(2,1)S(1)}, bf16[8,64,2048]{2,1,0:T(8,128)(2,1)S(1)}, u32[]{:S(2)}, u32[]{:S(2)}) collective-permute-start(bf16[8,64,2048]{2,1,0:T(8,128)(2,1)S(1)} %join.2.refs_0_), channel_id=1, source_target_pairs={{0,12},{1,13},{2,14},{3,15},{4,0},{5,1},{6,2},{7,3},{8,4},{9,5},{1... | collective-permute-start | bytes 6291464 | tf_op jit(solution)/shard_map/ppermute | solution.py:27
  84.2 46.9 %collective-permute-start.23 = (bf16[8,64,2048]{2,1,0:T(8,128)(2,1)S(1)}, bf16[8,64,2048]{2,1,0:T(8,128)(2,1)S(1)}, u32[]{:S(2)}, u32[]{:S(2)}) collective-permute-start(bf16[8,64,2048]{2,1,0:T(8,128)(2,1)S(1)} %join.2.refs_0_), channel_id=1, source_target_pairs={{0,4},{1,5},{2,6},{3,7},{4,8},{5,9},{6,10},{7,11},{8,12},{9,13},{1... | collective-permute-start | bytes 6291464 | tf_op jit(solution)/shard_map/ppermute | solution.py:27
  90.8 11.6 %collective-permute-start.12 = (bf16[2,512,256]{2,1,0:T(8,128)(2,1)S(1)}, bf16[2,512,256]{2,1,0:T(8,128)(2,1)S(1)}, u32[]{:S(2)}, u32[]{:S(2)}) collective-permute-start(bf16[2,512,256]{2,1,0:T(8,128)(2,1)S(1)} %choose_columns.7), channel_id=1, source_target_pairs={{0,96},{16,112},{32,0},{48,16},{64,32},{80,48},{96,64},{112,80},{1... | collective-permute-start | bytes 1572872 | tf_op jit(solution)/shard_map/ppermute | solution.py:19
  127.8 22.9 %collective-permute-start.33 = (bf16[4,64,2048]{2,1,0:T(8,128)(2,1)S(1)}, bf16[4,64,2048]{2,1,0:T(8,128)(2,1)S(1)}, u32[]{:S(2)}, u32[]{:S(2)}) collective-permute-start(bf16[4,64,2048]{2,1,0:T(8,128)(2,1)S(1)} %get-tuple-element.31), channel_id=1, source_target_pairs={{0,1},{1,2},{2,3},{3,0},{4,5},{5,6},{6,7},{7,4},{8,9},{9,10},{10,1... | collective-permute-start | bytes 3145736 | tf_op jit(solution)/shard_map/ppermute | solution.py:31
  127.9 22.8 %collective-permute-start.34 = (bf16[4,64,2048]{2,1,0:T(8,128)(2,1)S(1)}, bf16[4,64,2048]{2,1,0:T(8,128)(2,1)S(1)}, u32[]{:S(2)}, u32[]{:S(2)}) collective-permute-start(bf16[4,64,2048]{2,1,0:T(8,128)(2,1)S(1)} %get-tuple-element.32), channel_id=1, source_target_pairs={{0,3},{1,0},{2,1},{3,2},{4,7},{5,4},{6,5},{7,6},{8,11},{9,8},{10,9... | collective-permute-start | bytes 3145736 | tf_op jit(solution)/shard_map/ppermute | solution.py:31
  131.6 22.4 %collective-permute-start.25 = (bf16[4,64,2048]{2,1,0:T(8,128)(2,1)S(1)}, bf16[4,64,2048]{2,1,0:T(8,128)(2,1)S(1)}, u32[]{:S(2)}, u32[]{:S(2)}) collective-permute-start(bf16[4,64,2048]{2,1,0:T(8,128)(2,1)S(1)} %get-tuple-element.25), channel_id=1, source_target_pairs={{0,4},{1,5},{2,6},{3,7},{4,8},{5,9},{6,10},{7,11},{8,12},{9,13},{1... | collective-permute-start | bytes 3145736 | tf_op jit(solution)/shard_map/ppermute | solution.py:27
  131.7 22.3 %collective-permute-start.26 = (bf16[4,64,2048]{2,1,0:T(8,128)(2,1)S(1)}, bf16[4,64,2048]{2,1,0:T(8,128)(2,1)S(1)}, u32[]{:S(2)}, u32[]{:S(2)}) collective-permute-start(bf16[4,64,2048]{2,1,0:T(8,128)(2,1)S(1)} %get-tuple-element.26), channel_id=1, source_target_pairs={{0,12},{1,13},{2,14},{3,15},{4,0},{5,1},{6,2},{7,3},{8,4},{9,5},{1... | collective-permute-start | bytes 3145736 | tf_op jit(solution)/shard_map/ppermute | solution.py:27
  (7 other events, 82.7 us)

commit v5 on v4

--- a/solution.py
+++ b/solution.py
@@ -31,25 +31,39 @@
     return lax.ppermute(v, "col", [(4 * z + y, 4 * z + (y + d) % 4) for z in range(4) for y in range(4)])
 
 
+def copy_parts(inputs, outputs, others=()):
+    heights = [sum(high - low for _, low, high in parts) for parts in outputs]
+    skip, total = len(inputs) + len(others), sum(len(parts) for parts in outputs)
+
+    def kernel(*refs):
+        sems, copies = refs[-1], []
+        for parts, out in zip(outputs, refs[skip:]):
+            at = 0
+            for i, low, high in parts:
+                source, target = refs[i].at[pl.ds(low, high - low)], out.at[pl.ds(at, high - low)]
+                copies.append(pltpu.make_async_copy(source, target, sems.at[len(copies)]))
+                at += high - low
+        for copy in copies:
+            copy.start()
+        for copy in copies:
+            copy.wait()
+
+    tail = inputs[0].shape[1:]
+    return pl.pallas_call(
+        kernel,
+        in_specs=[ANY] * skip,
+        out_specs=[ANY] * len(outputs),
+        out_shape=[jax.ShapeDtypeStruct((h,) + tail, jnp.bfloat16) for h in heights],
+        scratch_shapes=[pltpu.SemaphoreType.DMA((total,))],
+        compiler_params=PARAMS,
+        cost_estimate=pl.CostEstimate(flops=0, bytes_accessed=4 * sum(heights) * tail[0] * tail[1], transcendentals=0),
+        name="copy_parts",
+    )(*inputs, *others)
+
+
 def halves(minus, plus, others=()):
-    count, b, n = minus.shape
-    half, step = count // 2, min(n, 1024)
-
-    def kernel(*refs):
-        refs[-2][...] = refs[0][...]
-        refs[-1][...] = refs[1][...]
-
-    spec = pl.BlockSpec((half, b, step), lambda i: (0, 0, i))
-    return pl.pallas_call(
-        kernel,
-        grid=(n // step,),
-        in_specs=[spec, pl.BlockSpec((half, b, step), lambda i: (1, 0, i))] + [ANY] * len(others),
-        out_specs=[spec, spec],
-        out_shape=[jax.ShapeDtypeStruct((half, b, n), jnp.bfloat16)] * 2,
-        compiler_params=PARAMS,
-        cost_estimate=pl.CostEstimate(flops=0, bytes_accessed=4 * b * n * count, transcendentals=0),
-        name="halves",
-    )(minus, plus, *others)
+    count = minus.shape[0]
+    return copy_parts([minus, plus], [[(0, 0, count // 2)], [(1, count // 2, count)]], others)
 
 
 def relay(v, shift, others=()):
@@ -59,26 +73,7 @@
 
 
 def join(pieces):
-    _, b, n = pieces[0].shape
-    step = 512
-
-    def kernel(*refs):
-        at = 0
-        for ref in refs[:-1]:
-            refs[-1][at : at + ref.shape[0]] = ref[...]
-            at += ref.shape[0]
-
-    total = sum(p.shape[0] for p in pieces)
-    return pl.pallas_call(
-        kernel,
-        grid=(n // step,),
-        in_specs=[pl.BlockSpec((p.shape[0], b, step), lambda i: (0, 0, i)) for p in pieces],
-        out_specs=pl.BlockSpec((total, b, step), lambda i: (0, 0, i)),
-        out_shape=jax.ShapeDtypeStruct((total, b, n), jnp.bfloat16),
-        compiler_params=PARAMS,
-        cost_estimate=pl.CostEstimate(flops=0, bytes_accessed=4 * b * n * total, transcendentals=0),
-        name="join",
-    )(*pieces)
+    return copy_parts(pieces, [[(i, 0, p.shape[0]) for i, p in enumerate(pieces)]])[0]
 
 
 ROW, OTHER, X, CORE, Z, Y, COL = range(7)

time: 159 us -> 158 us (level)
    pallas_call x7, Pallas kernels: 3.96 us -> 1.81 us  [copy_parts(): pl.pallas_call(kernel, in_specs=[ANY] * skip, out_specs=[ANY] * len(outpu...]
    ppermute x11, starting transfers between devices: 18.9 us -> 20.6 us  [shift_z(): lax.ppermute(v, 'col', [(4 * z + y, 4 * ((z + d) % 4) + y) for z in range...]
  transfers between devices with their start and end apart: 35 -> 35, of which waited for: 18 -> 16; matrix products, arithmetic and copies ran while one was open for 1% -> 1% of each run, Pallas kernels for 16% -> 16%
where the time goes in v5:
time: 158 us; the launch traced here: 157 us
  waiting for transfers between devices  76.5 us (48%)
  starting transfers between devices  49.9 us (32%)
  Pallas kernels  28.5 us (18%)
    ppermute x10, waiting for transfers between devices, shift_row_x(): lax.ppermute(v, 'row', [(2 * x + k, 2 * ((x + d) % 4) + k) for x in range...  32.6 us
    ppermute x11, waiting for transfers between devices, shift_y(): lax.ppermute(v, 'col', [(4 * z + y, 4 * z + (y + d) % 4) for z in range(4...  26.7 us
    ppermute x11, starting transfers between devices, shift_z(): lax.ppermute(v, 'col', [(4 * z + y, 4 * ((z + d) % 4) + y) for z in range...  20.6 us
    ppermute x11, starting transfers between devices, shift_y(): lax.ppermute(v, 'col', [(4 * z + y, 4 * z + (y + d) % 4) for z in range(4...  17.6 us
    pallas_call x4, Pallas kernels, product(): pl.pallas_call(kernel, grid=(n // step,), in_specs=specs, out_specs=pl.Bl...  15.8 us
    ppermute x11, waiting for transfers between devices, shift_z(): lax.ppermute(v, 'col', [(4 * z + y, 4 * ((z + d) % 4) + y) for z in range...  12.6 us
    ppermute x10, starting transfers between devices, shift_row_x(): lax.ppermute(v, 'row', [(2 * x + k, 2 * ((x + d) % 4) + k) for x in range...  11.6 us
    pallas_call x4, Pallas kernels, choose_columns(): pl.pallas_call(functools.partial(choose_kernel, d), grid_spec=pltpu.Prefe...  6.47 us
  transfers between devices with their start and end apart: 35, of which 16 were waited for; matrix products, arithmetic and copies ran while one was open for 1% of the time, Pallas kernels for 16%

profile of v5, /device:TPU:6, one launch (start us, length us, event | category | flops | bytes accessed | tf_op | source)
XLA Modules:
  0.0 156.7 jit_solution(14728362927758223944)
XLA Ops:
  0.8 2.4 %collective-permute-start.14 = (bf16[2,64,4096]{2,1,0:T(8,128)(2,1)}, bf16[2,64,4096]{2,1,0:T(8,128)(2,1)S(1)}, u32[]{:S(2)}, u32[]{:S(2)}) collective-permute-start(bf16[2,64,4096]{2,1,0:T(8,128)(2,1)} %refs_0_.3), channel_id=1, source_target_pairs={{0,32},{16,48},{32,64},{48,80},{64,96},{80,112},{96,0},{112,16},{1... | collective-permute-start | bytes 3145736 | tf_op jit(solution)/shard_map/ppermute | solution.py:19
  4.0 3.9 %collective-permute-start.2 = (f32[2,128]{1,0:T(2,128)S(1)}, f32[2,128]{1,0:T(2,128)S(1)}, u32[]{:S(2)}, u32[]{:S(2)}) collective-permute-start(f32[2,128]{1,0:T(2,128)S(1)} %broadcast_in_dim.8), channel_id=1, source_target_pairs={{0,8},{1,9},{2,10},{3,11},{4,12},{5,13},{6,14},{7,15},{8,0},{9,1},... | collective-permute-start | bytes 3080 | tf_op jit(solution)/shard_map/ppermute | solution.py:27
  11.4 1.9 %collective-permute-done = f32[2,128]{1,0:T(2,128)S(1)} collective-permute-done((f32[2,128]{1,0:T(2,128)S(1)}, f32[2,128]{1,0:T(2,128)S(1)}, u32[]{:S(2)}, u32[]{:S(2)}) %collective-permute-start) | collective-permute-done | bytes 1056 | tf_op jit(solution)/shard_map/ppermute | solution.py:27
  13.4 3.2 %collective-permute-start.5 = (f32[4,2,128]{2,1,0:T(2,128)S(1)}, f32[4,2,128]{2,1,0:T(2,128)S(1)}, u32[]{:S(2)}, u32[]{:S(2)}) collective-permute-start(f32[4,2,128]{2,1,0:T(2,128)S(1)} %pad_maximum_fusion.2.refs_2_), channel_id=1, source_target_pairs={{0,2},{1,3},{2,0},{3,1},{4,6},{5,7},{6,4},{7,5},{8,10},{9,11},{10,... | collective-permute-start | bytes 12296 | tf_op jit(solution)/shard_map/ppermute | solution.py:31
  18.7 7.6 %collective-permute-done.15.refs_1_.refs_2_ = bf16[2,64,4096]{2,1,0:T(8,128)(2,1)S(1)} collective-permute-done((bf16[2,64,4096]{2,1,0:T(8,128)(2,1)}, bf16[2,64,4096]{2,1,0:T(8,128)(2,1)S(1)}, u32[]{:S(2)}, u32[]{:S(2)}) %collective-permute-start.15) | collective-permute-done | bytes 1048608 | tf_op jit(solution)/shard_map/ppermute | solution.py:19
  27.3 3.0 %collective-permute-start.16 = (bf16[1,64,4096]{2,1,0:T(8,128)(2,1)}, bf16[1,64,4096]{2,1,0:T(8,128)(2,1)}, u32[]{:S(2)}, u32[]{:S(2)}) collective-permute-start(bf16[1,64,4096]{2,1,0:T(8,128)(2,1)} %get-tuple-element.20), channel_id=1, source_target_pairs={{0,32},{16,48},{32,64},{48,80},{64,96},{80,112},{96,0},{112,16},{1... | collective-permute-start | bytes 1572872 | tf_op jit(solution)/shard_map/ppermute | solution.py:19
  32.0 2.5 %collective-permute-start.7 = (f32[16,2,128]{2,1,0:T(2,128)S(1)}, f32[16,2,128]{2,1,0:T(2,128)S(1)}, u32[]{:S(2)}, u32[]{:S(2)}) collective-permute-start(f32[16,2,128]{2,1,0:T(2,128)S(1)} %constant_dynamic-update-slice_fusion), channel_id=1, source_target_pairs={{0,96},{16,112},{32,0},{48,16},{64,32},{80,48},{96,64},{112,80},{1... | collective-permute-start | bytes 49160 | tf_op jit(solution)/shard_map/ppermute | solution.py:19
  35.3 7.8 %collective-permute-done.8 = f32[16,2,128]{2,1,0:T(2,128)S(1)} collective-permute-done((f32[16,2,128]{2,1,0:T(2,128)S(1)}, f32[16,2,128]{2,1,0:T(2,128)S(1)}, u32[]{:S(2)}, u32[]{:S(2)}) %collective-permute-start.8) | collective-permute-done | bytes 16416 | tf_op jit(solution)/shard_map/ppermute | solution.py:19
  45.9 1.8 %pick_tiles.2.mine_ref = bf16[2,64,4096]{2,1,0:T(8,128)(2,1)S(1)} custom-call(s32[7]{0:T(128)S(1)} %stack.46.at_ref, s32[8]{0:T(128)S(1)} %fusion.name_ref, bf16[2,64,4096]{2,1,0:T(8,128)(2,1)S(1)} %copy-done, bf16[2,64,4096]{2,1,0:T(8,128)(2,1)S(1)} %collective-permute-done.14.refs_0_.refs_1_, ...), custom_call_target="tpu_custom_call" | custom-call | bytes 2097152 | tf_op jit(solution)/shard_map/pick_tiles/pallas_call | solution.py:218
  48.6 5.1 %collective-permute-start.28 = (bf16[2,64,2048]{2,1,0:T(8,128)(2,1)S(1)}, bf16[2,64,2048]{2,1,0:T(8,128)(2,1)S(1)}, u32[]{:S(2)}, u32[]{:S(2)}) collective-permute-start(bf16[2,64,2048]{2,1,0:T(8,128)(2,1)S(1)} %get-tuple-element.28.refs_0_), channel_id=1, source_target_pairs={{0,12},{1,13},{2,14},{3,15},{4,0},{5,1},{6,2},{7,3},{8,4},{9,5},{1... | collective-permute-start | bytes 1572872 | tf_op jit(solution)/shard_map/ppermute | solution.py:27
  53.7 2.9 %collective-permute-start.20 = (bf16[2,64,2048]{2,1,0:T(8,128)(2,1)S(1)}, bf16[2,64,2048]{2,1,0:T(8,128)(2,1)S(1)}, u32[]{:S(2)}, u32[]{:S(2)}) collective-permute-start(bf16[2,64,2048]{2,1,0:T(8,128)(2,1)S(1)} %get-tuple-element.22.refs_0_), channel_id=1, source_target_pairs={{0,3},{1,0},{2,1},{3,2},{4,7},{5,4},{6,5},{7,6},{8,11},{9,8},{10,9... | collective-permute-start | bytes 1572872 | tf_op jit(solution)/shard_map/ppermute | solution.py:31
  57.9 1.6 %choose_columns.5 = bf16[2,512,256]{2,1,0:T(8,128)(2,1)S(1)} custom-call(s32[7]{0:T(128)S(1)} %stack.46.at_ref, s32[128]{0:T(128)S(1)} %copy-done.3, bf16[512,1024]{1,0:T(8,128)(2,1)S(1)} %copy-done.1, f32[16,8,128]{2,1,0:T(8,128)S(1)} %pad_maximum_fusion.1.own_ref, f32[16,8,128]{2,1,0:T(8,128)S(1)} %collective-permute-done.9.other_ref, s32[8,16]{1,0:T(8,128)S(1)} %copy-done.2), custom_call_target="tpu_custom_call" | custom-call | flops 536870912 | bytes 1572864 | tf_op jit(solution)/shard_map/choose_columns/pallas_call | solution.py:133
  59.6 5.6 %collective-permute-done.28.refs_1_.refs_2_ = bf16[2,64,2048]{2,1,0:T(8,128)(2,1)S(1)} collective-permute-done((bf16[2,64,2048]{2,1,0:T(8,128)(2,1)S(1)}, bf16[2,64,2048]{2,1,0:T(8,128)(2,1)S(1)}, u32[]{:S(2)}, u32[]{:S(2)}) %collective-permute-start.28) | collective-permute-done | bytes 524320 | tf_op jit(solution)/shard_map/ppermute | solution.py:27
  65.2 3.4 %collective-permute-done.27.refs_0_.refs_1_ = bf16[2,64,2048]{2,1,0:T(8,128)(2,1)S(1)} collective-permute-done((bf16[2,64,2048]{2,1,0:T(8,128)(2,1)S(1)}, bf16[2,64,2048]{2,1,0:T(8,128)(2,1)S(1)}, u32[]{:S(2)}, u32[]{:S(2)}) %collective-permute-start.27) | collective-permute-done | bytes 524320 | tf_op jit(solution)/shard_map/ppermute | solution.py:27
  68.7 3.2 %collective-permute-start.30 = (bf16[1,64,2048]{2,1,0:T(8,128)(2,1)S(1)}, bf16[1,64,2048]{2,1,0:T(8,128)(2,1)S(1)}, u32[]{:S(2)}, u32[]{:S(2)}) collective-permute-start(bf16[1,64,2048]{2,1,0:T(8,128)(2,1)S(1)} %get-tuple-element.30), channel_id=1, source_target_pairs={{0,12},{1,13},{2,14},{3,15},{4,0},{5,1},{6,2},{7,3},{8,4},{9,5},{1... | collective-permute-start | bytes 786440 | tf_op jit(solution)/shard_map/ppermute | solution.py:27
  72.7 2.6 %collective-permute-start.22 = (bf16[1,64,2048]{2,1,0:T(8,128)(2,1)S(1)}, bf16[1,64,2048]{2,1,0:T(8,128)(2,1)S(1)}, u32[]{:S(2)}, u32[]{:S(2)}) collective-permute-start(bf16[1,64,2048]{2,1,0:T(8,128)(2,1)S(1)} %get-tuple-element.24), channel_id=1, source_target_pairs={{0,3},{1,0},{2,1},{3,2},{4,7},{5,4},{6,5},{7,6},{8,11},{9,8},{10,9... | collective-permute-start | bytes 786440 | tf_op jit(solution)/shard_map/ppermute | solution.py:31
  75.3 1.6 %choose_columns.6 = bf16[2,512,256]{2,1,0:T(8,128)(2,1)S(1)} custom-call(s32[7]{0:T(128)S(1)} %stack.46.at_ref, s32[128]{0:T(128)S(1)} %copy-done.3, bf16[512,1024]{1,0:T(8,128)(2,1)S(1)} %copy-done.1, f32[16,8,128]{2,1,0:T(8,128)S(1)} %pad_maximum_fusion.1.own_ref, f32[16,8,128]{2,1,0:T(8,128)S(1)} %collective-permute-done.9.other_ref, s32[8,16]{1,0:T(8,128)S(1)} %copy-done.2), custom_call_target="tpu_custom_call" | custom-call | flops 536870912 | bytes 1572864 | tf_op jit(solution)/shard_map/choose_columns/pallas_call | solution.py:133
  77.7 2.8 %collective-permute-start.32 = (bf16[8,64,2048]{2,1,0:T(8,128)(2,1)S(1)}, bf16[8,64,2048]{2,1,0:T(8,128)(2,1)S(1)}, u32[]{:S(2)}, u32[]{:S(2)}) collective-permute-start(bf16[8,64,2048]{2,1,0:T(8,128)(2,1)S(1)} %copy_parts.12.refs_0_), channel_id=1, source_target_pairs={{0,3},{1,0},{2,1},{3,2},{4,7},{5,4},{6,5},{7,6},{8,11},{9,8},{10,9... | collective-permute-start | bytes 6291464 | tf_op jit(solution)/shard_map/ppermute | solution.py:31
  80.7 3.0 %collective-permute-start.24 = (bf16[8,64,2048]{2,1,0:T(8,128)(2,1)S(1)}, bf16[8,64,2048]{2,1,0:T(8,128)(2,1)S(1)}, u32[]{:S(2)}, u32[]{:S(2)}) collective-permute-start(bf16[8,64,2048]{2,1,0:T(8,128)(2,1)S(1)} %copy_parts.9.refs_0_), channel_id=1, source_target_pairs={{0,12},{1,13},{2,14},{3,15},{4,0},{5,1},{6,2},{7,3},{8,4},{9,5},{1... | collective-permute-start | bytes 6291464 | tf_op jit(solution)/shard_map/ppermute | solution.py:27
  85.4 5.7 %collective-permute-done.11.refs_2_ = bf16[2,512,256]{2,1,0:T(8,128)(2,1)S(1)} collective-permute-done((bf16[2,512,256]{2,1,0:T(8,128)(2,1)S(1)}, bf16[2,512,256]{2,1,0:T(8,128)(2,1)S(1)}, u32[]{:S(2)}, u32[]{:S(2)}) %collective-permute-start.11) | collective-permute-done | bytes 524320 | tf_op jit(solution)/shard_map/ppermute | solution.py:19
  91.1 1.6 %choose_columns.4.refs_0_ = bf16[2,512,256]{2,1,0:T(8,128)(2,1)S(1)} custom-call(s32[7]{0:T(128)S(1)} %stack.46.at_ref, s32[128]{0:T(128)S(1)} %copy-done.3, bf16[512,1024]{1,0:T(8,128)(2,1)S(1)} %copy-done.1, f32[16,8,128]{2,1,0:T(8,128)S(1)} %pad_maximum_fusion.1.own_ref, f32[16,8,128]{2,1,0:T(8,128)S(1)} %collective-permute-done.9.other_ref, ...), custom_call_target="tpu_custom_call" | custom-call | flops 536870912 | bytes 1572864 | tf_op jit(solution)/shard_map/choose_columns/pallas_call | solution.py:133
  92.8 9.9 %collective-permute-done.12.refs_3_ = bf16[2,512,256]{2,1,0:T(8,128)(2,1)S(1)} collective-permute-done((bf16[2,512,256]{2,1,0:T(8,128)(2,1)S(1)}, bf16[2,512,256]{2,1,0:T(8,128)(2,1)S(1)}, u32[]{:S(2)}, u32[]{:S(2)}) %collective-permute-start.12) | collective-permute-done | bytes 524320 | tf_op jit(solution)/shard_map/ppermute | solution.py:19
  103.0 2.6 %collective-permute-done.13.refs_4_ = bf16[4,512,256]{2,1,0:T(8,128)(2,1)S(1)} collective-permute-done((bf16[4,512,256]{2,1,0:T(8,128)(2,1)S(1)}, bf16[4,512,256]{2,1,0:T(8,128)(2,1)S(1)}, u32[]{:S(2)}, u32[]{:S(2)}) %collective-permute-start.13) | collective-permute-done | bytes 1048608 | tf_op jit(solution)/shard_map/ppermute | solution.py:23
  107.2 17.0 %collective-permute-done.32.refs_1_.refs_2_ = bf16[8,64,2048]{2,1,0:T(8,128)(2,1)S(1)} collective-permute-done((bf16[8,64,2048]{2,1,0:T(8,128)(2,1)S(1)}, bf16[8,64,2048]{2,1,0:T(8,128)(2,1)S(1)}, u32[]{:S(2)}, u32[]{:S(2)}) %collective-permute-start.32) | collective-permute-done | bytes 2097184 | tf_op jit(solution)/shard_map/ppermute | solution.py:31
  124.2 2.8 %collective-permute-done.31.refs_0_.refs_1_ = bf16[8,64,2048]{2,1,0:T(8,128)(2,1)S(1)} collective-permute-done((bf16[8,64,2048]{2,1,0:T(8,128)(2,1)S(1)}, bf16[8,64,2048]{2,1,0:T(8,128)(2,1)S(1)}, u32[]{:S(2)}, u32[]{:S(2)}) %collective-permute-start.31) | collective-permute-done | bytes 2097184 | tf_op jit(solution)/shard_map/ppermute | solution.py:31
  127.3 3.2 %collective-permute-start.34 = (bf16[4,64,2048]{2,1,0:T(8,128)(2,1)S(1)}, bf16[4,64,2048]{2,1,0:T(8,128)(2,1)S(1)}, u32[]{:S(2)}, u32[]{:S(2)}) collective-permute-start(bf16[4,64,2048]{2,1,0:T(8,128)(2,1)S(1)} %get-tuple-element.32), channel_id=1, source_target_pairs={{0,3},{1,0},{2,1},{3,2},{4,7},{5,4},{6,5},{7,6},{8,11},{9,8},{10,9... | collective-permute-start | bytes 3145736 | tf_op jit(solution)/shard_map/ppermute | solution.py:31
  130.8 3.2 %collective-permute-start.26 = (bf16[4,64,2048]{2,1,0:T(8,128)(2,1)S(1)}, bf16[4,64,2048]{2,1,0:T(8,128)(2,1)S(1)}, u32[]{:S(2)}, u32[]{:S(2)}) collective-permute-start(bf16[4,64,2048]{2,1,0:T(8,128)(2,1)S(1)} %get-tuple-element.26), channel_id=1, source_target_pairs={{0,12},{1,13},{2,14},{3,15},{4,0},{5,1},{6,2},{7,3},{8,4},{9,5},{1... | collective-permute-start | bytes 3145736 | tf_op jit(solution)/shard_map/ppermute | solution.py:27
  134.0 4.8 %product.5.refs_2_ = f32[512,2048]{1,0:T(8,128)S(1)} custom-call(bf16[512,2048]{1,0:T(8,128)(2,1)S(1)} %get-tuple-element.27.left_ref, bf16[8,64,2048]{2,1,0:T(8,128)(2,1)S(1)} %copy_parts.12.refs_0_, bf16[8,64,2048]{2,1,0:T(8,128)(2,1)S(1)} %collective-permute-done.31.refs_0_.refs_1_, bf16[8,64,2048]{2,1,0:T(8,128)(2,1)S(1)} %collective-permute-done.32.refs_1_.refs_2_), custom_call_target="tpu_custom_call" | custom-call | flops 6442450944 | bytes 24117248 | tf_op jit(solution)/shard_map/product/pallas_call | solution.py:280
  138.8 4.8 %product.4.refs_2_ = f32[512,2048]{1,0:T(8,128)S(1)} custom-call(bf16[512,2048]{1,0:T(8,128)(2,1)S(1)} %get-tuple-element.19.left_ref, bf16[8,64,2048]{2,1,0:T(8,128)(2,1)S(1)} %copy_parts.9.refs_0_, bf16[8,64,2048]{2,1,0:T(8,128)(2,1)S(1)} %collective-permute-done.23.refs_0_.refs_1_, bf16[8,64,2048]{2,1,0:T(8,128)(2,1)S(1)} %collective-permute-done.24.refs_1_.refs_2_), custom_call_target="tpu_custom_call" | custom-call | flops 6442450944 | bytes 24117248 | tf_op jit(solution)/shard_map/product/pallas_call | solution.py:280
  143.6 6.8 %collective-permute-done.33.refs_0_ = bf16[4,64,2048]{2,1,0:T(8,128)(2,1)S(1)} collective-permute-done((bf16[4,64,2048]{2,1,0:T(8,128)(2,1)S(1)}, bf16[4,64,2048]{2,1,0:T(8,128)(2,1)S(1)}, u32[]{:S(2)}, u32[]{:S(2)}) %collective-permute-start.33) | collective-permute-done | bytes 1048608 | tf_op jit(solution)/shard_map/ppermute | solution.py:31
  150.4 3.1 %product.6.refs_3_ = bf16[512,4096]{1,0:T(8,128)(2,1)} custom-call(bf16[512,2048]{1,0:T(8,128)(2,1)S(1)} %get-tuple-element.27.left_ref, bf16[4,64,2048]{2,1,0:T(8,128)(2,1)S(1)} %collective-permute-done.33.refs_0_, bf16[4,64,2048]{2,1,0:T(8,128)(2,1)S(1)} %collective-permute-done.34.refs_1_, f32[512,2048]{1,0:T(8,128)S(1)} %product.5.refs_2_), custom_call_target="tpu_custom_call" | custom-call | flops 2147483648 | bytes 13631488 | tf_op jit(solution)/shard_map/product/pallas_call | solution.py:280
  153.5 3.1 %product.7 = bf16[512,4096]{1,0:T(8,128)(2,1)} custom-call(bf16[512,2048]{1,0:T(8,128)(2,1)S(1)} %get-tuple-element.19.left_ref, bf16[4,64,2048]{2,1,0:T(8,128)(2,1)S(1)} %collective-permute-done.25.refs_0_, bf16[4,64,2048]{2,1,0:T(8,128)(2,1)S(1)} %collective-permute-done.26.refs_1_, ...), custom_call_target="tpu_custom_call", output_to_operand_aliasing={{}: (4, {})} | custom-call | flops 2147483648 | bytes 13631488 | tf_op jit(solution)/shard_map/product/pallas_call | solution.py:280
  (84 shorter events, 21.4 us)
Async XLA Ops:
  0.0 26.3 %collective-permute-start.15 = (bf16[2,64,4096]{2,1,0:T(8,128)(2,1)}, bf16[2,64,4096]{2,1,0:T(8,128)(2,1)S(1)}, u32[]{:S(2)}, u32[]{:S(2)}) collective-permute-start(bf16[2,64,4096]{2,1,0:T(8,128)(2,1)} %refs_0_.3), channel_id=1, source_target_pairs={{0,96},{16,112},{32,0},{48,16},{64,32},{80,48},{96,64},{112,80},{1... | collective-permute-start | bytes 3145736 | tf_op jit(solution)/shard_map/ppermute | solution.py:19
  0.8 25.5 %collective-permute-start.14 = (bf16[2,64,4096]{2,1,0:T(8,128)(2,1)}, bf16[2,64,4096]{2,1,0:T(8,128)(2,1)S(1)}, u32[]{:S(2)}, u32[]{:S(2)}) collective-permute-start(bf16[2,64,4096]{2,1,0:T(8,128)(2,1)} %refs_0_.3), channel_id=1, source_target_pairs={{0,32},{16,48},{32,64},{48,80},{64,96},{80,112},{96,0},{112,16},{1... | collective-permute-start | bytes 3145736 | tf_op jit(solution)/shard_map/ppermute | solution.py:19
  4.0 6.0 %collective-permute-start.2 = (f32[2,128]{1,0:T(2,128)S(1)}, f32[2,128]{1,0:T(2,128)S(1)}, u32[]{:S(2)}, u32[]{:S(2)}) collective-permute-start(f32[2,128]{1,0:T(2,128)S(1)} %broadcast_in_dim.8), channel_id=1, source_target_pairs={{0,8},{1,9},{2,10},{3,11},{4,12},{5,13},{6,14},{7,15},{8,0},{9,1},... | collective-permute-start | bytes 3080 | tf_op jit(solution)/shard_map/ppermute | solution.py:27
  7.9 3.6 %collective-permute-start.1 = (f32[2,128]{1,0:T(2,128)S(1)}, f32[2,128]{1,0:T(2,128)S(1)}, u32[]{:S(2)}, u32[]{:S(2)}) collective-permute-start(f32[2,128]{1,0:T(2,128)S(1)} %broadcast_in_dim.8), channel_id=1, source_target_pairs={{0,12},{1,13},{2,14},{3,15},{4,0},{5,1},{6,2},{7,3},{8,4},{9,5},{1... | collective-permute-start | bytes 3080 | tf_op jit(solution)/shard_map/ppermute | solution.py:27
  8.6 4.8 %collective-permute-start = (f32[2,128]{1,0:T(2,128)S(1)}, f32[2,128]{1,0:T(2,128)S(1)}, u32[]{:S(2)}, u32[]{:S(2)}) collective-permute-start(f32[2,128]{1,0:T(2,128)S(1)} %broadcast_in_dim.8), channel_id=1, source_target_pairs={{0,4},{1,5},{2,6},{3,7},{4,8},{5,9},{6,10},{7,11},{8,12},{9,13},{1... | collective-permute-start | bytes 3080 | tf_op jit(solution)/shard_map/ppermute | solution.py:27
  13.4 16.9 %collective-permute-start.5 = (f32[4,2,128]{2,1,0:T(2,128)S(1)}, f32[4,2,128]{2,1,0:T(2,128)S(1)}, u32[]{:S(2)}, u32[]{:S(2)}) collective-permute-start(f32[4,2,128]{2,1,0:T(2,128)S(1)} %pad_maximum_fusion.2.refs_2_), channel_id=1, source_target_pairs={{0,2},{1,3},{2,0},{3,1},{4,6},{5,7},{6,4},{7,5},{8,10},{9,11},{10,... | collective-permute-start | bytes 12296 | tf_op jit(solution)/shard_map/ppermute | solution.py:31
  16.7 13.7 %collective-permute-start.4 = (f32[4,2,128]{2,1,0:T(2,128)S(1)}, f32[4,2,128]{2,1,0:T(2,128)S(1)}, u32[]{:S(2)}, u32[]{:S(2)}) collective-permute-start(f32[4,2,128]{2,1,0:T(2,128)S(1)} %pad_maximum_fusion.2.refs_2_), channel_id=1, source_target_pairs={{0,3},{1,0},{2,1},{3,2},{4,7},{5,4},{6,5},{7,6},{8,11},{9,8},{10,9... | collective-permute-start | bytes 12296 | tf_op jit(solution)/shard_map/ppermute | solution.py:31
  17.7 12.6 %collective-permute-start.3 = (f32[4,2,128]{2,1,0:T(2,128)S(1)}, f32[4,2,128]{2,1,0:T(2,128)S(1)}, u32[]{:S(2)}, u32[]{:S(2)}) collective-permute-start(f32[4,2,128]{2,1,0:T(2,128)S(1)} %pad_maximum_fusion.2.refs_2_), channel_id=1, source_target_pairs={{0,1},{1,2},{2,3},{3,0},{4,5},{5,6},{6,7},{7,4},{8,9},{9,10},{10,1... | collective-permute-start | bytes 12296 | tf_op jit(solution)/shard_map/ppermute | solution.py:31
  27.3 17.5 %collective-permute-start.16 = (bf16[1,64,4096]{2,1,0:T(8,128)(2,1)}, bf16[1,64,4096]{2,1,0:T(8,128)(2,1)}, u32[]{:S(2)}, u32[]{:S(2)}) collective-permute-start(bf16[1,64,4096]{2,1,0:T(8,128)(2,1)} %get-tuple-element.20), channel_id=1, source_target_pairs={{0,32},{16,48},{32,64},{48,80},{64,96},{80,112},{96,0},{112,16},{1... | collective-permute-start | bytes 1572872 | tf_op jit(solution)/shard_map/ppermute | solution.py:19
  30.3 14.5 %collective-permute-start.17 = (bf16[1,64,4096]{2,1,0:T(8,128)(2,1)}, bf16[1,64,4096]{2,1,0:T(8,128)(2,1)}, u32[]{:S(2)}, u32[]{:S(2)}) collective-permute-start(bf16[1,64,4096]{2,1,0:T(8,128)(2,1)} %get-tuple-element.21), channel_id=1, source_target_pairs={{0,96},{16,112},{32,0},{48,16},{64,32},{80,48},{96,64},{112,80},{1... | collective-permute-start | bytes 1572872 | tf_op jit(solution)/shard_map/ppermute | solution.py:19
  30.4 12.8 %collective-permute-start.8 = (f32[16,2,128]{2,1,0:T(2,128)S(1)}, f32[16,2,128]{2,1,0:T(2,128)S(1)}, u32[]{:S(2)}, u32[]{:S(2)}) collective-permute-start(f32[16,2,128]{2,1,0:T(2,128)S(1)} %constant_dynamic-update-slice_fusion), channel_id=1, source_target_pairs={{0,64},{16,80},{32,96},{48,112},{64,0},{80,16},{96,32},{112,48},{1... | collective-permute-start | bytes 49160 | tf_op jit(solution)/shard_map/ppermute | solution.py:19
  32.0 12.6 %collective-permute-start.7 = (f32[16,2,128]{2,1,0:T(2,128)S(1)}, f32[16,2,128]{2,1,0:T(2,128)S(1)}, u32[]{:S(2)}, u32[]{:S(2)}) collective-permute-start(f32[16,2,128]{2,1,0:T(2,128)S(1)} %constant_dynamic-update-slice_fusion), channel_id=1, source_target_pairs={{0,96},{16,112},{32,0},{48,16},{64,32},{80,48},{96,64},{112,80},{1... | collective-permute-start | bytes 49160 | tf_op jit(solution)/shard_map/ppermute | solution.py:19
  34.5 10.1 %collective-permute-start.6 = (f32[16,2,128]{2,1,0:T(2,128)S(1)}, f32[16,2,128]{2,1,0:T(2,128)S(1)}, u32[]{:S(2)}, u32[]{:S(2)}) collective-permute-start(f32[16,2,128]{2,1,0:T(2,128)S(1)} %constant_dynamic-update-slice_fusion), channel_id=1, source_target_pairs={{0,32},{16,48},{32,64},{48,80},{64,96},{80,112},{96,0},{112,16},{1... | collective-permute-start | bytes 49160 | tf_op jit(solution)/shard_map/ppermute | solution.py:19
  48.6 16.6 %collective-permute-start.28 = (bf16[2,64,2048]{2,1,0:T(8,128)(2,1)S(1)}, bf16[2,64,2048]{2,1,0:T(8,128)(2,1)S(1)}, u32[]{:S(2)}, u32[]{:S(2)}) collective-permute-start(bf16[2,64,2048]{2,1,0:T(8,128)(2,1)S(1)} %get-tuple-element.28.refs_0_), channel_id=1, source_target_pairs={{0,12},{1,13},{2,14},{3,15},{4,0},{5,1},{6,2},{7,3},{8,4},{9,5},{1... | collective-permute-start | bytes 1572872 | tf_op jit(solution)/shard_map/ppermute | solution.py:27
  53.7 14.9 %collective-permute-start.27 = (bf16[2,64,2048]{2,1,0:T(8,128)(2,1)S(1)}, bf16[2,64,2048]{2,1,0:T(8,128)(2,1)S(1)}, u32[]{:S(2)}, u32[]{:S(2)}) collective-permute-start(bf16[2,64,2048]{2,1,0:T(8,128)(2,1)S(1)} %get-tuple-element.28.refs_0_), channel_id=1, source_target_pairs={{0,4},{1,5},{2,6},{3,7},{4,8},{5,9},{6,10},{7,11},{8,12},{9,13},{1... | collective-permute-start | bytes 1572872 | tf_op jit(solution)/shard_map/ppermute | solution.py:27
  53.7 18.3 %collective-permute-start.20 = (bf16[2,64,2048]{2,1,0:T(8,128)(2,1)S(1)}, bf16[2,64,2048]{2,1,0:T(8,128)(2,1)S(1)}, u32[]{:S(2)}, u32[]{:S(2)}) collective-permute-start(bf16[2,64,2048]{2,1,0:T(8,128)(2,1)S(1)} %get-tuple-element.22.refs_0_), channel_id=1, source_target_pairs={{0,3},{1,0},{2,1},{3,2},{4,7},{5,4},{6,5},{7,6},{8,11},{9,8},{10,9... | collective-permute-start | bytes 1572872 | tf_op jit(solution)/shard_map/ppermute | solution.py:31
  56.6 15.3 %collective-permute-start.19 = (bf16[2,64,2048]{2,1,0:T(8,128)(2,1)S(1)}, bf16[2,64,2048]{2,1,0:T(8,128)(2,1)S(1)}, u32[]{:S(2)}, u32[]{:S(2)}) collective-permute-start(bf16[2,64,2048]{2,1,0:T(8,128)(2,1)S(1)} %get-tuple-element.22.refs_0_), channel_id=1, source_target_pairs={{0,1},{1,2},{2,3},{3,0},{4,5},{5,6},{6,7},{7,4},{8,9},{9,10},{10,1... | collective-permute-start | bytes 1572872 | tf_op jit(solution)/shard_map/ppermute | solution.py:31
  59.5 24.2 %collective-permute-start.10 = (bf16[2,512,256]{2,1,0:T(8,128)(2,1)S(1)}, bf16[2,512,256]{2,1,0:T(8,128)(2,1)S(1)}, u32[]{:S(2)}, u32[]{:S(2)}) collective-permute-start(bf16[2,512,256]{2,1,0:T(8,128)(2,1)S(1)} %choose_columns.5), channel_id=1, source_target_pairs={{0,32},{16,48},{32,64},{48,80},{64,96},{80,112},{96,0},{112,16},{1... | collective-permute-start | bytes 1572872 | tf_op jit(solution)/shard_map/ppermute | solution.py:19
  68.6 8.5 %collective-permute-start.29 = (bf16[1,64,2048]{2,1,0:T(8,128)(2,1)S(1)}, bf16[1,64,2048]{2,1,0:T(8,128)(2,1)S(1)}, u32[]{:S(2)}, u32[]{:S(2)}) collective-permute-start(bf16[1,64,2048]{2,1,0:T(8,128)(2,1)S(1)} %get-tuple-element.29), channel_id=1, source_target_pairs={{0,4},{1,5},{2,6},{3,7},{4,8},{5,9},{6,10},{7,11},{8,12},{9,13},{1... | collective-permute-start | bytes 786440 | tf_op jit(solution)/shard_map/ppermute | solution.py:27
  68.7 8.8 %collective-permute-start.30 = (bf16[1,64,2048]{2,1,0:T(8,128)(2,1)S(1)}, bf16[1,64,2048]{2,1,0:T(8,128)(2,1)S(1)}, u32[]{:S(2)}, u32[]{:S(2)}) collective-permute-start(bf16[1,64,2048]{2,1,0:T(8,128)(2,1)S(1)} %get-tuple-element.30), channel_id=1, source_target_pairs={{0,12},{1,13},{2,14},{3,15},{4,0},{5,1},{6,2},{7,3},{8,4},{9,5},{1... | collective-permute-start | bytes 786440 | tf_op jit(solution)/shard_map/ppermute | solution.py:27
  72.0 8.5 %collective-permute-start.21 = (bf16[1,64,2048]{2,1,0:T(8,128)(2,1)S(1)}, bf16[1,64,2048]{2,1,0:T(8,128)(2,1)S(1)}, u32[]{:S(2)}, u32[]{:S(2)}) collective-permute-start(bf16[1,64,2048]{2,1,0:T(8,128)(2,1)S(1)} %get-tuple-element.23), channel_id=1, source_target_pairs={{0,1},{1,2},{2,3},{3,0},{4,5},{5,6},{6,7},{7,4},{8,9},{9,10},{10,1... | collective-permute-start | bytes 786440 | tf_op jit(solution)/shard_map/ppermute | solution.py:31
  72.7 7.8 %collective-permute-start.22 = (bf16[1,64,2048]{2,1,0:T(8,128)(2,1)S(1)}, bf16[1,64,2048]{2,1,0:T(8,128)(2,1)S(1)}, u32[]{:S(2)}, u32[]{:S(2)}) collective-permute-start(bf16[1,64,2048]{2,1,0:T(8,128)(2,1)S(1)} %get-tuple-element.24), channel_id=1, source_target_pairs={{0,3},{1,0},{2,1},{3,2},{4,7},{5,4},{6,5},{7,6},{8,11},{9,8},{10,9... | collective-permute-start | bytes 786440 | tf_op jit(solution)/shard_map/ppermute | solution.py:31
  77.1 14.0 %collective-permute-start.11 = (bf16[2,512,256]{2,1,0:T(8,128)(2,1)S(1)}, bf16[2,512,256]{2,1,0:T(8,128)(2,1)S(1)}, u32[]{:S(2)}, u32[]{:S(2)}) collective-permute-start(bf16[2,512,256]{2,1,0:T(8,128)(2,1)S(1)} %choose_columns.6), channel_id=1, source_target_pairs={{0,64},{16,80},{32,96},{48,112},{64,0},{80,16},{96,32},{112,48},{1... | collective-permute-start | bytes 1572872 | tf_op jit(solution)/shard_map/ppermute | solution.py:19
  77.7 46.5 %collective-permute-start.32 = (bf16[8,64,2048]{2,1,0:T(8,128)(2,1)S(1)}, bf16[8,64,2048]{2,1,0:T(8,128)(2,1)S(1)}, u32[]{:S(2)}, u32[]{:S(2)}) collective-permute-start(bf16[8,64,2048]{2,1,0:T(8,128)(2,1)S(1)} %copy_parts.12.refs_0_), channel_id=1, source_target_pairs={{0,3},{1,0},{2,1},{3,2},{4,7},{5,4},{6,5},{7,6},{8,11},{9,8},{10,9... | collective-permute-start | bytes 6291464 | tf_op jit(solution)/shard_map/ppermute | solution.py:31
  80.5 46.5 %collective-permute-start.31 = (bf16[8,64,2048]{2,1,0:T(8,128)(2,1)S(1)}, bf16[8,64,2048]{2,1,0:T(8,128)(2,1)S(1)}, u32[]{:S(2)}, u32[]{:S(2)}) collective-permute-start(bf16[8,64,2048]{2,1,0:T(8,128)(2,1)S(1)} %copy_parts.12.refs_0_), channel_id=1, source_target_pairs={{0,1},{1,2},{2,3},{3,0},{4,5},{5,6},{6,7},{7,4},{8,9},{9,10},{10,1... | collective-permute-start | bytes 6291464 | tf_op jit(solution)/shard_map/ppermute | solution.py:31
  80.7 49.8 %collective-permute-start.24 = (bf16[8,64,2048]{2,1,0:T(8,128)(2,1)S(1)}, bf16[8,64,2048]{2,1,0:T(8,128)(2,1)S(1)}, u32[]{:S(2)}, u32[]{:S(2)}) collective-permute-start(bf16[8,64,2048]{2,1,0:T(8,128)(2,1)S(1)} %copy_parts.9.refs_0_), channel_id=1, source_target_pairs={{0,12},{1,13},{2,14},{3,15},{4,0},{5,1},{6,2},{7,3},{8,4},{9,5},{1... | collective-permute-start | bytes 6291464 | tf_op jit(solution)/shard_map/ppermute | solution.py:27
  83.8 46.8 %collective-permute-start.23 = (bf16[8,64,2048]{2,1,0:T(8,128)(2,1)S(1)}, bf16[8,64,2048]{2,1,0:T(8,128)(2,1)S(1)}, u32[]{:S(2)}, u32[]{:S(2)}) collective-permute-start(bf16[8,64,2048]{2,1,0:T(8,128)(2,1)S(1)} %copy_parts.9.refs_0_), channel_id=1, source_target_pairs={{0,4},{1,5},{2,6},{3,7},{4,8},{5,9},{6,10},{7,11},{8,12},{9,13},{1... | collective-permute-start | bytes 6291464 | tf_op jit(solution)/shard_map/ppermute | solution.py:27
  91.1 11.6 %collective-permute-start.12 = (bf16[2,512,256]{2,1,0:T(8,128)(2,1)S(1)}, bf16[2,512,256]{2,1,0:T(8,128)(2,1)S(1)}, u32[]{:S(2)}, u32[]{:S(2)}) collective-permute-start(bf16[2,512,256]{2,1,0:T(8,128)(2,1)S(1)} %choose_columns.7), channel_id=1, source_target_pairs={{0,96},{16,112},{32,0},{48,16},{64,32},{80,48},{96,64},{112,80},{1... | collective-permute-start | bytes 1572872 | tf_op jit(solution)/shard_map/ppermute | solution.py:19
  127.2 23.2 %collective-permute-start.33 = (bf16[4,64,2048]{2,1,0:T(8,128)(2,1)S(1)}, bf16[4,64,2048]{2,1,0:T(8,128)(2,1)S(1)}, u32[]{:S(2)}, u32[]{:S(2)}) collective-permute-start(bf16[4,64,2048]{2,1,0:T(8,128)(2,1)S(1)} %get-tuple-element.31), channel_id=1, source_target_pairs={{0,1},{1,2},{2,3},{3,0},{4,5},{5,6},{6,7},{7,4},{8,9},{9,10},{10,1... | collective-permute-start | bytes 3145736 | tf_op jit(solution)/shard_map/ppermute | solution.py:31
  127.3 23.1 %collective-permute-start.34 = (bf16[4,64,2048]{2,1,0:T(8,128)(2,1)S(1)}, bf16[4,64,2048]{2,1,0:T(8,128)(2,1)S(1)}, u32[]{:S(2)}, u32[]{:S(2)}) collective-permute-start(bf16[4,64,2048]{2,1,0:T(8,128)(2,1)S(1)} %get-tuple-element.32), channel_id=1, source_target_pairs={{0,3},{1,0},{2,1},{3,2},{4,7},{5,4},{6,5},{7,6},{8,11},{9,8},{10,9... | collective-permute-start | bytes 3145736 | tf_op jit(solution)/shard_map/ppermute | solution.py:31
  130.7 22.8 %collective-permute-start.25 = (bf16[4,64,2048]{2,1,0:T(8,128)(2,1)S(1)}, bf16[4,64,2048]{2,1,0:T(8,128)(2,1)S(1)}, u32[]{:S(2)}, u32[]{:S(2)}) collective-permute-start(bf16[4,64,2048]{2,1,0:T(8,128)(2,1)S(1)} %get-tuple-element.25), channel_id=1, source_target_pairs={{0,4},{1,5},{2,6},{3,7},{4,8},{5,9},{6,10},{7,11},{8,12},{9,13},{1... | collective-permute-start | bytes 3145736 | tf_op jit(solution)/shard_map/ppermute | solution.py:27
  130.8 22.7 %collective-permute-start.26 = (bf16[4,64,2048]{2,1,0:T(8,128)(2,1)S(1)}, bf16[4,64,2048]{2,1,0:T(8,128)(2,1)S(1)}, u32[]{:S(2)}, u32[]{:S(2)}) collective-permute-start(bf16[4,64,2048]{2,1,0:T(8,128)(2,1)S(1)} %get-tuple-element.26), channel_id=1, source_target_pairs={{0,12},{1,13},{2,14},{3,15},{4,0},{5,1},{6,2},{7,3},{8,4},{9,5},{1... | collective-permute-start | bytes 3145736 | tf_op jit(solution)/shard_map/ppermute | solution.py:27
  (7 other events, 82.1 us)
